TPU v7x, 256 devices: a whole 4x4x8 slice. The times are simulated.
256 devices in a mesh: seq: 32 (over z, y_hi, core), dp: 8 (over x, y_lo).
Axes of the slice: x: 4, y: 4 (y_hi: 2, y_lo: 2; y = y_hi * 2 + y_lo), z: 8, core: 2. Of those that a mesh axis runs over, the one named last changes fastest.
Arguments:
- video: bfloat16 [8, 32, 256, 1152], P('dp', 'seq'), may hold values from -6 to 6
- spatial_in: bfloat16 [1152, 1728], replicated, may hold values from -0.1875 to 0.1875
- spatial_out: bfloat16 [576, 1152], replicated, may hold values from -1 to 1
- temporal_in: bfloat16 [1152, 1728], replicated, may hold values from -0.1875 to 0.1875
- temporal_out: bfloat16 [576, 1152], replicated, may hold values from -1 to 1
- cotangent: bfloat16 [8, 32, 256, 1152], P('dp', 'seq'), may hold values from -6 to 6
Outputs:
- blocks_out: bfloat16 [8, 32, 256, 1152], P('dp', 'seq')
- grad_video: bfloat16 [8, 32, 256, 1152], P('dp', 'seq')
- grad_in: float32 [1152, 1728], P('seq', 'dp')
- grad_out: float32 [576, 1152], P('seq', 'dp')
All inputs are finite; a program needn't handle non-finite values.
Results may differ from a plain program's by a relative error of at most 0.034.
Values may be sent and summed in bfloat16 or wider, within the bound.
A program may use at most 128 MiB of HBM per device.

v0:
```python
import jax
import jax.numpy as jnp
from jax import lax
from jax.sharding import PartitionSpec as P

HEADS = 8
HEAD = 72


def norm_forward(inputs):
    center = inputs - jnp.mean(inputs, -1, keepdims=True)
    inverse = lax.rsqrt(jnp.mean(center * center, -1, keepdims=True) + 1e-06)
    return (center * inverse, inverse)


def norm_backward(normed, inverse, incoming):
    return inverse * (
        incoming
        - jnp.mean(incoming, -1, keepdims=True)
        - normed * jnp.mean(incoming * normed, -1, keepdims=True)
    )


def attend(queries, key_rows, val_rows, factor):
    scores = (
        jnp.einsum("glhd,gmhd->ghlm", queries, key_rows, preferred_element_type=jnp.float32)
        * factor
    )
    exponent = jnp.exp(scores)
    shares = exponent / jnp.sum(exponent, -1, keepdims=True)
    weights = shares.astype(jnp.bfloat16)
    attended = jnp.einsum(
        "ghlm,gmhd->glhd", weights, val_rows, preferred_element_type=jnp.float32
    ).astype(jnp.bfloat16)
    return (attended, shares, weights)


def attend_back(queries, key_rows, val_rows, shares, weights, incoming, factor):
    grad_val = jnp.einsum(
        "ghlm,glhd->gmhd", weights, incoming, preferred_element_type=jnp.float32
    ).astype(jnp.bfloat16)
    grad_weights = jnp.einsum(
        "glhd,gmhd->ghlm", incoming, val_rows, preferred_element_type=jnp.float32
    )
    grad_score = (
        shares * (grad_weights - jnp.sum(grad_weights * shares, -1, keepdims=True)) * factor
    )
    grad_query = jnp.einsum(
        "ghlm,gmhd->glhd", grad_score, key_rows.astype(jnp.float32), precision=lax.Precision.HIGHEST
    ).astype(jnp.bfloat16)
    grad_key = jnp.einsum(
        "ghlm,glhd->gmhd", grad_score, queries.astype(jnp.float32), precision=lax.Precision.HIGHEST
    ).astype(jnp.bfloat16)
    return (grad_query, grad_key, grad_val)


def local(video, spatial_in, spatial_out, temporal_in, temporal_out, cotangent):
    batch, frames, places, width = video.shape
    heads_dim = temporal_out.shape[0]
    factor = HEAD ** (-0.5)
    groups = lax.axis_size("seq")
    spread = places // groups
    all_frames = frames * groups
    count_rows = batch * frames * places
    video_wide = video.astype(jnp.float32)
    spatial_normed, spatial_inverse = norm_forward(video_wide)
    spatial_h = spatial_normed.astype(jnp.bfloat16).reshape(count_rows, width)
    spatial_qkv = (
        jnp.dot(spatial_h, spatial_in, preferred_element_type=jnp.float32)
        .astype(jnp.bfloat16)
        .reshape(batch * frames, places, 3, HEADS, HEAD)
    )
    spatial_att, spatial_shares, spatial_weights = attend(
        spatial_qkv[:, :, 0], spatial_qkv[:, :, 1], spatial_qkv[:, :, 2], factor
    )
    residual = (
        video_wide
        + jnp.dot(
            spatial_att.reshape(count_rows, heads_dim),
            spatial_out,
            preferred_element_type=jnp.float32,
        ).reshape(video.shape)
    ).astype(jnp.bfloat16)
    temporal_normed, temporal_inverse = norm_forward(residual.astype(jnp.float32))
    temporal_h = temporal_normed.astype(jnp.bfloat16).reshape(count_rows, width)
    temporal_qkv = (
        jnp.dot(temporal_h, temporal_in, preferred_element_type=jnp.float32)
        .astype(jnp.bfloat16)
        .reshape(batch, frames, groups, spread, 3 * heads_dim)
    )
    position_qkv = lax.all_to_all(temporal_qkv, "seq", split_axis=2, concat_axis=1, tiled=True)
    position_qkv = position_qkv.reshape(batch, all_frames, spread, 3 * heads_dim)
    swapped = jnp.swapaxes(position_qkv, 1, 2).reshape(batch * spread, all_frames, 3, HEADS, HEAD)
    temporal_att, temporal_shares, temporal_weights = attend(
        swapped[:, :, 0], swapped[:, :, 1], swapped[:, :, 2], factor
    )
    back_layout = jnp.swapaxes(
        temporal_att.reshape(batch, spread, all_frames, heads_dim), 1, 2
    ).reshape(batch, all_frames, 1, spread, heads_dim)
    frame_att = lax.all_to_all(back_layout, "seq", split_axis=1, concat_axis=2, tiled=True)
    frame_rows = frame_att.reshape(count_rows, heads_dim)
    blocks_out = (
        residual.astype(jnp.float32)
        + jnp.dot(frame_rows, temporal_out, preferred_element_type=jnp.float32).reshape(video.shape)
    ).astype(jnp.bfloat16)
    moved = lax.all_to_all(
        cotangent.reshape(batch, frames, groups, spread, width),
        "seq",
        split_axis=2,
        concat_axis=1,
        tiled=True,
    )
    moved_rows = jnp.swapaxes(moved.reshape(batch, all_frames, spread, width), 1, 2).reshape(
        batch * spread * all_frames, width
    )
    att_rows = temporal_att.reshape(batch * spread * all_frames, heads_dim)
    grad_out = jnp.dot(att_rows.T, moved_rows, preferred_element_type=jnp.float32)
    grad_att = (
        jnp.dot(moved_rows, temporal_out.T, preferred_element_type=jnp.float32)
        .astype(jnp.bfloat16)
        .reshape(batch * spread, all_frames, HEADS, HEAD)
    )
    temporal_grads = attend_back(
        swapped[:, :, 0],
        swapped[:, :, 1],
        swapped[:, :, 2],
        temporal_shares,
        temporal_weights,
        grad_att,
        factor,
    )
    grad_pos = jnp.stack(temporal_grads, 2).reshape(batch, spread, all_frames, 3 * heads_dim)
    grad_pos = jnp.swapaxes(grad_pos, 1, 2).reshape(batch, all_frames, 1, spread, 3 * heads_dim)
    grad_qkv = lax.all_to_all(grad_pos, "seq", split_axis=1, concat_axis=2, tiled=True).reshape(
        count_rows, 3 * heads_dim
    )
    grad_in = jnp.dot(temporal_h.T, grad_qkv, preferred_element_type=jnp.float32)
    grad_norm_t = jnp.dot(grad_qkv, temporal_in.T, preferred_element_type=jnp.float32).reshape(
        video.shape
    )
    grad_residual = (
        cotangent.astype(jnp.float32)
        + norm_backward(temporal_normed, temporal_inverse, grad_norm_t)
    ).astype(jnp.bfloat16)
    grad_spatial = (
        jnp.dot(
            grad_residual.reshape(count_rows, width),
            spatial_out.T,
            preferred_element_type=jnp.float32,
        )
        .astype(jnp.bfloat16)
        .reshape(batch * frames, places, HEADS, HEAD)
    )
    spatial_grads = attend_back(
        spatial_qkv[:, :, 0],
        spatial_qkv[:, :, 1],
        spatial_qkv[:, :, 2],
        spatial_shares,
        spatial_weights,
        grad_spatial,
        factor,
    )
    grad_sqkv = jnp.stack(spatial_grads, 2).reshape(count_rows, 3 * heads_dim)
    grad_norm_s = jnp.dot(grad_sqkv, spatial_in.T, preferred_element_type=jnp.float32).reshape(
        video.shape
    )
    grad_video = (
        grad_residual.astype(jnp.float32)
        + norm_backward(spatial_normed, spatial_inverse, grad_norm_s)
    ).astype(jnp.bfloat16)
    grad_in, grad_out = (
        lax.psum_scatter(
            grad_in.astype(jnp.bfloat16), "seq", scatter_dimension=0, tiled=True
        ).astype(jnp.float32),
        lax.psum_scatter(
            grad_out.astype(jnp.bfloat16), "seq", scatter_dimension=0, tiled=True
        ).astype(jnp.float32),
    )
    grad_in, grad_out = (
        lax.psum_scatter(
            grad_in.astype(jnp.bfloat16), "dp", scatter_dimension=1, tiled=True
        ).astype(jnp.float32),
        lax.psum_scatter(
            grad_out.astype(jnp.bfloat16), "dp", scatter_dimension=1, tiled=True
        ).astype(jnp.float32),
    )
    return (blocks_out, grad_video, grad_in, grad_out)


def solution(mesh):
    in_specs = (P("dp", "seq", None, None), P(), P(), P(), P(), P("dp", "seq", None, None))
    out_specs = (
        P("dp", "seq", None, None),
        P("dp", "seq", None, None),
        P("seq", "dp"),
        P("seq", "dp"),
    )
    return jax.shard_map(local, mesh=mesh, in_specs=in_specs, out_specs=out_specs, check_vma=False)
```

profile of v0, /device:TPU:8, one launch (start us, length us, event | category | flops | bytes accessed | tf_op | source)
XLA Modules:
  0.0 617.0 jit_solution(4988626145081766134)
XLA Ops:
  7.2 10.8 %all-to-all-start.2 = ((bf16[1,1,32,8,1152]{4,3,1,0,2:T(8,128)(2,1)}), bf16[1,1,32,8,1152]{4,3,1,0,2:T(8,128)(2,1)}, u32[]{:S(2)}, u32[]{:S(2)}) async-start(bf16[1,1,32,8,1152]{4,3,1,0,2:T(8,128)(2,1)} %bitcast.181), calls=%async_computation.2 | async-start | bytes 1179648 | tf_op jit(solution)/shard_map/all_to_all | solution.py:106
  18.5 3.6 convolution_convert_fusion.3
  26.2 1.4 convolution_convert_fusion.2
  27.6 1.4 copy.58
  29.0 8.5 %all-to-all-done.2 = bf16[1,1,32,8,1152]{4,3,1,0,2:T(8,128)(2,1)} async-done(((bf16[1,1,32,8,1152]{4,3,1,0,2:T(8,128)(2,1)}), bf16[1,1,32,8,1152]{4,3,1,0,2:T(8,128)(2,1)}, u32[]{:S(2)}, u32[]{:S(2)}) %all-to-all-start.2) | async-done | bytes 589856 | tf_op jit(solution)/shard_map/all_to_all | solution.py:106
  37.5 4.7 all-to-all-start
  44.1 2.6 convolution_convert_fusion.9
  46.7 1.9 copy.69
  48.6 2.3 reshape.259
  50.9 17.6 %all-to-all-done = bf16[1,1,32,8,1728]{4,3,1,0,2:T(8,128)(2,1)S(1)} async-done(((bf16[1,1,32,8,1728]{4,3,1,0,2:T(8,128)(2,1)}), bf16[1,1,32,8,1728]{4,3,1,0,2:T(8,128)(2,1)S(1)}, u32[]{:S(2)}, u32[]{:S(2)}) %all-to-all-start) | async-done | bytes 884768 | tf_op jit(solution)/shard_map/all_to_all | solution.py:91
  68.4 2.6 reshape.276
  71.1 2.5 fusion.63
  73.6 2.1 fusion.42
  75.7 2.2 fusion.17
  79.0 2.1 multiply_reduce_fusion.2
  82.1 2.2 reshape.268
  84.3 2.2 reshape.252
  86.5 1.8 copy.66
  88.4 4.9 all-to-all-start.1
  93.5 2.8 convolution_convert_fusion.1
  96.4 2.5 fusion.15
  98.9 1.3 fusion.14
  100.7 1.8 copy.73
  102.4 2.8 reshape.260
  105.3 1.4 copy.74
  107.8 8.8 %all-to-all-start.3 = ((bf16[1,32,1,8,1728]{4,3,2,0,1:T(8,128)(2,1)}), bf16[1,32,1,8,1728]{4,3,2,0,1:T(8,128)(2,1)S(1)}, u32[]{:S(2)}, u32[]{:S(2)}) async-start(bf16[1,32,1,8,1728]{4,3,2,0,1:T(8,128)(2,1)} %copy.74), calls=%async_computation.3 | async-start | bytes 1835008 | tf_op jit(solution)/shard_map/all_to_all | solution.py:134
  119.8 248.7 %all-reduce.9.cloned.1.call-done = bf16[576,1152]{1,0:T(8,128)(2,1)} async-done(((bf16[576,1152]{1,0:T(8,128)(2,1)}), bf16[576,1152]{1,0:T(8,128)(2,1)}) %all-reduce.9.cloned.1.call-update) | async-done | bytes 1327120
  370.4 2.9 fusion.4
  373.3 35.3 %reduce-scatter.7.cloned.1.call-done = bf16[144,18]{1,0:T(8,128)(2,1)} async-done(((bf16[1152,18]{1,0:T(8,128)(2,1)}), bf16[144,18]{1,0:T(8,128)(2,1)}) %reduce-scatter.7.cloned.1.call-update) | async-done | bytes 5200
  410.0 4.5 fusion.24
  414.5 1.4 reduce_sum.115
  415.9 1.8 fusion.27
  418.4 1.2 copy-done.10
  419.6 1.2 fusion.30
  421.5 2.4 fusion.29
  423.9 2.1 fusion.28
  426.0 3.3 convolution_convert_fusion
  429.4 83.8 %fusion = bf16[40,1728]{1,0:T(8,128)(2,1)S(1)} fusion(bf16[1152,1728]{1,0:T(8,128)(2,1)} %convolution_convert_fusion), kind=kCustom, calls=%all-reduce-scatter | all-reduce-scatter fusion | flops 2211841 | bytes 4120576
  513.2 1.4 collective-permute-start.2
  514.6 1.3 collective-permute-start.1
  515.9 2.0 collective-permute-start
  518.0 4.6 fusion.18
  523.2 1.5 reduce_sum.118
  524.6 1.3 collective-permute-start.3
  527.3 1.7 concatenate
  529.8 2.6 fusion.22
  532.3 76.7 %all-reduce.7.cloned.1.call-done = bf16[36,1728]{1,0:T(8,128)(2,1)} async-done(((bf16[36,1728]{1,0:T(8,128)(2,1)}), bf16[36,1728]{1,0:T(8,128)(2,1)}) %all-reduce.7.cloned.1.call-update) | async-done | bytes 124432
  609.0 1.4 dynamic-slice_convert_fusion
  (104 shorter events, 18.8 us)
Async XLA Ops:
  7.2 16.9 %copy-start = (bf16[576,1152]{1,0:T(8,128)(2,1)S(1)}, bf16[576,1152]{1,0:T(8,128)(2,1)}, u32[]{:S(2)}) copy-start(bf16[576,1152]{1,0:T(8,128)(2,1)} %param.8) | copy-start | bytes 3981316
  7.2 10.9 %copy-start.2 = (bf16[1,1,256,1152]{3,2,1,0:T(8,128)(2,1)S(1)}, bf16[1,1,256,1152]{3,2,1,0:T(8,128)(2,1)}, u32[]{:S(2)}) copy-start(bf16[1,1,256,1152]{3,2,1,0:T(8,128)(2,1)} %param.6) | copy-start | bytes 1769476
  7.2 30.3 %all-to-all-start.2 = ((bf16[1,1,32,8,1152]{4,3,1,0,2:T(8,128)(2,1)}), bf16[1,1,32,8,1152]{4,3,1,0,2:T(8,128)(2,1)}, u32[]{:S(2)}, u32[]{:S(2)}) async-start(bf16[1,1,32,8,1152]{4,3,1,0,2:T(8,128)(2,1)} %bitcast.181), calls=%async_computation.2 | async-start | bytes 1179648 | tf_op jit(solution)/shard_map/all_to_all | solution.py:106
  18.2 3.9 copy-start.23
  18.5 3.6 copy-start.27
  22.1 0.9 copy-start.13
  22.7 1.3 copy-start.9
  22.7 1.3 copy-start.25
  24.0 2.1 copy-start.30
  24.8 0.5 copy-start.19
  25.3 0.5 copy-start.21
  37.5 31.0 %all-to-all-start = ((bf16[1,1,32,8,1728]{4,3,1,0,2:T(8,128)(2,1)}), bf16[1,1,32,8,1728]{4,3,1,0,2:T(8,128)(2,1)S(1)}, u32[]{:S(2)}, u32[]{:S(2)}) async-start(bf16[1,1,32,8,1728]{4,3,1,0,2:T(8,128)(2,1)} %bitcast.11), calls=%async_computation | async-start | bytes 1835008 | tf_op jit(solution)/shard_map/all_to_all | solution.py:91
  43.3 0.8 copy-start.6
  75.7 2.2 copy-start.5
  77.9 1.0 copy-start.4
  88.4 19.4 %all-to-all-start.1 = ((bf16[1,32,1,8,576]{4,3,2,0,1:T(8,128)(2,1)}), bf16[1,32,1,8,576]{4,3,2,0,1:T(8,128)(2,1)}, u32[]{:S(2)}, u32[]{:S(2)}) async-start(bf16[1,32,1,8,576]{4,3,2,0,1:T(8,128)(2,1)} %copy.66), calls=%async_computation.1 | async-start | bytes 655360 | tf_op jit(solution)/shard_map/all_to_all | solution.py:100
  93.3 275.1 %all-reduce.9.cloned.1.call-start = ((), (), s32[]{:S(2)}) async-start(), calls=%async_computation.7 | async-start | bytes 2654208
  96.4 2.5 copy-start.1
  96.4 2.5 copy-start.11
  96.4 2.5 copy-start.15
  98.9 1.4 copy-start.12
  106.7 9.9 %copy-start.31 = (u32[256]{0:T(256)S(1)}, u32[256]{0:T(256)}, u32[]{:S(2)}) copy-start(u32[256]{0:T(256)} %constant.25) | copy-start | bytes 3076
  106.7 11.2 %copy-start.29 = (u32[256]{0:T(256)S(1)}, u32[256]{0:T(256)}, u32[]{:S(2)}) copy-start(u32[256]{0:T(256)} %constant.21) | copy-start | bytes 3076
  107.8 302.3 %all-to-all-start.3 = ((bf16[1,32,1,8,1728]{4,3,2,0,1:T(8,128)(2,1)}), bf16[1,32,1,8,1728]{4,3,2,0,1:T(8,128)(2,1)S(1)}, u32[]{:S(2)}, u32[]{:S(2)}) async-start(bf16[1,32,1,8,1728]{4,3,2,0,1:T(8,128)(2,1)} %copy.74), calls=%async_computation.3 | async-start | bytes 1835008 | tf_op jit(solution)/shard_map/all_to_all | solution.py:134
  116.6 291.9 %reduce-scatter.7.cloned.1.call-start = ((), (), s32[]{:S(2)}) async-start(), calls=%async_computation.5 | async-start | bytes 331776
  370.3 39.7 %copy-start.20 = (f32[256]{0:T(256)S(1)}, f32[256]{0:T(256)}, u32[]{:S(2)}) copy-start(f32[256]{0:T(256)} %copy-done.19) | copy-start | bytes 3076
  370.3 39.7 %copy-start.22 = (f32[256]{0:T(256)S(1)}, f32[256]{0:T(256)}, u32[]{:S(2)}) copy-start(f32[256]{0:T(256)} %copy-done.21) | copy-start | bytes 3076
  370.3 238.7 %all-reduce.7.cloned.1.call-start = ((), (), s32[]{:S(2)}) async-start(), calls=%async_computation.6 | async-start | bytes 286720
  417.8 3.0 copy-start.7
  417.8 1.8 copy-start.10
  417.8 1.8 copy-start.26
  419.6 1.2 copy-start.14
  429.4 88.5 %copy-start.16 = (bf16[1,256,1,8,72]{1,4,3,2,0:T(8,128)(2,1)S(1)}, bf16[1,256,1,8,72]{1,4,3,2,0:T(8,128)(2,1)}, u32[]{:S(2)}) copy-start(bf16[1,256,1,8,72]{1,4,3,2,0:T(8,128)(2,1)} %fusion.30) | copy-start | bytes 884740
  429.4 88.5 %copy-start.17 = (bf16[1,256,1,8,72]{1,4,3,2,0:T(8,128)(2,1)S(1)}, bf16[1,256,1,8,72]{1,4,3,2,0:T(8,128)(2,1)}, u32[]{:S(2)}) copy-start(bf16[1,256,1,8,72]{1,4,3,2,0:T(8,128)(2,1)} %fusion.29) | copy-start | bytes 884740
  429.4 88.5 %copy-start.18 = (bf16[1,256,1,8,72]{1,4,3,2,0:T(8,128)(2,1)S(1)}, bf16[1,256,1,8,72]{1,4,3,2,0:T(8,128)(2,1)}, u32[]{:S(2)}) copy-start(bf16[1,256,1,8,72]{1,4,3,2,0:T(8,128)(2,1)} %fusion.28) | copy-start | bytes 884740
  513.1 4.9 copy-start.3
  513.1 4.9 copy-start.24
  513.2 4.9 copy-start.28
  513.2 14.1 %collective-permute-start.2 = (bf16[40,1728]{1,0:T(8,128)(2,1)S(1)}, bf16[40,1728]{1,0:T(8,128)(2,1)S(1)}, u32[]{:S(2)}, u32[]{:S(2)}) collective-permute-start(bf16[40,1728]{1,0:T(8,128)(2,1)S(1)} %fusion), channel_id=1, source_target_pairs={{0,24},{8,32},{16,40},{24,48},{32,56},{40,64},{48,72},{56,80},{64,... | collective-permute-start | bytes 414728
  514.6 12.7 %collective-permute-start.1 = (bf16[40,1728]{1,0:T(8,128)(2,1)S(1)}, bf16[40,1728]{1,0:T(8,128)(2,1)S(1)}, u32[]{:S(2)}, u32[]{:S(2)}) collective-permute-start(bf16[40,1728]{1,0:T(8,128)(2,1)S(1)} %fusion), channel_id=1, source_target_pairs={{0,16},{8,24},{16,32},{24,40},{32,48},{40,56},{48,64},{56,72},{64,... | collective-permute-start | bytes 414728
  515.9 11.4 %collective-permute-start = (bf16[40,1728]{1,0:T(8,128)(2,1)S(1)}, bf16[40,1728]{1,0:T(8,128)(2,1)}, u32[]{:S(2)}, u32[]{:S(2)}) collective-permute-start(bf16[40,1728]{1,0:T(8,128)(2,1)S(1)} %fusion), channel_id=1, source_target_pairs={{0,8},{8,16},{16,24},{24,32},{32,40},{40,48},{48,56},{56,64},{64,7... | collective-permute-start | bytes 414728
  523.2 6.6 %copy-start.8 = (bf16[1,1,256,1152]{3,2,1,0:T(8,128)(2,1)S(1)}, bf16[1,1,256,1152]{3,2,1,0:T(8,128)(2,1)}, u32[]{:S(2)}) copy-start(bf16[1,1,256,1152]{3,2,1,0:T(8,128)(2,1)} %copy-done.7) | copy-start | bytes 1769476
  524.6 2.7 collective-permute-start.3
Sparse Core Ops, SparseCore 0:
  96.8 271.6 all-reduce.8
  371.7 36.8 reduce-scatter.6
  529.9 79.1 all-reduce.6
where the time goes:
time: 621 us; the launch traced here: 617 us
  waiting for transfers between devices  389 us (63%)
  blocking collectives  83.8 us (13%)
  matrix products  45.3 us (7%)
  local copies, waits for them, and re-layouts  35.9 us (6%)
  starting transfers between devices  35.5 us (6%)
  between operations  16.2 us (3%)
  other arithmetic  11.8 us (2%)
    unnamed x10, waiting for transfers between devices  362 us
    unnamed x1, blocking collectives  83.8 us
    all_to_all x1, waiting for transfers between devices, local(): lax.all_to_all(temporal_qkv, 'seq', split_axis=2, concat_axis=1, tiled=True)  17.6 us
  transfers between devices with their start and end apart: 11, of which 7 were waited for; matrix products, arithmetic and copies ran while one was open for 8% of the time, Pallas kernels for 0%

commit v1 on v0

v1 whole, which is shorter than its diff:
```python
import jax
import jax.numpy as jnp
from jax import lax
from jax.sharding import PartitionSpec as P

HEADS = 8
HEAD = 72
F32 = jnp.float32
BF16 = jnp.bfloat16


def norm_forward(inputs):
    center = inputs - jnp.mean(inputs, -1, keepdims=True)
    inverse = lax.rsqrt(jnp.mean(center * center, -1, keepdims=True) + 1e-06)
    return (center * inverse, inverse)


def norm_backward(normed, inverse, incoming):
    return inverse * (
        incoming
        - jnp.mean(incoming, -1, keepdims=True)
        - normed * jnp.mean(incoming * normed, -1, keepdims=True)
    )


def dot(a, b):
    return jnp.dot(a, b, preferred_element_type=F32)


def dot_t(a, b):
    return lax.dot_general(a, b, (((1,), (1,)), ((), ())), preferred_element_type=F32)


def t_dot(a, b):
    return lax.dot_general(a, b, (((0,), (0,)), ((), ())), preferred_element_type=F32)


def forward_heads(qkv, mask, factor):
    rows = qkv.shape[0]
    q, k, v = [t.reshape(rows, HEADS, HEAD) for t in jnp.split(qkv, 3, axis=1)]
    scores = jnp.einsum("lhd,mhd->hlm", q, k, preferred_element_type=F32) * factor
    exponent = jnp.exp(scores)
    if mask is not None:
        exponent = jnp.where(mask, exponent, 0.0)
    shares = exponent / jnp.sum(exponent, -1, keepdims=True)
    weights = shares.astype(BF16)
    att = jnp.einsum("hlm,mhd->lhd", weights, v, preferred_element_type=F32).astype(BF16)
    return att.reshape(rows, HEADS * HEAD), shares, weights


def backward_heads(qkv, shares, weights, incoming, factor):
    rows = qkv.shape[0]
    q, k, v = [t.reshape(rows, HEADS, HEAD) for t in jnp.split(qkv, 3, axis=1)]
    g = incoming.reshape(rows, HEADS, HEAD)
    gv = jnp.einsum("hlm,lhd->mhd", weights, g, preferred_element_type=F32)
    e = jnp.einsum("lhd,mhd->hlm", g, v, preferred_element_type=F32)
    r = shares * (e - jnp.sum(e * shares, -1, keepdims=True)) * factor
    r = r.astype(BF16)
    gq = jnp.einsum("hlm,mhd->lhd", r, k, preferred_element_type=F32)
    gk = jnp.einsum("hlm,lhd->mhd", r, q, preferred_element_type=F32)
    return jnp.stack([gq.astype(BF16), gk.astype(BF16), gv.astype(BF16)], 1).reshape(rows, -1)


def scatter_sum(grad, groups_seq):
    rows, cols = grad.shape
    n_dp = lax.axis_size("dp")
    n_seq = lax.axis_size("seq")
    pairs = [(2 * i, 2 * i + 1) for i in range(n_seq // 2)]
    same = [tuple(range(c, n_seq, 2)) for c in range(2)]
    piece_r, piece_c = rows // n_seq, cols // n_dp
    x = grad.astype(BF16).reshape(n_seq // 2, 2, piece_r, cols)
    x = jnp.swapaxes(x, 0, 1)
    x = lax.all_to_all(x, "seq", 0, 0, axis_index_groups=pairs, tiled=True)
    x = jnp.sum(x.astype(F32), 0).astype(BF16)
    x = x.reshape(n_seq // 2 * piece_r, n_dp, piece_c)
    x = jnp.swapaxes(x, 0, 1)
    x = lax.all_to_all(x, "dp", 0, 0, tiled=True)
    x = jnp.sum(x.astype(F32), 0).astype(BF16)
    x = x.reshape(n_seq // 2, piece_r, piece_c)
    x = lax.all_to_all(x, "seq", 0, 0, axis_index_groups=same, tiled=True)
    return jnp.sum(x.astype(F32), 0)


def local(video, spatial_in, spatial_out, temporal_in, temporal_out, cotangent):
    width = video.shape[-1]
    places = video.shape[2]
    rows = places
    groups = lax.axis_size("seq")
    spread = places // groups
    factor = HEAD ** (-0.5)
    cot = cotangent.reshape(rows, width)
    vid = video.reshape(rows, width).astype(F32)

    def swap(x):
        y = lax.all_to_all(x.reshape(groups, spread, x.shape[-1]), "seq", 0, 0, tiled=True)
        return y.reshape(rows, x.shape[-1])

    grad_att = swap(dot_t(cot, temporal_out).astype(BF16))
    s_norm, s_inv = norm_forward(vid)
    s_qkv = dot(s_norm.astype(BF16), spatial_in).astype(BF16)
    s_att, s_shares, s_weights = forward_heads(s_qkv, None, factor)
    residual = (vid + dot(s_att, spatial_out)).astype(BF16)
    t_norm, t_inv = norm_forward(residual.astype(F32))
    h = swap(t_norm.astype(BF16))
    qkv = dot(h, temporal_in).astype(BF16)
    place = lax.broadcasted_iota(jnp.int32, (rows, rows), 0) % spread
    other = lax.broadcasted_iota(jnp.int32, (rows, rows), 1) % spread
    mask = (place == other)[None]
    att, shares, weights = forward_heads(qkv, mask, factor)
    frame_att = swap(att)
    g_qkv = backward_heads(qkv, shares, weights, grad_att, factor)
    grad_in = scatter_sum(t_dot(h, g_qkv), groups)
    g_h = swap(dot_t(g_qkv, temporal_in).astype(BF16)).astype(F32)
    grad_out = scatter_sum(t_dot(frame_att, cot), groups)
    blocks_out = (residual.astype(F32) + dot(frame_att, temporal_out)).astype(BF16)
    grad_res = (cot.astype(F32) + norm_backward(t_norm, t_inv, g_h)).astype(BF16)
    g_spatial = dot_t(grad_res, spatial_out).astype(BF16)
    g_sqkv = backward_heads(s_qkv, s_shares, s_weights, g_spatial, factor)
    g_sh = dot_t(g_sqkv, spatial_in)
    grad_video = (grad_res.astype(F32) + norm_backward(s_norm, s_inv, g_sh)).astype(BF16)
    return (blocks_out.reshape(video.shape), grad_video.reshape(video.shape), grad_in, grad_out)


def solution(mesh):
    in_specs = (P("dp", "seq", None, None), P(), P(), P(), P(), P("dp", "seq", None, None))
    out_specs = (
        P("dp", "seq", None, None),
        P("dp", "seq", None, None),
        P("seq", "dp"),
        P("seq", "dp"),
    )
    return jax.shard_map(local, mesh=mesh, in_specs=in_specs, out_specs=out_specs, check_vma=False)
```

time: 621 us -> 270 us (0.43)
  waiting for transfers between devices: 389 us -> 57.5 us
  blocking collectives: 83.8 us -> 6.84 us
  local copies, waits for them, and re-layouts: 35.9 us -> 60.8 us
  starting transfers between devices: 35.5 us -> 59.3 us
  between operations: 16.2 us -> 1.04 us
  matrix products: 45.3 us -> 58.3 us
  other arithmetic: 11.8 us -> 22.3 us
    unnamed x10 -> x0, waiting for transfers between devices: 362 us -> none
    unnamed x1 -> x0, blocking collectives: 83.8 us -> none
    all_to_all x4 -> x9, waiting for transfers between devices: 27.1 us -> 57.5 us  [the longest x4 22 us: swap(): lax.all_to_all(x.reshape(groups, spread, x.shape[-1]), 'seq', 0, 0, tiled...]
    all_to_all x4 -> x9, starting transfers between devices: 29.3 us -> 59.3 us  [the longest x4 29.9 us: swap(): lax.all_to_all(x.reshape(groups, spread, x.shape[-1]), 'seq', 0, 0, tiled...]
    transpose x0 -> x4, local copies, waits for them, and re-layouts: none -> 15.7 us  [scatter_sum(): x = jnp.swapaxes(x, 0, 1)]
    dot_general x21 -> x22, matrix products: 43.1 us -> 58.3 us  [the longest x4 10.8 us: dot(): return jnp.dot(a, b, preferred_element_type=F32)]
    reduce_sum x0 -> x7, other arithmetic: none -> 13.5 us  [the longest x4 10.8 us: scatter_sum(): x = jnp.sum(x.astype(F32), 0).astype(BF16)]
    all_to_all x0 -> x1, blocking collectives: none -> 6.84 us  [scatter_sum(): x = lax.all_to_all(x, 'seq', 0, 0, axis_index_groups=pairs, tiled=True)]
  transfers between devices with their start and end apart: 11 -> 9, of which waited for: 7 -> 6; matrix products, arithmetic and copies ran while one was open for 8% -> 41% of each run, Pallas kernels for 0% -> 0%
where the time goes in v1:
time: 270 us; the launch traced here: 266 us
  local copies, waits for them, and re-layouts  60.8 us (23%)
  starting transfers between devices  59.3 us (22%)
  matrix products  58.3 us (22%)
  waiting for transfers between devices  57.5 us (21%)
  other arithmetic  22.3 us (8%)
  blocking collectives  6.84 us (3%)
    all_to_all x4, starting transfers between devices, swap(): lax.all_to_all(x.reshape(groups, spread, x.shape[-1]), 'seq', 0, 0, tiled...  29.9 us
    all_to_all x4, waiting for transfers between devices, swap(): lax.all_to_all(x.reshape(groups, spread, x.shape[-1]), 'seq', 0, 0, tiled...  22 us
    all_to_all x2, waiting for transfers between devices, scatter_sum(): x = lax.all_to_all(x, 'dp', 0, 0, tiled=True)  18.5 us
    all_to_all x2, waiting for transfers between devices, scatter_sum(): x = lax.all_to_all(x, 'seq', 0, 0, axis_index_groups=same, tiled=True)  17 us
    transpose x4, local copies, waits for them, and re-layouts, scatter_sum(): x = jnp.swapaxes(x, 0, 1)  15.7 us
    all_to_all x2, starting transfers between devices, scatter_sum(): x = lax.all_to_all(x, 'seq', 0, 0, axis_index_groups=same, tiled=True)  12.6 us
    all_to_all x2, starting transfers between devices, scatter_sum(): x = lax.all_to_all(x, 'dp', 0, 0, tiled=True)  11.1 us
    reduce_sum x4, other arithmetic, scatter_sum(): x = jnp.sum(x.astype(F32), 0).astype(BF16)  10.8 us
  transfers between devices with their start and end apart: 9, of which 6 were waited for; matrix products, arithmetic and copies ran while one was open for 41% of the time, Pallas kernels for 0%

profile of v1, /device:TPU:8, one launch (start us, length us, event | category | flops | bytes accessed | tf_op | source)
XLA Modules:
  0.0 266.2 jit_solution(11140385660173879692)
XLA Ops:
  0.7 2.2 convolution_convert_fusion.6
  3.8 10.6 %all-to-all-start.2 = ((bf16[32,8,576]{2,1,0:T(8,128)(2,1)}), bf16[32,8,576]{2,1,0:T(8,128)(2,1)S(1)}, u32[]{:S(2)}, u32[]{:S(2)}) async-start(bf16[32,8,576]{2,1,0:T(8,128)(2,1)} %bitcast.15), calls=%async_computation.2 | async-start | bytes 655360 | tf_op jit(solution)/shard_map/all_to_all | solution.py:95
  14.9 3.6 %convolution_convert_fusion.3 = bf16[256,1728]{0,1:T(8,128)(2,1)S(1)} fusion(bf16[1152,1728]{0,1:T(8,128)(2,1)} %param.7, bf16[1,1,256,1152]{3,2,1,0:T(8,128)(2,1)S(1)} %copy-done.1, f32[256]{0:T(256)S(1)} %add_rsqrt_fusion.1, f32[256]{0:T(256)S(1)} %broadcast_multiply_fusion.5), kind=kOutput, calls=%fused_computation.9 | convolution fusion | flops 1020837888 | bytes 5457920 | tf_op jit(solution)/shard_map/dot_general | solution.py:27
  23.2 5.6 %all-to-all-done.2 = bf16[32,8,576]{2,1,0:T(8,128)(2,1)S(1)} async-done(((bf16[32,8,576]{2,1,0:T(8,128)(2,1)}), bf16[32,8,576]{2,1,0:T(8,128)(2,1)S(1)}, u32[]{:S(2)}, u32[]{:S(2)}) %all-to-all-start.2) | async-done | bytes 294944 | tf_op jit(solution)/shard_map/all_to_all | solution.py:95
  28.8 4.8 %all-to-all-start = ((bf16[32,8,1152]{2,1,0:T(8,128)(2,1)}), bf16[32,8,1152]{2,1,0:T(8,128)(2,1)}, u32[]{:S(2)}, u32[]{:S(2)}) async-start(bf16[32,8,1152]{2,1,0:T(8,128)(2,1)} %fusion.80), calls=%async_computation | async-start | bytes 1179648 | tf_op jit(solution)/shard_map/all_to_all | solution.py:95
  36.5 16.4 %all-to-all-done = bf16[32,8,1152]{2,1,0:T(8,128)(2,1)} async-done(((bf16[32,8,1152]{2,1,0:T(8,128)(2,1)}), bf16[32,8,1152]{2,1,0:T(8,128)(2,1)}, u32[]{:S(2)}, u32[]{:S(2)}) %all-to-all-start) | async-done | bytes 589856 | tf_op jit(solution)/shard_map/all_to_all | solution.py:95
  52.9 3.7 %convolution_convert_fusion.2 = bf16[256,1728]{0,1:T(8,128)(2,1)S(1)} fusion(bf16[1152,1728]{0,1:T(8,128)(2,1)} %param.9, bf16[32,8,1152]{2,1,0:T(8,128)(2,1)} %all-to-all-done), kind=kOutput, calls=%fused_computation.8 | convolution fusion | flops 1019658240 | bytes 5455872 | tf_op jit(solution)/shard_map/dot_general | solution.py:27
  58.5 2.0 fusion.28
  60.5 5.6 %fusion.63 = bf16[256,1,8,72]{0,3,2,1:T(8,128)(2,1)} fusion(bf16[256,8,72]{0,2,1:T(8,128)(2,1)} %bitcast.162, f32[8,256,256]{1,2,0:T(8,128)} %fusion.120, f32[8,256,256]{1,2,0:T(8,128)} %get-tuple-element.17, f32[8,256]{1,0:T(8,128)S(1)} %get-tuple-element.16, pred[256,256]{0,1:T(8,128)(4,1)S(1)} %select_compare_fusion), kind=kOutput, calls=%fused_computation.65 | convolution fusion | flops 81414400 | bytes 4857856 | tf_op jit(solution)/shard_map/hlm,mhd->lhd/dot_general | solution.py:59
  66.1 5.6 %fusion.60 = bf16[256,1,8,72]{0,3,2,1:T(8,128)(2,1)} fusion(bf16[256,8,72]{0,2,1:T(8,128)(2,1)} %bitcast.160, f32[8,256,256]{1,2,0:T(8,128)} %fusion.120, f32[8,256,256]{1,2,0:T(8,128)} %get-tuple-element.17, f32[8,256]{1,0:T(8,128)S(1)} %get-tuple-element.16, pred[256,256]{0,1:T(8,128)(4,1)S(1)} %select_compare_fusion), kind=kOutput, calls=%fused_computation.64 | convolution fusion | flops 81414400 | bytes 4857856 | tf_op jit(solution)/shard_map/hlm,lhd->mhd/dot_general | solution.py:60
  71.7 3.1 %fusion.73 = bf16[256,1,8,72]{0,3,2,1:T(8,128)(2,1)} fusion(bf16[256,8,72]{0,2,1:T(8,128)(2,1)S(1)} %copy.52, f32[8,256,256]{1,2,0:T(8,128)} %get-tuple-element.17, f32[8,256]{1,0:T(8,128)S(1)} %get-tuple-element.16, pred[256,256]{0,1:T(8,128)(4,1)S(1)} %select_compare_fusion), kind=kOutput, calls=%fused_computation.69 | convolution fusion | flops 77742080 | bytes 2760704 | tf_op jit(solution)/shard_map/hlm,lhd->mhd/dot_general | solution.py:55
  76.5 2.2 reshape_reshape.6
  78.7 4.7 %all-to-all-start.1 = ((bf16[32,8,576]{2,1,0:T(8,128)(2,1)}), bf16[32,8,576]{2,1,0:T(8,128)(2,1)S(1)}, u32[]{:S(2)}, u32[]{:S(2)}) async-start(bf16[32,8,576]{2,1,0:T(8,128)(2,1)} %reshape_reshape.6), calls=%async_computation.1 | async-start | bytes 655360 | tf_op jit(solution)/shard_map/all_to_all | solution.py:95
  85.6 4.4 %convolution_convert_fusion = bf16[1152,1728]{0,1:T(8,128)(2,1)} fusion(bf16[256,1728]{0,1:T(8,128)(2,1)S(1)} %bitcast.146, bf16[32,8,1152]{2,1,0:T(8,128)(2,1)} %all-to-all-done), kind=kOutput, calls=%fused_computation.2 | convolution fusion | flops 1021206528 | bytes 5455872 | tf_op jit(solution)/shard_map/dot_general | solution.py:35
  89.9 6.4 %copy.60 = bf16[1152,1728]{1,0:T(8,128)(2,1)} copy(bf16[1152,1728]{0,1:T(8,128)(2,1)} %convolution_convert_fusion) | data formatting | bytes 7962624 | tf_op jit(solution)/shard_map/convert_element_type | solution.py:71
  96.4 6.9 %reshape.237 = bf16[16,2,36,1728]{3,2,1,0:T(8,128)(2,1)} reshape(bf16[1152,1728]{1,0:T(8,128)(2,1)} %copy.60) | data formatting | bytes 7962624 | tf_op jit(solution)/shard_map/reshape | solution.py:71
  103.3 5.7 %copy.61 = bf16[2,16,36,1728]{3,1,2,0:T(8,128)(2,1)} copy(bf16[2,16,36,1728]{3,2,0,1:T(8,128)(2,1)} %bitcast.143) | data formatting | bytes 7962624 | tf_op jit(solution)/shard_map/transpose | solution.py:72
  109.0 2.2 fusion.5
  111.2 5.6 %all-to-all-start.4 = ((bf16[2,16,36,1728]{3,1,2,0:T(8,128)(2,1)}), bf16[2,16,36,1728]{3,1,2,0:T(8,128)(2,1)}, u32[]{:S(2)}, u32[]{:S(2)}) async-start(bf16[2,16,36,1728]{3,1,2,0:T(8,128)(2,1)} %copy.61), calls=%async_computation.4 | async-start | bytes 8257536 | tf_op jit(solution)/shard_map/all_to_all | solution.py:73
  116.9 2.7 %convolution_convert_fusion.1 = bf16[576,1152]{1,0:T(8,128)(2,1)} fusion(bf16[1,1,256,1152]{3,2,1,0:T(8,128)(2,1)} %param.11, bf16[32,8,576]{2,1,0:T(8,128)(2,1)S(1)} %all-to-all-done.1), kind=kOutput, calls=%fused_computation.3 | convolution fusion | flops 340402176 | bytes 2211840 | tf_op jit(solution)/shard_map/dot_general | solution.py:35
  119.6 3.3 %reshape.240 = bf16[16,2,18,1152]{3,2,1,0:T(8,128)(2,1)} reshape(bf16[576,1152]{1,0:T(8,128)(2,1)} %convolution_convert_fusion.1) | data formatting | bytes 2654208 | tf_op jit(solution)/shard_map/reshape | solution.py:71
  122.9 2.8 %copy.65 = bf16[2,16,18,1152]{3,1,2,0:T(8,128)(2,1)} copy(bf16[2,16,18,1152]{3,2,0,1:T(8,128)(2,1)} %bitcast.145) | data formatting | bytes 2654208 | tf_op jit(solution)/shard_map/transpose | solution.py:72
  125.7 6.8 %all_to_all.50 = bf16[2,16,18,1152]{3,1,2,0:T(8,128)(2,1)} all-to-all(bf16[2,16,18,1152]{3,1,2,0:T(8,128)(2,1)} %copy.65), channel_id=1, replica_groups={{0,8},{16,24},{32,40},{48,56},{64,72},{80,88},{96,104},{112,120},{128,1..., dimensions={0} | all-to-all | bytes 2654208 | tf_op jit(solution)/shard_map/all_to_all | solution.py:73
  132.5 9.9 %all-to-all-start.3 = ((bf16[32,8,1152]{2,1,0:T(8,128)(2,1)}), bf16[32,8,1152]{2,1,0:T(8,128)(2,1)}, u32[]{:S(2)}, u32[]{:S(2)}) async-start(bf16[32,8,1152]{2,1,0:T(8,128)(2,1)} %fusion.5), calls=%async_computation.3 | async-start | bytes 1179648 | tf_op jit(solution)/shard_map/all_to_all | solution.py:95
  142.4 4.9 %reduce_sum.186 = bf16[16,36,1728]{2,0,1:T(8,128)(2,1)} reduce(bf16[2,16,36,1728]{3,1,2,0:T(8,128)(2,1)} %all-to-all-done.4, bf16[]{:T(256)} %constant.39.clone.1), dimensions={0}, to_apply=%region_12.13 | reduce | flops 995328 | bytes 5971970 | tf_op jit(solution)/shard_map/reduce_sum | solution.py:74
  147.3 3.6 %copy.62 = bf16[16,36,1728]{2,1,0:T(8,128)(2,1)} copy(bf16[16,36,1728]{2,0,1:T(8,128)(2,1)} %reduce_sum.186) | data formatting | bytes 3981312 | tf_op jit(solution)/shard_map/reduce_sum | solution.py:74
  150.8 6.2 %reshape.238 = bf16[576,8,216]{2,1,0:T(8,128)(2,1)} reshape(bf16[16,36,1728]{2,1,0:T(8,128)(2,1)} %copy.62) | data formatting | bytes 3981312 | tf_op jit(solution)/shard_map/reshape | solution.py:75
  157.0 4.8 %copy.63 = bf16[8,576,216]{1,2,0:T(8,128)(2,1)} copy(bf16[8,576,216]{2,0,1:T(8,128)(2,1)} %bitcast.144) | data formatting | bytes 3981312 | tf_op jit(solution)/shard_map/transpose | solution.py:76
  161.7 2.6 reduce_sum.189
  164.3 2.1 copy.66
  166.5 3.6 %reshape.241 = bf16[288,8,144]{2,1,0:T(8,128)(2,1)} reshape(bf16[16,18,1152]{2,1,0:T(8,128)(2,1)} %copy.66) | data formatting | bytes 1327104 | tf_op jit(solution)/shard_map/reshape | solution.py:75
  170.1 2.4 copy.67
  172.5 2.8 %fusion.6 = bf16[1,1,256,1152]{3,2,1,0:T(8,128)(2,1)} fusion(f32[256,1152]{1,0:T(8,128)S(1)} %get-tuple-element.15, bf16[576,1152]{1,0:T(8,128)(2,1)} %param.10, bf16[32,8,576]{2,1,0:T(8,128)(2,1)S(1)} %all-to-all-done.1), kind=kOutput, calls=%fused_computation.13 | convolution fusion | flops 340328448 | bytes 3391488 | tf_op jit(solution)/shard_map/dot_general | solution.py:27
  175.2 5.7 %all-to-all-start.8 = ((bf16[8,288,144]{1,2,0:T(8,128)(2,1)}), bf16[8,288,144]{1,2,0:T(8,128)(2,1)}, u32[]{:S(2)}, u32[]{:S(2)}) async-start(bf16[8,288,144]{1,2,0:T(8,128)(2,1)} %copy.67), calls=%async_computation.8 | async-start | bytes 1769472 | tf_op jit(solution)/shard_map/all_to_all | solution.py:77
  186.8 7.5 %all-to-all-done.8 = bf16[8,288,144]{1,2,0:T(8,128)(2,1)} async-done(((bf16[8,288,144]{1,2,0:T(8,128)(2,1)}), bf16[8,288,144]{1,2,0:T(8,128)(2,1)}, u32[]{:S(2)}, u32[]{:S(2)}) %all-to-all-start.8) | async-done | bytes 663584 | tf_op jit(solution)/shard_map/all_to_all | solution.py:77
  194.3 5.3 %all-to-all-start.5 = ((bf16[8,576,216]{1,2,0:T(8,128)(2,1)}), bf16[8,576,216]{1,2,0:T(8,128)(2,1)}, u32[]{:S(2)}, u32[]{:S(2)}) async-start(bf16[8,576,216]{1,2,0:T(8,128)(2,1)} %copy.63), calls=%async_computation.5 | async-start | bytes 4423680 | tf_op jit(solution)/shard_map/all_to_all | solution.py:77
  199.7 1.9 fusion.121
  201.5 4.6 %fusion.69 = bf16[256,1,8,72]{0,3,2,1:T(8,128)(2,1)S(1)} fusion(bf16[256,8,72]{0,2,1:T(8,128)(2,1)S(1)} %bitcast.152, f32[8,256,256]{1,2,0:T(8,128)} %fusion.121, f32[8,256,256]{1,2,0:T(8,128)} %copy-done.6, f32[8,256]{1,0:T(8,128)S(1)} %get-tuple-element.12), kind=kOutput, calls=%fused_computation.67 | convolution fusion | flops 80365824 | bytes 4792320 | tf_op jit(solution)/shard_map/hlm,mhd->lhd/dot_general | solution.py:59
  206.1 4.6 %fusion.66 = bf16[256,1,8,72]{0,3,2,1:T(8,128)(2,1)S(1)} fusion(bf16[256,8,72]{0,2,1:T(8,128)(2,1)S(1)} %bitcast.150, f32[8,256,256]{1,2,0:T(8,128)} %fusion.121, f32[8,256,256]{1,2,0:T(8,128)} %copy-done.6, f32[8,256]{1,0:T(8,128)S(1)} %get-tuple-element.12), kind=kOutput, calls=%fused_computation.66 | convolution fusion | flops 80365824 | bytes 4792320 | tf_op jit(solution)/shard_map/hlm,lhd->mhd/dot_general | solution.py:60
  210.7 2.2 fusion.74
  213.5 2.4 fusion.116
  218.3 11.1 %all-to-all-done.5 = bf16[8,576,216]{1,2,0:T(8,128)(2,1)} async-done(((bf16[8,576,216]{1,2,0:T(8,128)(2,1)}), bf16[8,576,216]{1,2,0:T(8,128)(2,1)}, u32[]{:S(2)}, u32[]{:S(2)}) %all-to-all-start.5) | async-done | bytes 1990688 | tf_op jit(solution)/shard_map/all_to_all | solution.py:77
  229.4 9.1 %all-to-all-start.9 = ((bf16[16,2,1296]{2,1,0:T(2,128)(2,1)}), bf16[16,2,1296]{2,1,0:T(2,128)(2,1)S(1)}, u32[]{:S(2)}, u32[]{:S(2)}) async-start(bf16[16,2,1296]{2,1,0:T(2,128)(2,1)} %reshape.244), calls=%async_computation.9 | async-start | bytes 180224 | tf_op jit(solution)/shard_map/all_to_all | solution.py:80
  238.5 2.1 reduce_sum.187
  241.5 7.7 %all-to-all-done.9 = bf16[16,2,1296]{2,1,0:T(2,128)(2,1)S(1)} async-done(((bf16[16,2,1296]{2,1,0:T(2,128)(2,1)}), bf16[16,2,1296]{2,1,0:T(2,128)(2,1)S(1)}, u32[]{:S(2)}, u32[]{:S(2)}) %all-to-all-start.9) | async-done | bytes 82976 | tf_op jit(solution)/shard_map/all_to_all | solution.py:80
  249.2 3.5 %all-to-all-start.6 = ((bf16[16,36,216]{2,1,0:T(8,128)(2,1)}), bf16[16,36,216]{2,1,0:T(8,128)(2,1)S(1)}, u32[]{:S(2)}, u32[]{:S(2)}) async-start(bf16[16,36,216]{2,1,0:T(8,128)(2,1)} %reshape.239), calls=%async_computation.6 | async-start | bytes 655360 | tf_op jit(solution)/shard_map/all_to_all | solution.py:80
  252.8 2.6 fusion.81
  256.2 9.3 %all-to-all-done.6 = bf16[16,36,216]{2,1,0:T(8,128)(2,1)S(1)} async-done(((bf16[16,36,216]{2,1,0:T(8,128)(2,1)}), bf16[16,36,216]{2,1,0:T(8,128)(2,1)S(1)}, u32[]{:S(2)}, u32[]{:S(2)}) %all-to-all-start.6) | async-done | bytes 248864 | tf_op jit(solution)/shard_map/all_to_all | solution.py:80
  (85 shorter events, 25.9 us)
Async XLA Ops:
  0.6 20.5 %copy-start = (bf16[576,1152]{1,0:T(8,128)(2,1)S(1)}, bf16[576,1152]{1,0:T(8,128)(2,1)}, u32[]{:S(2)}) copy-start(bf16[576,1152]{1,0:T(8,128)(2,1)} %param.8) | copy-start | bytes 3981316
  0.6 13.7 %copy-start.1 = (bf16[1,1,256,1152]{3,2,1,0:T(8,128)(2,1)S(1)}, bf16[1,1,256,1152]{3,2,1,0:T(8,128)(2,1)}, u32[]{:S(2)}) copy-start(bf16[1,1,256,1152]{3,2,1,0:T(8,128)(2,1)} %param.6) | copy-start | bytes 1769476
  3.8 25.0 %all-to-all-start.2 = ((bf16[32,8,576]{2,1,0:T(8,128)(2,1)}), bf16[32,8,576]{2,1,0:T(8,128)(2,1)S(1)}, u32[]{:S(2)}, u32[]{:S(2)}) async-start(bf16[32,8,576]{2,1,0:T(8,128)(2,1)} %bitcast.15), calls=%async_computation.2 | async-start | bytes 655360 | tf_op jit(solution)/shard_map/all_to_all | solution.py:95
  18.5 0.7 copy-start.7
  18.5 1.3 copy-start.9
  18.5 1.8 copy-start.11
  19.8 1.3 copy-start.6
  28.8 24.0 %all-to-all-start = ((bf16[32,8,1152]{2,1,0:T(8,128)(2,1)}), bf16[32,8,1152]{2,1,0:T(8,128)(2,1)}, u32[]{:S(2)}, u32[]{:S(2)}) async-start(bf16[32,8,1152]{2,1,0:T(8,128)(2,1)} %fusion.80), calls=%async_computation | async-start | bytes 1179648 | tf_op jit(solution)/shard_map/all_to_all | solution.py:95
  56.6 3.9 %copy-start.13 = (bf16[256,576]{0,1:T(8,128)(2,1)}, bf16[256,576]{0,1:T(8,128)(2,1)S(1)}, u32[]{:S(2)}) copy-start(bf16[256,576]{0,1:T(8,128)(2,1)S(1)} %get-tuple-element.8) | copy-start | bytes 884740
  56.6 3.8 %copy-start.15 = (bf16[256,576]{0,1:T(8,128)(2,1)}, bf16[256,576]{0,1:T(8,128)(2,1)S(1)}, u32[]{:S(2)}) copy-start(bf16[256,576]{0,1:T(8,128)(2,1)S(1)} %get-tuple-element.7) | copy-start | bytes 884740
  56.6 3.8 %copy-start.16 = (bf16[256,576]{0,1:T(8,128)(2,1)}, bf16[256,576]{0,1:T(8,128)(2,1)S(1)}, u32[]{:S(2)}) copy-start(bf16[256,576]{0,1:T(8,128)(2,1)S(1)} %get-tuple-element.6) | copy-start | bytes 884740
  71.7 3.1 %copy-start.14 = (bf16[256,576]{0,1:T(8,128)(2,1)S(1)}, bf16[256,576]{0,1:T(8,128)(2,1)}, u32[]{:S(2)}) copy-start(bf16[256,576]{0,1:T(8,128)(2,1)} %copy-done.13) | copy-start | bytes 884740
  71.7 3.1 %copy-start.19 = (f32[8,256,256]{1,2,0:T(8,128)S(1)}, f32[8,256,256]{1,2,0:T(8,128)}, u32[]{:S(2)}) copy-start(f32[8,256,256]{1,2,0:T(8,128)} %get-tuple-element.17) | copy-start | bytes 6291460
  78.7 32.5 %all-to-all-start.1 = ((bf16[32,8,576]{2,1,0:T(8,128)(2,1)}), bf16[32,8,576]{2,1,0:T(8,128)(2,1)S(1)}, u32[]{:S(2)}, u32[]{:S(2)}) async-start(bf16[32,8,576]{2,1,0:T(8,128)(2,1)} %reshape_reshape.6), calls=%async_computation.1 | async-start | bytes 655360 | tf_op jit(solution)/shard_map/all_to_all | solution.py:95
  84.7 0.9 copy-start.2
  103.3 5.7 %copy-start.3 = (bf16[256,3,8,72]{0,3,2,1:T(8,128)(2,1)S(1)}, bf16[256,3,8,72]{0,3,2,1:T(8,128)(2,1)}, u32[]{:S(2)}) copy-start(bf16[256,3,8,72]{0,3,2,1:T(8,128)(2,1)} %copy-done.2) | copy-start | bytes 2654212
  103.3 5.7 %copy-start.17 = (bf16[1152,1728]{0,1:T(8,128)(2,1)S(1)}, bf16[1152,1728]{0,1:T(8,128)(2,1)}, u32[]{:S(2)}) copy-start(bf16[1152,1728]{0,1:T(8,128)(2,1)} %param.9) | copy-start | bytes 11943940
  111.2 14.4 %all-to-all-start.4 = ((bf16[2,16,36,1728]{3,1,2,0:T(8,128)(2,1)}), bf16[2,16,36,1728]{3,1,2,0:T(8,128)(2,1)}, u32[]{:S(2)}, u32[]{:S(2)}) async-start(bf16[2,16,36,1728]{3,1,2,0:T(8,128)(2,1)} %copy.61), calls=%async_computation.4 | async-start | bytes 8257536 | tf_op jit(solution)/shard_map/all_to_all | solution.py:73
  132.5 42.7 %all-to-all-start.3 = ((bf16[32,8,1152]{2,1,0:T(8,128)(2,1)}), bf16[32,8,1152]{2,1,0:T(8,128)(2,1)}, u32[]{:S(2)}, u32[]{:S(2)}) async-start(bf16[32,8,1152]{2,1,0:T(8,128)(2,1)} %fusion.5), calls=%async_computation.3 | async-start | bytes 1179648 | tf_op jit(solution)/shard_map/all_to_all | solution.py:95
  175.2 19.1 %all-to-all-start.8 = ((bf16[8,288,144]{1,2,0:T(8,128)(2,1)}), bf16[8,288,144]{1,2,0:T(8,128)(2,1)}, u32[]{:S(2)}, u32[]{:S(2)}) async-start(bf16[8,288,144]{1,2,0:T(8,128)(2,1)} %copy.67), calls=%async_computation.8 | async-start | bytes 1769472 | tf_op jit(solution)/shard_map/all_to_all | solution.py:77
  185.4 0.8 copy-start.4
  186.8 12.8 %copy-start.12 = (bf16[256,576]{0,1:T(8,128)(2,1)S(1)}, bf16[256,576]{0,1:T(8,128)(2,1)}, u32[]{:S(2)}) copy-start(bf16[256,576]{0,1:T(8,128)(2,1)} %copy-done.11) | copy-start | bytes 884740
  194.3 35.1 %all-to-all-start.5 = ((bf16[8,576,216]{1,2,0:T(8,128)(2,1)}), bf16[8,576,216]{1,2,0:T(8,128)(2,1)}, u32[]{:S(2)}, u32[]{:S(2)}) async-start(bf16[8,576,216]{1,2,0:T(8,128)(2,1)} %copy.63), calls=%async_computation.5 | async-start | bytes 4423680 | tf_op jit(solution)/shard_map/all_to_all | solution.py:77
  199.6 1.9 copy-start.10
  201.5 4.6 %copy-start.8 = (bf16[256,576]{0,1:T(8,128)(2,1)S(1)}, bf16[256,576]{0,1:T(8,128)(2,1)}, u32[]{:S(2)}) copy-start(bf16[256,576]{0,1:T(8,128)(2,1)} %copy-done.7) | copy-start | bytes 884740
  210.7 2.8 %copy-start.18 = (bf16[1152,1728]{0,1:T(8,128)(2,1)S(1)}, bf16[1152,1728]{0,1:T(8,128)(2,1)}, u32[]{:S(2)}) copy-start(bf16[1152,1728]{0,1:T(8,128)(2,1)} %param.7) | copy-start | bytes 11943940
  229.4 19.8 %all-to-all-start.9 = ((bf16[16,2,1296]{2,1,0:T(2,128)(2,1)}), bf16[16,2,1296]{2,1,0:T(2,128)(2,1)S(1)}, u32[]{:S(2)}, u32[]{:S(2)}) async-start(bf16[16,2,1296]{2,1,0:T(2,128)(2,1)} %reshape.244), calls=%async_computation.9 | async-start | bytes 180224 | tf_op jit(solution)/shard_map/all_to_all | solution.py:80
  238.5 14.3 %copy-start.5 = (bf16[256,1152]{1,0:T(8,128)(2,1)S(1)}, bf16[256,1152]{1,0:T(8,128)(2,1)}, u32[]{:S(2)}) copy-start(bf16[256,1152]{1,0:T(8,128)(2,1)} %copy-done.4) | copy-start | bytes 1769476
  249.2 16.3 %all-to-all-start.6 = ((bf16[16,36,216]{2,1,0:T(8,128)(2,1)}), bf16[16,36,216]{2,1,0:T(8,128)(2,1)S(1)}, u32[]{:S(2)}, u32[]{:S(2)}) async-start(bf16[16,36,216]{2,1,0:T(8,128)(2,1)} %reshape.239), calls=%async_computation.6 | async-start | bytes 655360 | tf_op jit(solution)/shard_map/all_to_all | solution.py:80

commit v2 on v1

v2 whole, which is shorter than its diff:
```python
import jax
import jax.numpy as jnp
from jax import lax
from jax.experimental import pallas as pl
from jax.experimental.pallas import tpu as pltpu
from jax.sharding import PartitionSpec as P

HEADS = 8
HEAD = 72
D = 1152
HD = 576
N = 256
PAD = 640
FACTOR = HEAD ** (-0.5)
F32 = jnp.float32
BF16 = jnp.bfloat16
MESH = pl.DeviceIdType.MESH
CHUNK = 32
ROWS = 216
ZROWS = 64


def dot(a, b):
    return jnp.dot(a, b, preferred_element_type=F32)


def dot_nt(a, b):
    return lax.dot_general(a, b, (((1,), (1,)), ((), ())), preferred_element_type=F32)


def dot_tn(a, b):
    return lax.dot_general(a, b, (((0,), (0,)), ((), ())), preferred_element_type=F32)


def window(head):
    start = head * HEAD
    low = start // 128 * 128
    wide = 128 if start + HEAD <= low + 128 else 256
    return start - low, slice(low, low + wide), wide


def head_mask(offset, wide):
    lane = lax.broadcasted_iota(jnp.int32, (N, wide), 1)
    return (lane >= offset) & (lane < offset + HEAD)


def scratch_shapes():
    slab = (2, ROWS, 128)
    vm = lambda *shape: pltpu.VMEM(shape, BF16)
    vf = lambda *shape: pltpu.VMEM(shape, F32)
    dma = pltpu.SemaphoreType.DMA
    return dict(
        vid=vm(N, D), cot=vm(N, D), wsi=vm(D, 3 * HD), wso=vm(HD, D), wti=vm(D, 3 * HD), wto=vm(HD, D),
        ga_send=vm(32, 8, HD), ga_recv=vm(32, 8, HD), h_send=vm(32, 8, D), h_recv=vm(32, 8, D),
        at_send=vm(32, 8, HD), at_recv=vm(32, 8, HD), gh_send=vm(32, 8, D), gh_recv=vm(32, 8, D),
        sh=vm(N, D), sq=vm(N, PAD), sk=vm(N, PAD), sv=vm(N, PAD), sw=vm(HEADS, N, N),
        th=vm(N, D), tq=vm(N, PAD), tk=vm(N, PAD), tv=vm(N, PAD), tw=vm(HEADS, N, N),
        acc=vf(N, PAD), accq=vf(N, PAD), acck=vf(N, PAD), accv=vf(N, PAD),
        small=vm(N, PAD), nat=vm(N, 1792), big=vf(N, D),
        res=vm(N, D), s_mean=vf(N, 128), s_inv=vf(N, 128), t_mean=vf(N, 128), t_inv=vf(N, 128),
        turn=vf(D, N), h_t=vm(D, N), att_t=vm(HD, N),
        gpad=vm(8, N, 256), cpad=vm(8, N, 256),
        part=vm(2, 2, 4, 4, *slab), c_recv=vm(2, 4, 4, *slab),
        one_recv=vm(2, 2, 2, *slab), two_recv=vm(2, 2, 4, *slab),
        mid=vm(2, 4, *slab), three_recv=vm(2, 2, ROWS, 128), four_recv=vm(2, 2, *slab),
        zsum=vf(2, *slab), z_send=vm(8, 2, ZROWS, 128), z_recv=vm(8, 2, ZROWS, 128),
        load=dma((6,)), a_send=dma((4,)), a_recv=dma((4,)), c_ssem=dma((2, 4)), c_rsem=dma((2, 4)),
        one_ssem=dma((2, 2)), one_rsem=dma((2, 2)), two_ssem=dma((2, 2, 2)), two_rsem=dma((2, 2, 2)),
        three_ssem=dma((2, 2)), three_rsem=dma((2, 2)), four_ssem=dma((2, 2, 2)), four_rsem=dma((2, 2, 2)),
        z_ssem=dma, z_rsem=dma,
    )


def rows_of(step, size=CHUNK):
    return pl.ds(pl.multiple_of(step * size, size), size)


def slabs_of(step, size=CHUNK // 8):
    return pl.ds(step * size, size)


def mean_of(x):
    return jnp.sum(x, -1, keepdims=True) * (1.0 / D)


def normalize(x):
    center = x - mean_of(x)
    inverse = lax.rsqrt(mean_of(center * center) + 1e-06)
    return center, inverse


def project(src, w, q, k, v):
    x = src[...]
    q[...] = dot(x, w[:, 0:PAD]).astype(BF16)
    k[...] = pltpu.roll(dot(x, w[:, 512:D]), PAD - 64, 1).astype(BF16)
    v[:, 512:PAD] = jnp.zeros((N, 128), BF16)
    v[:, 0:HD] = dot(x, w[:, D : 3 * HD]).astype(BF16)


def forward_heads(q, k, v, weights, acc, keep):
    for head in range(HEADS):
        offset, cut, wide = window(head)
        mine = head_mask(offset, wide)
        queries = jnp.where(mine, q[:, cut].astype(F32), 0.0).astype(BF16)
        p = jnp.exp(dot_nt(queries, k[:, cut]) * FACTOR)
        if keep is not None:
            p = jnp.where(keep, p, 0.0)
        w = (p * (1.0 / jnp.sum(p, -1, keepdims=True))).astype(BF16)
        weights[head] = w
        out = dot(w, v[:, cut])
        acc[:, cut] = out if head == 0 else jnp.where(mine, out, acc[:, cut])


def backward_heads(q, k, v, weights, grad, accq, acck, accv):
    for head in range(HEADS):
        offset, cut, wide = window(head)
        mine = head_mask(offset, wide)
        g = grad[:, cut]
        w = weights[head]
        e = dot_nt(jnp.where(mine, g.astype(F32), 0.0).astype(BF16), v[:, cut])
        p = w.astype(F32)
        r = (p * (e - jnp.sum(e * p, -1, keepdims=True)) * FACTOR).astype(BF16)
        for acc, out in ((accv, dot_tn(w, g)), (accq, dot(r, k[:, cut])), (acck, dot_tn(r, q[:, cut]))):
            acc[:, cut] = out if head == 0 else jnp.where(mine, out, acc[:, cut])


def join(nat, accq, acck, accv):
    lane = lax.broadcasted_iota(jnp.int32, (N, 128), 1)
    moved = pltpu.roll(acck[...], 64, 1)
    nat[:, 0:512] = accq[:, 0:512].astype(BF16)
    nat[:, 512:640] = jnp.where(lane < 64, accq[:, 512:640], moved[:, 0:128]).astype(BF16)
    nat[:, 640:1152] = moved[:, 128:640].astype(BF16)
    nat[:, 1152:1664] = accv[:, 0:512].astype(BF16)
    nat[:, 1664:1792] = jnp.where(lane < 64, accv[:, 512:640], 0.0).astype(BF16)


def kernel(vid_hbm, wsi_hbm, wso_hbm, wti_hbm, wto_hbm, cot_hbm, o_out, o_gv, o_gi, o_go, names, *refs):
    r = dict(zip(names, refs))
    seq = lax.axis_index("seq")
    dp = lax.axis_index("dp")
    z, y_hi, core = seq // 4, seq // 2 % 2, seq % 2
    x, y_lo = dp // 2, dp % 2
    y = y_hi * 2 + y_lo

    def at_seq(s):
        return {"seq": s, "dp": dp}

    def at_x(to):
        return {"seq": seq, "dp": to * 2 + y_lo}

    def at_y(to):
        return {"seq": z * 4 + to // 2 * 2 + core, "dp": x * 2 + to % 2}

    loads = []
    for i, (src, dst) in enumerate(
        ((cot_hbm, "cot"), (wto_hbm, "wto"), (vid_hbm, "vid"), (wsi_hbm, "wsi"), (wso_hbm, "wso"), (wti_hbm, "wti"))
    ):
        copy = pltpu.make_async_copy(src, r[dst], r["load"].at[i])
        copy.start()
        loads.append(copy)

    barrier = pltpu.get_barrier_semaphore()

    def greet(k, carry):
        pl.semaphore_signal(barrier, inc=1, device_id=at_seq(lax.rem(seq + k, 32)), device_id_type=MESH)
        return carry

    lax.fori_loop(1, 32, greet, 0)
    for step in (1, 3):
        pl.semaphore_signal(barrier, inc=1, device_id=at_x((x + step) % 4), device_id_type=MESH)
        pl.semaphore_signal(barrier, inc=1, device_id=at_y((y + step) % 4), device_id_type=MESH)

    def exchange(which, send, recv):
        def one(i, carry):
            k = 16 + (i + 1) // 2 * (1 - 2 * (i % 2))
            to = lax.rem(seq + k, 32)
            pltpu.make_async_remote_copy(
                src_ref=send.at[to],
                dst_ref=recv.at[seq],
                send_sem=r["a_send"].at[which],
                recv_sem=r["a_recv"].at[which],
                device_id=at_seq(to),
                device_id_type=MESH,
            ).start()
            return carry

        lax.fori_loop(0, 31, one, 0)
        recv[seq] = send[seq]

    def wait_exchange(which, recv):
        some = recv.at[pl.ds(0, 31)]
        pltpu.make_async_copy(some, some, r["a_recv"].at[which]).wait()

    def wait_sent(which, send):
        some = send.at[pl.ds(0, 31)]
        pltpu.make_async_copy(some, some, r["a_send"].at[which]).wait()

    loads[0].wait()
    loads[1].wait()
    ga = dot_nt(r["cot"][...], r["wto"][...])
    r["ga_send"][...] = ga.reshape(32, 8, HD).astype(BF16)
    pl.semaphore_wait(barrier, 35)
    exchange(0, r["ga_send"], r["ga_recv"])

    loads[2].wait()

    def norm_video(i, carry):
        rows = rows_of(i)
        v = r["vid"][rows, :].astype(F32)
        mean = mean_of(v)
        center = v - mean
        inverse = lax.rsqrt(mean_of(center * center) + 1e-06)
        r["s_mean"][rows, :] = jnp.broadcast_to(mean, (CHUNK, 128))
        r["s_inv"][rows, :] = jnp.broadcast_to(inverse, (CHUNK, 128))
        r["sh"][rows, :] = (center * inverse).astype(BF16)
        return carry

    lax.fori_loop(0, N // CHUNK, norm_video, 0)
    loads[3].wait()
    project(r["sh"], r["wsi"], r["sq"], r["sk"], r["sv"])
    forward_heads(r["sq"], r["sk"], r["sv"], r["sw"], r["acc"], None)
    r["small"][...] = r["acc"][...].astype(BF16)
    loads[4].wait()
    for n in range(0, D, 384):
        r["big"][:, n : n + 384] = dot(r["small"][:, 0:HD], r["wso"][:, n : n + 384])

    def norm_residual(i, carry):
        rows = rows_of(i)
        v = (r["vid"][rows, :].astype(F32) + r["big"][rows, :]).astype(BF16)
        r["res"][rows, :] = v
        v = v.astype(F32)
        mean = mean_of(v)
        center = v - mean
        inverse = lax.rsqrt(mean_of(center * center) + 1e-06)
        r["t_mean"][rows, :] = jnp.broadcast_to(mean, (CHUNK, 128))
        r["t_inv"][rows, :] = jnp.broadcast_to(inverse, (CHUNK, 128))
        r["h_send"][slabs_of(i)] = (center * inverse).reshape(CHUNK // 8, 8, D).astype(BF16)
        return carry

    lax.fori_loop(0, N // CHUNK, norm_residual, 0)
    exchange(1, r["h_send"], r["h_recv"])

    for b in range(8):
        part = r["cot"][:, 128 * b : 128 * b + 256].astype(F32)
        if b:
            part = pltpu.roll(part, 256 - 16 * b, 1)
        r["cpad"][b] = part.astype(BF16)
    loads[5].wait()

    wait_exchange(0, r["ga_recv"])
    r["small"][:, 512:PAD] = jnp.zeros((N, 128), BF16)
    r["small"][:, 0:HD] = r["ga_recv"][...].astype(F32).reshape(N, HD).astype(BF16)
    wait_exchange(1, r["h_recv"])

    def take_h(i, carry):
        v = r["h_recv"][slabs_of(i)].astype(F32).reshape(CHUNK, D)
        r["th"][rows_of(i), :] = v.astype(BF16)
        return carry

    lax.fori_loop(0, N // CHUNK, take_h, 0)
    project(r["th"], r["wti"], r["tq"], r["tk"], r["tv"])
    place = lax.broadcasted_iota(jnp.int32, (N, N), 0) % 8
    other = lax.broadcasted_iota(jnp.int32, (N, N), 1) % 8
    forward_heads(r["tq"], r["tk"], r["tv"], r["tw"], r["acc"], place == other)
    r["at_send"][...] = r["acc"][:, 0:HD].reshape(32, 8, HD).astype(BF16)
    exchange(2, r["at_send"], r["at_recv"])

    backward_heads(r["tq"], r["tk"], r["tv"], r["tw"], r["small"], r["accq"], r["acck"], r["accv"])
    join(r["nat"], r["accq"], r["acck"], r["accv"])
    for n in range(0, D, 384):
        r["big"][:, n : n + 384] = dot_nt(r["nat"][:, 0 : 3 * HD], r["wti"][n : n + 384, :])

    def give_gh(i, carry):
        r["gh_send"][slabs_of(i)] = r["big"][rows_of(i), :].reshape(CHUNK // 8, 8, D).astype(BF16)
        return carry

    lax.fori_loop(0, N // CHUNK, give_gh, 0)
    exchange(3, r["gh_send"], r["gh_recv"])

    r["turn"][...] = r["th"][...].astype(F32).T
    for c in range(2):
        for hi in range(2):
            for quad in range(2):
                pieces = []
                for zz in range(4 * quad, 4 * quad + 4):
                    first = zz * 144 + hi * 72 + c * 36
                    pieces.append(r["turn"][first : first + 36, :])
                low = c * 576 + hi * 288 + quad * 144
                r["h_t"][low : low + 144, :] = jnp.concatenate(pieces, 0).astype(BF16)
    for b in range(8):
        low = 216 * b // 128 * 128
        off = 216 * b - low
        part = r["nat"][:, low : low + 384].astype(F32)
        if off:
            part = pltpu.roll(part, 384 - off, 1)
        r["gpad"][b] = part[:, 0:256].astype(BF16)

    wait_exchange(2, r["at_recv"])
    r["acc"][:, 0:HD] = r["at_recv"][...].astype(F32).reshape(N, HD)
    r["turn"][0:HD, :] = r["acc"][:, 0:HD].T
    for c in range(2):
        for hi in range(2):
            pieces = []
            for zz in range(8):
                first = zz * 72 + hi * 36 + c * 18
                pieces.append(r["turn"][first : first + 18, :])
            low = c * 288 + hi * 144
            r["att_t"][low : low + 144, :] = jnp.concatenate(pieces, 0).astype(BF16)

    def core_copy(ab, xx):
        if ab == 0:
            src, dst = r["part"].at[1 - core, 0, xx], r["c_recv"].at[0, xx]
        else:
            src, dst = r["part"].at[1 - core, 1, :, xx], r["c_recv"].at[1, :, xx]
        return pltpu.make_async_remote_copy(
            src_ref=src, dst_ref=dst, send_sem=r["c_ssem"].at[ab, xx], recv_sem=r["c_rsem"].at[ab, xx],
            device_id=at_seq(seq + 1 - 2 * core), device_id_type=MESH,
        )

    for xx in range(4):
        for lo in range(2):
            b = 2 * xx + lo
            g_in = dot(r["h_t"][...], r["gpad"][b]).astype(BF16)
            g_out = dot(r["att_t"][...], r["cpad"][b])
            for c in range(2):
                for hi in range(2):
                    for ab in range(2):
                        yy = hi * 2 + lo
                        slot = (c, 0, xx, yy) if ab == 0 else (c, 1, yy, xx)
                        low = c * 576 + hi * 288 + ab * 144
                        low_out = c * 288 + hi * 144 + ab * 72
                        for half in range(2):
                            lanes = slice(half * 128, half * 128 + 128)
                            r["part"][slot + (half, slice(0, 144))] = g_in[low : low + 144, lanes]
                            r["part"][slot + (half, slice(144, 216))] = g_out[low_out : low_out + 72, lanes].astype(BF16)
        core_copy(0, xx).start()
        core_copy(1, xx).start()

    def add_in(dst, dst_at, src, src_at):
        dst[dst_at] = (dst[dst_at].astype(F32) + src[src_at].astype(F32)).astype(BF16)

    for xx in range(4):
        for ab in range(2):
            core_copy(ab, xx).wait_recv()
            for yy in range(4):
                slot = (xx, yy) if ab == 0 else (yy, xx)
                add_in(r["part"], (core, ab) + slot, r["c_recv"], (ab,) + slot)

    def places(first, ab):
        if (ab == 0) == first:
            return x, at_x
        return y, at_y

    def one_copy(ab, way):
        me, where = places(True, ab)
        to = (me + (1, 3)[way]) % 4
        return pltpu.make_async_remote_copy(
            src_ref=r["part"].at[core, ab, (me + 2) % 4, pl.ds(2 * way, 2)], dst_ref=r["one_recv"].at[ab, way],
            send_sem=r["one_ssem"].at[ab, way], recv_sem=r["one_rsem"].at[ab, way],
            device_id=where(to), device_id_type=MESH,
        )

    def two_copy(ab, way, late):
        me, where = places(True, ab)
        to = (me + (1, 3)[way]) % 4
        low = 2 * way if late else 2 - 2 * way
        return pltpu.make_async_remote_copy(
            src_ref=r["part"].at[core, ab, to, pl.ds(low, 2)], dst_ref=r["two_recv"].at[ab, way, pl.ds(low, 2)],
            send_sem=r["two_ssem"].at[ab, way, late], recv_sem=r["two_rsem"].at[ab, way, late],
            device_id=where(to), device_id_type=MESH,
        )

    def three_copy(ab, way):
        me, where = places(False, ab)
        to = (me + (1, 3)[way]) % 4
        return pltpu.make_async_remote_copy(
            src_ref=r["mid"].at[ab, (me + 2) % 4, way], dst_ref=r["three_recv"].at[ab, way],
            send_sem=r["three_ssem"].at[ab, way], recv_sem=r["three_rsem"].at[ab, way],
            device_id=where(to), device_id_type=MESH,
        )

    def four_copy(ab, way, late):
        me, where = places(False, ab)
        to = (me + (1, 3)[way]) % 4
        half = way if late else 1 - way
        return pltpu.make_async_remote_copy(
            src_ref=r["mid"].at[ab, to, half], dst_ref=r["four_recv"].at[ab, way, half],
            send_sem=r["four_ssem"].at[ab, way, late], recv_sem=r["four_rsem"].at[ab, way, late],
            device_id=where(to), device_id_type=MESH,
        )

    both = ((0, 0), (1, 0), (0, 1), (1, 1))
    for ab, way in both:
        one_copy(ab, way).start()
    for ab, way in both:
        two_copy(ab, way, 0).start()

    r["small"][:, 0:HD] = r["acc"][:, 0:HD].astype(BF16)
    for n in range(0, D, 384):
        o_out[:, n : n + 384] = (
            r["res"][:, n : n + 384].astype(F32) + dot(r["small"][:, 0:HD], r["wto"][:, n : n + 384])
        ).astype(BF16)

    for ab, way in both:
        one_copy(ab, way).wait_recv()
        me, _ = places(True, ab)
        to = (me + (1, 3)[way]) % 4
        for yy in range(2):
            add_in(r["part"], (core, ab, to, 2 * way + yy), r["one_recv"], (ab, way, yy))
        two_copy(ab, way, 1).start()

    wait_exchange(3, r["gh_recv"])

    def norm_back_residual(i, carry):
        rows = rows_of(i)
        g = r["gh_recv"][slabs_of(i)].astype(F32).reshape(CHUNK, D)
        inverse = r["t_inv"][rows, 0:1]
        n = (r["res"][rows, :].astype(F32) - r["t_mean"][rows, 0:1]) * inverse
        back = inverse * (g - mean_of(g) - n * mean_of(g * n))
        r["res"][rows, :] = (r["cot"][rows, :].astype(F32) + back).astype(BF16)
        return carry

    lax.fori_loop(0, N // CHUNK, norm_back_residual, 0)
    r["small"][:, 0:HD] = dot_nt(r["res"][...], r["wso"][...]).astype(BF16)
    backward_heads(r["sq"], r["sk"], r["sv"], r["sw"], r["small"], r["accq"], r["acck"], r["accv"])

    for ab in range(2):
        for way in range(2):
            for late in range(2):
                two_copy(ab, way, late).wait_recv()
        me, _ = places(True, ab)
        for j in range(4):
            r["mid"][ab, j] = (
                r["part"][core, ab, me, j].astype(F32)
                + r["two_recv"][ab, 0, j].astype(F32)
                + r["two_recv"][ab, 1, j].astype(F32)
            ).astype(BF16)
        for way in range(2):
            three_copy(ab, way).start()
        for way in range(2):
            four_copy(ab, way, 0).start()

    join(r["nat"], r["accq"], r["acck"], r["accv"])
    for n in range(0, D, 384):
        r["big"][:, n : n + 384] = dot_nt(r["nat"][:, 0 : 3 * HD], r["wsi"][n : n + 384, :])

    for ab, way in both:
        three_copy(ab, way).wait_recv()
        me, _ = places(False, ab)
        to = (me + (1, 3)[way]) % 4
        add_in(r["mid"], (ab, to, way), r["three_recv"], (ab, way))
        four_copy(ab, way, 1).start()

    def norm_back_video(i, carry):
        rows = rows_of(i)
        g = r["big"][rows, :]
        inverse = r["s_inv"][rows, 0:1]
        n = (r["vid"][rows, :].astype(F32) - r["s_mean"][rows, 0:1]) * inverse
        back = inverse * (g - mean_of(g) - n * mean_of(g * n))
        o_gv[rows, :] = (r["res"][rows, :].astype(F32) + back).astype(BF16)
        return carry

    lax.fori_loop(0, N // CHUNK, norm_back_video, 0)

    for ab in range(2):
        for way in range(2):
            for late in range(2):
                four_copy(ab, way, late).wait_recv()
        me, _ = places(False, ab)
        for half in range(2):
            r["zsum"][ab, half] = (
                r["mid"][ab, me, half].astype(F32)
                + r["four_recv"][ab, 0, half].astype(F32)
                + r["four_recv"][ab, 1, half].astype(F32)
            )
            for j in range(4):
                piece = jnp.concatenate(
                    [
                        r["zsum"][ab, half, 36 * j : 36 * j + 36, :],
                        r["zsum"][ab, half, 144 + 18 * j : 144 + 18 * j + 18, :],
                        jnp.zeros((ZROWS - 54, 128), F32),
                    ],
                    0,
                )
                r["z_send"][4 * ab + j, half] = piece.astype(BF16)

    def z_one(k, carry):
        to = lax.rem(z + k, 8)
        pltpu.make_async_remote_copy(
            src_ref=r["z_send"].at[to], dst_ref=r["z_recv"].at[z], send_sem=r["z_ssem"], recv_sem=r["z_rsem"],
            device_id=at_seq(to * 4 + y_hi * 2 + core), device_id_type=MESH,
        ).start()
        return carry

    lax.fori_loop(1, 8, z_one, 0)
    r["z_recv"][z] = r["z_send"][z]
    some = r["z_recv"].at[pl.ds(0, 7)]
    pltpu.make_async_copy(some, some, r["z_rsem"]).wait()
    for half in range(2):
        total = r["z_recv"][0, half].astype(F32)
        for j in range(1, 8):
            total = total + r["z_recv"][j, half].astype(F32)
        if half == 0:
            o_gi[:, 0:128] = total[0:36, :]
            o_go[:, 0:128] = total[36:54, :]
        else:
            o_gi[:, 128:216] = total[0:36, 0:88]
            o_go[:, 128:144] = total[36:54, 0:16]

    for which, name in enumerate(("ga_send", "h_send", "at_send", "gh_send")):
        wait_sent(which, r[name])
    for ab in range(2):
        for xx in range(4):
            core_copy(ab, xx).wait_send()
        for way in range(2):
            one_copy(ab, way).wait_send()
            three_copy(ab, way).wait_send()
            for late in range(2):
                two_copy(ab, way, late).wait_send()
                four_copy(ab, way, late).wait_send()
    some = r["z_send"].at[pl.ds(0, 7)]
    pltpu.make_async_copy(some, some, r["z_ssem"]).wait()


def local(video, spatial_in, spatial_out, temporal_in, temporal_out, cotangent):
    shapes = scratch_shapes()
    names = tuple(shapes)
    anywhere = pl.BlockSpec(memory_space=pl.ANY)
    whole = pl.BlockSpec(memory_space=pltpu.VMEM)

    def body(*refs):
        kernel(*refs[:10], names, *refs[10:])

    out, grad_video, grad_in, grad_out = pl.pallas_call(
        body,
        out_shape=(
            jax.ShapeDtypeStruct((N, D), BF16),
            jax.ShapeDtypeStruct((N, D), BF16),
            jax.ShapeDtypeStruct((36, 216), F32),
            jax.ShapeDtypeStruct((18, 144), F32),
        ),
        in_specs=[anywhere] * 6,
        out_specs=(whole,) * 4,
        scratch_shapes=list(shapes.values()),
        compiler_params=pltpu.CompilerParams(
            collective_id=0, has_side_effects=True, vmem_limit_bytes=60 * 1024 * 1024
        ),
        cost_estimate=pl.CostEstimate(flops=9_000_000_000, bytes_accessed=13_000_000, transcendentals=1_100_000),
    )(video.reshape(N, D), spatial_in, spatial_out, temporal_in, temporal_out, cotangent.reshape(N, D))
    return (out.reshape(video.shape), grad_video.reshape(video.shape), grad_in, grad_out)


def solution(mesh):
    in_specs = (P("dp", "seq", None, None), P(), P(), P(), P(), P("dp", "seq", None, None))
    out_specs = (
        P("dp", "seq", None, None),
        P("dp", "seq", None, None),
        P("seq", "dp"),
        P("seq", "dp"),
    )
    return jax.shard_map(local, mesh=mesh, in_specs=in_specs, out_specs=out_specs, check_vma=False)
```

time: 270 us -> 110 us (0.41)
  Pallas kernels: 0 us -> 88.1 us
  starting transfers between devices: 59.3 us -> 0 us
  matrix products: 58.3 us -> 0 us
  waiting for transfers between devices: 57.5 us -> 0 us
  local copies, waits for them, and re-layouts: 60.8 us -> 19.5 us
  other arithmetic: 22.3 us -> 0 us
  blocking collectives: 6.84 us -> 0 us
    pallas_call x0 -> x1, Pallas kernels: none -> 88.1 us  [local(): pl.pallas_call(body, out_shape=(jax.ShapeDtypeStruct((N, D), BF16), jax.S...]
    all_to_all x9 -> x0, starting transfers between devices: 59.3 us -> none  [the longest x4 29.9 us: swap(): lax.all_to_all(x.reshape(groups, spread, x.shape[-1]), 'seq', 0, 0, tiled...]
    dot_general x22 -> x0, matrix products: 58.3 us -> none  [the longest x4 10.8 us: dot(): return jnp.dot(a, b, preferred_element_type=F32)]
    all_to_all x9 -> x0, waiting for transfers between devices: 57.5 us -> none  [the longest x4 22 us: swap(): lax.all_to_all(x.reshape(groups, spread, x.shape[-1]), 'seq', 0, 0, tiled...]
    reshape x6 -> x0, local copies, waits for them, and re-layouts: 20.9 us -> none  [the longest x2 10.2 us: scatter_sum(): x = grad.astype(BF16).reshape(n_seq // 2, 2, piece_r, cols)]
    transpose x4 -> x0, local copies, waits for them, and re-layouts: 15.7 us -> none  [scatter_sum(): x = jnp.swapaxes(x, 0, 1)]
    reduce_sum x11 -> x0, other arithmetic: 15.5 us -> none  [the longest x4 10.8 us: scatter_sum(): x = jnp.sum(x.astype(F32), 0).astype(BF16)]
    unnamed x42 -> x6, local copies, waits for them, and re-layouts: 4.82 us -> 19.5 us
  transfers between devices with their start and end apart: 9 -> 0, of which waited for: 6 -> 0; matrix products, arithmetic and copies ran while one was open for 41% -> 0% of each run, Pallas kernels for 0% -> 0%
where the time goes in v2:
time: 110 us; the launch traced here: 108 us
  Pallas kernels  88.1 us (80%)
  local copies, waits for them, and re-layouts  19.5 us (18%)
    pallas_call x1, Pallas kernels, local(): pl.pallas_call(body, out_shape=(jax.ShapeDtypeStruct((N, D), BF16), jax.S...  88.1 us
    unnamed x6, local copies, waits for them, and re-layouts  19.5 us

profile of v2, /device:TPU:8, one launch (start us, length us, event | category | flops | bytes accessed | tf_op | source)
XLA Modules:
  0.0 108.2 jit_solution(14557401580256491475)
XLA Ops:
  0.6 6.4 %copy.10.refs_1_ = bf16[1152,1728]{1,0:T(8,128)(2,1)} copy(bf16[1152,1728]{0,1:T(8,128)(2,1)} %param.7) | data formatting | bytes 7962624 | tf_op args[1]
  7.1 6.4 %copy.11.refs_3_ = bf16[1152,1728]{1,0:T(8,128)(2,1)} copy(bf16[1152,1728]{0,1:T(8,128)(2,1)} %param.9) | data formatting | bytes 7962624 | tf_op args[3]
  13.5 88.1 %shard_map.93 = (bf16[256,1152]{1,0:T(8,128)(2,1)}, bf16[256,1152]{1,0:T(8,128)(2,1)}, f32[36,216]{1,0:T(8,128)}, f32[18,144]{1,0:T(8,128)}) custom-call(bf16[256,1152]{1,0:T(8,128)(2,1)} %bitcast.6, bf16[1152,1728]{1,0:T(8,128)(2,1)} %copy.10.refs_1_, bf16[576,1152]{1,0:T(8,128)(2,1)} %refs_2_.1, bf16[1152,1728]{1,0:T(8,128)(2,1)} %copy.11.refs_3_, ...), custom_call_target="tpu_custom_call" | custom-call | flops 8999999488 | bytes 13000000 | tf_op jit(solution)/shard_map/pallas_call | solution.py:534
  101.6 1.9 %copy.16 = bf16[1,1,256,1152]{3,2,1,0:T(8,128)(2,1)} copy(bf16[1,1,256,1152]{3,2,1,0:T(8,128)(2,1)} %bitcast.5) | data formatting | bytes 1179648
  103.5 1.9 %copy.17 = bf16[1,1,256,1152]{3,2,1,0:T(8,128)(2,1)} copy(bf16[1,1,256,1152]{3,2,1,0:T(8,128)(2,1)} %bitcast.4) | data formatting | bytes 1179648
  105.4 1.4 %copy.18 = f32[36,216]{1,0:T(8,128)} copy(f32[36,216]{1,0:T(8,128)} %get-tuple-element.18) | data formatting | bytes 62208
  106.8 1.3 %copy.19 = f32[18,144]{1,0:T(8,128)} copy(f32[18,144]{1,0:T(8,128)} %get-tuple-element.19) | data formatting | bytes 20736

commit v3 on v2

--- a/solution.py
+++ b/solution.py
@@ -16,7 +16,7 @@
 BF16 = jnp.bfloat16
 MESH = pl.DeviceIdType.MESH
 CHUNK = 32
-ROWS = 216
+ROWS = 224
 ZROWS = 64
 
 
@@ -30,6 +30,14 @@
 
 def dot_tn(a, b):
     return lax.dot_general(a, b, (((0,), (0,)), ((), ())), preferred_element_type=F32)
+
+
+def remote(kind, **ends):
+    return pltpu.make_async_remote_copy(**ends)
+
+
+def drain(kind, some, sem):
+    pltpu.make_async_copy(some, some, sem).wait()
 
 
 def window(head):
@@ -50,7 +58,7 @@
     vf = lambda *shape: pltpu.VMEM(shape, F32)
     dma = pltpu.SemaphoreType.DMA
     return dict(
-        vid=vm(N, D), cot=vm(N, D), wsi=vm(D, 3 * HD), wso=vm(HD, D), wti=vm(D, 3 * HD), wto=vm(HD, D),
+        vid=vm(N, D), cot=vm(N, D), wsi=vm(3 * HD, D), wso=vm(HD, D), wti=vm(3 * HD, D), wto=vm(HD, D),
         ga_send=vm(32, 8, HD), ga_recv=vm(32, 8, HD), h_send=vm(32, 8, D), h_recv=vm(32, 8, D),
         at_send=vm(32, 8, HD), at_recv=vm(32, 8, HD), gh_send=vm(32, 8, D), gh_recv=vm(32, 8, D),
         sh=vm(N, D), sq=vm(N, PAD), sk=vm(N, PAD), sv=vm(N, PAD), sw=vm(HEADS, N, N),
@@ -64,7 +72,7 @@
         one_recv=vm(2, 2, 2, *slab), two_recv=vm(2, 2, 4, *slab),
         mid=vm(2, 4, *slab), three_recv=vm(2, 2, ROWS, 128), four_recv=vm(2, 2, *slab),
         zsum=vf(2, *slab), z_send=vm(8, 2, ZROWS, 128), z_recv=vm(8, 2, ZROWS, 128),
-        load=dma((6,)), a_send=dma((4,)), a_recv=dma((4,)), c_ssem=dma((2, 4)), c_rsem=dma((2, 4)),
+        load=dma((6,)), a_send=dma((4,)), a_recv=dma((4,)), c_ssem=dma((2, 2, 4)), c_rsem=dma((2, 2, 4)),
         one_ssem=dma((2, 2)), one_rsem=dma((2, 2)), two_ssem=dma((2, 2, 2)), two_rsem=dma((2, 2, 2)),
         three_ssem=dma((2, 2)), three_rsem=dma((2, 2)), four_ssem=dma((2, 2, 2)), four_rsem=dma((2, 2, 2)),
         z_ssem=dma, z_rsem=dma,
@@ -91,10 +99,10 @@
 
 def project(src, w, q, k, v):
     x = src[...]
-    q[...] = dot(x, w[:, 0:PAD]).astype(BF16)
-    k[...] = pltpu.roll(dot(x, w[:, 512:D]), PAD - 64, 1).astype(BF16)
+    q[...] = dot_nt(x, w[0:PAD, :]).astype(BF16)
+    k[...] = dot_nt(x, w[HD : HD + PAD, :]).astype(BF16)
     v[:, 512:PAD] = jnp.zeros((N, 128), BF16)
-    v[:, 0:HD] = dot(x, w[:, D : 3 * HD]).astype(BF16)
+    v[:, 0:HD] = dot_nt(x, w[D : 3 * HD, :]).astype(BF16)
 
 
 def forward_heads(q, k, v, weights, acc, keep):
@@ -153,7 +161,7 @@
 
     loads = []
     for i, (src, dst) in enumerate(
-        ((cot_hbm, "cot"), (wto_hbm, "wto"), (vid_hbm, "vid"), (wsi_hbm, "wsi"), (wso_hbm, "wso"), (wti_hbm, "wti"))
+        ((vid_hbm, "vid"), (cot_hbm, "cot"), (wto_hbm, "wto"), (wsi_hbm, "wsi"), (wso_hbm, "wso"), (wti_hbm, "wti"))
     ):
         copy = pltpu.make_async_copy(src, r[dst], r["load"].at[i])
         copy.start()
@@ -170,39 +178,33 @@
         pl.semaphore_signal(barrier, inc=1, device_id=at_x((x + step) % 4), device_id_type=MESH)
         pl.semaphore_signal(barrier, inc=1, device_id=at_y((y + step) % 4), device_id_type=MESH)
 
+    def slab_copy(which, send, recv, to):
+        return remote(
+            "swap",
+            src_ref=send.at[to],
+            dst_ref=recv.at[seq],
+            send_sem=r["a_send"].at[which],
+            recv_sem=r["a_recv"].at[which],
+            device_id=at_seq(to),
+            device_id_type=MESH,
+        )
+
     def exchange(which, send, recv):
         def one(i, carry):
             k = 16 + (i + 1) // 2 * (1 - 2 * (i % 2))
-            to = lax.rem(seq + k, 32)
-            pltpu.make_async_remote_copy(
-                src_ref=send.at[to],
-                dst_ref=recv.at[seq],
-                send_sem=r["a_send"].at[which],
-                recv_sem=r["a_recv"].at[which],
-                device_id=at_seq(to),
-                device_id_type=MESH,
-            ).start()
+            slab_copy(which, send, recv, lax.rem(seq + k, 32)).start()
             return carry
 
         lax.fori_loop(0, 31, one, 0)
         recv[seq] = send[seq]
 
     def wait_exchange(which, recv):
-        some = recv.at[pl.ds(0, 31)]
-        pltpu.make_async_copy(some, some, r["a_recv"].at[which]).wait()
+        drain("swap", recv.at[pl.ds(0, 31)], r["a_recv"].at[which])
 
     def wait_sent(which, send):
-        some = send.at[pl.ds(0, 31)]
-        pltpu.make_async_copy(some, some, r["a_send"].at[which]).wait()
+        drain("swap", send.at[pl.ds(0, 31)], r["a_send"].at[which])
 
     loads[0].wait()
-    loads[1].wait()
-    ga = dot_nt(r["cot"][...], r["wto"][...])
-    r["ga_send"][...] = ga.reshape(32, 8, HD).astype(BF16)
-    pl.semaphore_wait(barrier, 35)
-    exchange(0, r["ga_send"], r["ga_recv"])
-
-    loads[2].wait()
 
     def norm_video(i, carry):
         rows = rows_of(i)
@@ -216,6 +218,13 @@
         return carry
 
     lax.fori_loop(0, N // CHUNK, norm_video, 0)
+    loads[1].wait()
+    loads[2].wait()
+    ga = dot_nt(r["cot"][...], r["wto"][...])
+    r["ga_send"][...] = ga.reshape(32, 8, HD).astype(BF16)
+    pl.semaphore_wait(barrier, 35)
+    exchange(0, r["ga_send"], r["ga_recv"])
+
     loads[3].wait()
     project(r["sh"], r["wsi"], r["sq"], r["sk"], r["sv"])
     forward_heads(r["sq"], r["sk"], r["sv"], r["sw"], r["acc"], None)
@@ -224,7 +233,8 @@
     for n in range(0, D, 384):
         r["big"][:, n : n + 384] = dot(r["small"][:, 0:HD], r["wso"][:, n : n + 384])
 
-    def norm_residual(i, carry):
+    def norm_residual(step, carry):
+        i = lax.rem(z + 4 + (step + 1) // 2 * (1 - 2 * (step % 2)), 8)
         rows = rows_of(i)
         v = (r["vid"][rows, :].astype(F32) + r["big"][rows, :]).astype(BF16)
         r["res"][rows, :] = v
@@ -235,10 +245,17 @@
         r["t_mean"][rows, :] = jnp.broadcast_to(mean, (CHUNK, 128))
         r["t_inv"][rows, :] = jnp.broadcast_to(inverse, (CHUNK, 128))
         r["h_send"][slabs_of(i)] = (center * inverse).reshape(CHUNK // 8, 8, D).astype(BF16)
+        for j in range(4):
+            to = i * 4 + lax.rem(seq + 2 + j, 4)
+
+            @pl.when(to != seq)
+            def _():
+                slab_copy(1, r["h_send"], r["h_recv"], to).start()
+
         return carry
 
     lax.fori_loop(0, N // CHUNK, norm_residual, 0)
-    exchange(1, r["h_send"], r["h_recv"])
+    r["h_recv"][seq] = r["h_send"][seq]
 
     for b in range(8):
         part = r["cot"][:, 128 * b : 128 * b + 256].astype(F32)
@@ -268,7 +285,7 @@
     backward_heads(r["tq"], r["tk"], r["tv"], r["tw"], r["small"], r["accq"], r["acck"], r["accv"])
     join(r["nat"], r["accq"], r["acck"], r["accv"])
     for n in range(0, D, 384):
-        r["big"][:, n : n + 384] = dot_nt(r["nat"][:, 0 : 3 * HD], r["wti"][n : n + 384, :])
+        r["big"][:, n : n + 384] = dot(r["nat"][:, 0 : 3 * HD], r["wti"][:, n : n + 384])
 
     def give_gh(i, carry):
         r["gh_send"][slabs_of(i)] = r["big"][rows_of(i), :].reshape(CHUNK // 8, 8, D).astype(BF16)
@@ -295,6 +312,36 @@
             part = pltpu.roll(part, 384 - off, 1)
         r["gpad"][b] = part[:, 0:256].astype(BF16)
 
+    def core_copy(which, ab, xx):
+        rows = (pl.ds(0, 144), pl.ds(144, ROWS - 144))[which]
+        if ab == 0:
+            src, dst = r["part"].at[1 - core, 0, xx, :, :, rows], r["c_recv"].at[0, xx, :, :, rows]
+        else:
+            src, dst = r["part"].at[1 - core, 1, :, xx, :, rows], r["c_recv"].at[1, :, xx, :, rows]
+        return remote(
+            "core",
+            src_ref=src, dst_ref=dst, send_sem=r["c_ssem"].at[which, ab, xx], recv_sem=r["c_rsem"].at[which, ab, xx],
+            device_id=at_seq(seq + 1 - 2 * core), device_id_type=MESH,
+        )
+
+    def fill(which, xx, lo, value):
+        size = (144, 72)[which]
+        for c in range(2):
+            for hi in range(2):
+                for ab in range(2):
+                    yy = hi * 2 + lo
+                    slot = (c, 0, xx, yy) if ab == 0 else (c, 1, yy, xx)
+                    low = size * (c * 4 + hi * 2 + ab)
+                    for half in range(2):
+                        to = slot + (half, slice(144 * which, 144 * which + size))
+                        r["part"][to] = value[low : low + size, half * 128 : half * 128 + 128].astype(BF16)
+
+    for xx in range(4):
+        for lo in range(2):
+            fill(0, xx, lo, dot(r["h_t"][...], r["gpad"][2 * xx + lo]))
+        core_copy(0, 0, xx).start()
+        core_copy(0, 1, xx).start()
+
     wait_exchange(2, r["at_recv"])
     r["acc"][:, 0:HD] = r["at_recv"][...].astype(F32).reshape(N, HD)
     r["turn"][0:HD, :] = r["acc"][:, 0:HD].T
@@ -307,41 +354,25 @@
             low = c * 288 + hi * 144
             r["att_t"][low : low + 144, :] = jnp.concatenate(pieces, 0).astype(BF16)
 
-    def core_copy(ab, xx):
-        if ab == 0:
-            src, dst = r["part"].at[1 - core, 0, xx], r["c_recv"].at[0, xx]
-        else:
-            src, dst = r["part"].at[1 - core, 1, :, xx], r["c_recv"].at[1, :, xx]
-        return pltpu.make_async_remote_copy(
-            src_ref=src, dst_ref=dst, send_sem=r["c_ssem"].at[ab, xx], recv_sem=r["c_rsem"].at[ab, xx],
-            device_id=at_seq(seq + 1 - 2 * core), device_id_type=MESH,
-        )
-
     for xx in range(4):
         for lo in range(2):
-            b = 2 * xx + lo
-            g_in = dot(r["h_t"][...], r["gpad"][b]).astype(BF16)
-            g_out = dot(r["att_t"][...], r["cpad"][b])
-            for c in range(2):
-                for hi in range(2):
-                    for ab in range(2):
-                        yy = hi * 2 + lo
-                        slot = (c, 0, xx, yy) if ab == 0 else (c, 1, yy, xx)
-                        low = c * 576 + hi * 288 + ab * 144
-                        low_out = c * 288 + hi * 144 + ab * 72
-                        for half in range(2):
-                            lanes = slice(half * 128, half * 128 + 128)
-                            r["part"][slot + (half, slice(0, 144))] = g_in[low : low + 144, lanes]
-                            r["part"][slot + (half, slice(144, 216))] = g_out[low_out : low_out + 72, lanes].astype(BF16)
-        core_copy(0, xx).start()
-        core_copy(1, xx).start()
+            fill(1, xx, lo, dot(r["att_t"][...], r["cpad"][2 * xx + lo]))
+        core_copy(1, 0, xx).start()
+        core_copy(1, 1, xx).start()
+
+    r["small"][:, 0:HD] = r["acc"][:, 0:HD].astype(BF16)
+    for n in range(0, D, 384):
+        o_out[:, n : n + 384] = (
+            r["res"][:, n : n + 384].astype(F32) + dot(r["small"][:, 0:HD], r["wto"][:, n : n + 384])
+        ).astype(BF16)
 
     def add_in(dst, dst_at, src, src_at):
         dst[dst_at] = (dst[dst_at].astype(F32) + src[src_at].astype(F32)).astype(BF16)
 
     for xx in range(4):
         for ab in range(2):
-            core_copy(ab, xx).wait_recv()
+            core_copy(0, ab, xx).wait_recv()
+            core_copy(1, ab, xx).wait_recv()
             for yy in range(4):
                 slot = (xx, yy) if ab == 0 else (yy, xx)
                 add_in(r["part"], (core, ab) + slot, r["c_recv"], (ab,) + slot)
@@ -354,7 +385,8 @@
     def one_copy(ab, way):
         me, where = places(True, ab)
         to = (me + (1, 3)[way]) % 4
-        return pltpu.make_async_remote_copy(
+        return remote(
+            "one",
             src_ref=r["part"].at[core, ab, (me + 2) % 4, pl.ds(2 * way, 2)], dst_ref=r["one_recv"].at[ab, way],
             send_sem=r["one_ssem"].at[ab, way], recv_sem=r["one_rsem"].at[ab, way],
             device_id=where(to), device_id_type=MESH,
@@ -364,7 +396,8 @@
         me, where = places(True, ab)
         to = (me + (1, 3)[way]) % 4
         low = 2 * way if late else 2 - 2 * way
-        return pltpu.make_async_remote_copy(
+        return remote(
+            "two",
             src_ref=r["part"].at[core, ab, to, pl.ds(low, 2)], dst_ref=r["two_recv"].at[ab, way, pl.ds(low, 2)],
             send_sem=r["two_ssem"].at[ab, way, late], recv_sem=r["two_rsem"].at[ab, way, late],
             device_id=where(to), device_id_type=MESH,
@@ -373,7 +406,8 @@
     def three_copy(ab, way):
         me, where = places(False, ab)
         to = (me + (1, 3)[way]) % 4
-        return pltpu.make_async_remote_copy(
+        return remote(
+            "three",
             src_ref=r["mid"].at[ab, (me + 2) % 4, way], dst_ref=r["three_recv"].at[ab, way],
             send_sem=r["three_ssem"].at[ab, way], recv_sem=r["three_rsem"].at[ab, way],
             device_id=where(to), device_id_type=MESH,
@@ -383,7 +417,8 @@
         me, where = places(False, ab)
         to = (me + (1, 3)[way]) % 4
         half = way if late else 1 - way
-        return pltpu.make_async_remote_copy(
+        return remote(
+            "four",
             src_ref=r["mid"].at[ab, to, half], dst_ref=r["four_recv"].at[ab, way, half],
             send_sem=r["four_ssem"].at[ab, way, late], recv_sem=r["four_rsem"].at[ab, way, late],
             device_id=where(to), device_id_type=MESH,
@@ -394,12 +429,6 @@
         one_copy(ab, way).start()
     for ab, way in both:
         two_copy(ab, way, 0).start()
-
-    r["small"][:, 0:HD] = r["acc"][:, 0:HD].astype(BF16)
-    for n in range(0, D, 384):
-        o_out[:, n : n + 384] = (
-            r["res"][:, n : n + 384].astype(F32) + dot(r["small"][:, 0:HD], r["wto"][:, n : n + 384])
-        ).astype(BF16)
 
     for ab, way in both:
         one_copy(ab, way).wait_recv()
@@ -442,7 +471,7 @@
 
     join(r["nat"], r["accq"], r["acck"], r["accv"])
     for n in range(0, D, 384):
-        r["big"][:, n : n + 384] = dot_nt(r["nat"][:, 0 : 3 * HD], r["wsi"][n : n + 384, :])
+        r["big"][:, n : n + 384] = dot(r["nat"][:, 0 : 3 * HD], r["wsi"][:, n : n + 384])
 
     for ab, way in both:
         three_copy(ab, way).wait_recv()
@@ -486,7 +515,8 @@
 
     def z_one(k, carry):
         to = lax.rem(z + k, 8)
-        pltpu.make_async_remote_copy(
+        remote(
+            "z",
             src_ref=r["z_send"].at[to], dst_ref=r["z_recv"].at[z], send_sem=r["z_ssem"], recv_sem=r["z_rsem"],
             device_id=at_seq(to * 4 + y_hi * 2 + core), device_id_type=MESH,
         ).start()
@@ -494,8 +524,7 @@
 
     lax.fori_loop(1, 8, z_one, 0)
     r["z_recv"][z] = r["z_send"][z]
-    some = r["z_recv"].at[pl.ds(0, 7)]
-    pltpu.make_async_copy(some, some, r["z_rsem"]).wait()
+    drain("z", r["z_recv"].at[pl.ds(0, 7)], r["z_rsem"])
     for half in range(2):
         total = r["z_recv"][0, half].astype(F32)
         for j in range(1, 8):
@@ -511,15 +540,20 @@
         wait_sent(which, r[name])
     for ab in range(2):
         for xx in range(4):
-            core_copy(ab, xx).wait_send()
+            core_copy(0, ab, xx).wait_send()
+            core_copy(1, ab, xx).wait_send()
         for way in range(2):
             one_copy(ab, way).wait_send()
             three_copy(ab, way).wait_send()
             for late in range(2):
                 two_copy(ab, way, late).wait_send()
                 four_copy(ab, way, late).wait_send()
-    some = r["z_send"].at[pl.ds(0, 7)]
-    pltpu.make_async_copy(some, some, r["z_ssem"]).wait()
+    drain("z", r["z_send"].at[pl.ds(0, 7)], r["z_ssem"])
+
+
+def hand_over(*refs):
+    for source, result in zip(refs[:4], refs[4:]):
+        result[...] = source[...]
 
 
 def local(video, spatial_in, spatial_out, temporal_in, temporal_out, cotangent):
@@ -531,14 +565,15 @@
     def body(*refs):
         kernel(*refs[:10], names, *refs[10:])
 
-    out, grad_video, grad_in, grad_out = pl.pallas_call(
+    results = (
+        jax.ShapeDtypeStruct((N, D), BF16),
+        jax.ShapeDtypeStruct((N, D), BF16),
+        jax.ShapeDtypeStruct((36, 216), F32),
+        jax.ShapeDtypeStruct((18, 144), F32),
+    )
+    held = pl.pallas_call(
         body,
-        out_shape=(
-            jax.ShapeDtypeStruct((N, D), BF16),
-            jax.ShapeDtypeStruct((N, D), BF16),
-            jax.ShapeDtypeStruct((36, 216), F32),
-            jax.ShapeDtypeStruct((18, 144), F32),
-        ),
+        out_shape=results,
         in_specs=[anywhere] * 6,
         out_specs=(whole,) * 4,
         scratch_shapes=list(shapes.values()),
@@ -546,7 +581,14 @@
             collective_id=0, has_side_effects=True, vmem_limit_bytes=60 * 1024 * 1024
         ),
         cost_estimate=pl.CostEstimate(flops=9_000_000_000, bytes_accessed=13_000_000, transcendentals=1_100_000),
-    )(video.reshape(N, D), spatial_in, spatial_out, temporal_in, temporal_out, cotangent.reshape(N, D))
+    )(video.reshape(N, D), spatial_in.T, spatial_out, temporal_in.T, temporal_out, cotangent.reshape(N, D))
+    out, grad_video, grad_in, grad_out = pl.pallas_call(
+        hand_over,
+        out_shape=results,
+        in_specs=[whole] * 4,
+        out_specs=(whole,) * 4,
+        cost_estimate=pl.CostEstimate(flops=0, bytes_accessed=2_400_000, transcendentals=0),
+    )(*held)
     return (out.reshape(video.shape), grad_video.reshape(video.shape), grad_in, grad_out)
 
 

time: 110 us -> 91.9 us (0.84); the launches traced: 108 us -> 91.8 us
  local copies, waits for them, and re-layouts: 19.5 us -> 0 us
  Pallas kernels: 88.1 us -> 91.1 us
    unnamed x6 -> x0, local copies, waits for them, and re-layouts: 19.5 us -> none
    pallas_call x1 -> x2, Pallas kernels: 88.1 us -> 91.1 us  [the longest x1 88.8 us: local(): pl.pallas_call(body, out_shape=results, in_specs=[anywhere] * 6, out_spec...]
where the time goes in v3:
time: 91.9 us; the launch traced here: 91.8 us
  Pallas kernels  91.1 us (99%)
    pallas_call x1, Pallas kernels, local(): pl.pallas_call(body, out_shape=results, in_specs=[anywhere] * 6, out_spec...  88.8 us
    pallas_call x1, Pallas kernels, local(): pl.pallas_call(hand_over, out_shape=results, in_specs=[whole] * 4, out_sp...  2.3 us

profile of v3, /device:TPU:8, one launch (start us, length us, event | category | flops | bytes accessed | tf_op | source)
XLA Modules:
  0.0 91.8 jit_solution(16317699502551874918)
XLA Ops:
  0.6 88.8 %shard_map.93 = (bf16[256,1152]{1,0:T(8,128)(2,1)}, bf16[256,1152]{1,0:T(8,128)(2,1)}, f32[36,216]{1,0:T(8,128)}, f32[18,144]{1,0:T(8,128)}) custom-call(bf16[256,1152]{1,0:T(8,128)(2,1)} %bitcast.8, bf16[1728,1152]{1,0:T(8,128)(2,1)} %bitcast.6, bf16[576,1152]{1,0:T(8,128)(2,1)} %refs_2_.1, bf16[1728,1152]{1,0:T(8,128)(2,1)} %bitcast.7, ...), custom_call_target="tpu_custom_call" | custom-call | flops 8999999488 | bytes 13000000 | tf_op jit(solution)/shard_map/pallas_call | solution.py:574
  89.5 2.3 %shard_map.94 = (bf16[256,1152]{1,0:T(8,128)(2,1)}, bf16[256,1152]{1,0:T(8,128)(2,1)}, f32[36,216]{1,0:T(8,128)}, f32[18,144]{1,0:T(8,128)}) custom-call(bf16[256,1152]{1,0:T(8,128)(2,1)} %get-tuple-element.12.refs_0_, bf16[256,1152]{1,0:T(8,128)(2,1)} %get-tuple-element.13.refs_1_, f32[36,216]{1,0:T(8,128)} %get-tuple-element.14.refs_2_, ...), custom_call_target="tpu_custom_call" | custom-call | bytes 2400000 | tf_op jit(solution)/shard_map/pallas_call | solution.py:585

commit v4 on v3

--- a/solution.py
+++ b/solution.py
@@ -16,8 +16,7 @@
 BF16 = jnp.bfloat16
 MESH = pl.DeviceIdType.MESH
 CHUNK = 32
-ROWS = 224
-ZROWS = 64
+ZROWS = 56
 
 
 def dot(a, b):
@@ -53,7 +52,7 @@
 
 
 def scratch_shapes():
-    slab = (2, ROWS, 128)
+    slab, thin = (2, 144, 128), (2, 48, 128)
     vm = lambda *shape: pltpu.VMEM(shape, BF16)
     vf = lambda *shape: pltpu.VMEM(shape, F32)
     dma = pltpu.SemaphoreType.DMA
@@ -68,13 +67,15 @@
         res=vm(N, D), s_mean=vf(N, 128), s_inv=vf(N, 128), t_mean=vf(N, 128), t_inv=vf(N, 128),
         turn=vf(D, N), h_t=vm(D, N), att_t=vm(HD, N),
         gpad=vm(8, N, 256), cpad=vm(8, N, 256),
-        part=vm(2, 2, 4, 4, *slab), c_recv=vm(2, 4, 4, *slab),
-        one_recv=vm(2, 2, 2, *slab), two_recv=vm(2, 2, 4, *slab),
-        mid=vm(2, 4, *slab), three_recv=vm(2, 2, ROWS, 128), four_recv=vm(2, 2, *slab),
-        zsum=vf(2, *slab), z_send=vm(8, 2, ZROWS, 128), z_recv=vm(8, 2, ZROWS, 128),
+        part_in=vm(2, 2, 4, 4, *slab), part_out=vm(2, 2, 4, 4, *thin),
+        c_recv_in=vm(2, 4, 4, *slab), c_recv_out=vm(2, 4, 4, *thin),
+        one_in=vm(2, 2, 2, *slab), one_out=vm(2, 2, 2, *thin), two_in=vm(2, 2, 4, *slab), two_out=vm(2, 2, 4, *thin),
+        mid_in=vm(2, 4, *slab), mid_out=vm(2, 4, *thin),
+        three_in=vm(2, 2, *slab[1:]), three_out=vm(2, 2, *thin[1:]), four_in=vm(2, 2, *slab), four_out=vm(2, 2, *thin),
+        zsum=vf(2, 2, 216, 128), z_send=vm(8, 2, ZROWS, 128), z_recv=vm(8, 2, ZROWS, 128),
         load=dma((6,)), a_send=dma((4,)), a_recv=dma((4,)), c_ssem=dma((2, 2, 4)), c_rsem=dma((2, 2, 4)),
-        one_ssem=dma((2, 2)), one_rsem=dma((2, 2)), two_ssem=dma((2, 2, 2)), two_rsem=dma((2, 2, 2)),
-        three_ssem=dma((2, 2)), three_rsem=dma((2, 2)), four_ssem=dma((2, 2, 2)), four_rsem=dma((2, 2, 2)),
+        one_ssem=dma((2, 2, 2)), one_rsem=dma((2, 2, 2)), two_ssem=dma((2, 2, 2, 2)), two_rsem=dma((2, 2, 2, 2)),
+        three_ssem=dma((2, 2, 2)), three_rsem=dma((2, 2, 2)), four_ssem=dma((2, 2, 2, 2)), four_rsem=dma((2, 2, 2, 2)),
         z_ssem=dma, z_rsem=dma,
     )
 
@@ -217,7 +218,7 @@
         r["sh"][rows, :] = (center * inverse).astype(BF16)
         return carry
 
-    lax.fori_loop(0, N // CHUNK, norm_video, 0)
+    lax.fori_loop(0, N // CHUNK, norm_video, 0, unroll=2)
     loads[1].wait()
     loads[2].wait()
     ga = dot_nt(r["cot"][...], r["wto"][...])
@@ -295,14 +296,14 @@
     exchange(3, r["gh_send"], r["gh_recv"])
 
     r["turn"][...] = r["th"][...].astype(F32).T
-    for c in range(2):
-        for hi in range(2):
-            for quad in range(2):
+    for ab in range(2):
+        for c in range(2):
+            for hi in range(2):
                 pieces = []
-                for zz in range(4 * quad, 4 * quad + 4):
+                for zz in range(4 * ab, 4 * ab + 4):
                     first = zz * 144 + hi * 72 + c * 36
                     pieces.append(r["turn"][first : first + 36, :])
-                low = c * 576 + hi * 288 + quad * 144
+                low = ab * 576 + c * 288 + hi * 144
                 r["h_t"][low : low + 144, :] = jnp.concatenate(pieces, 0).astype(BF16)
     for b in range(8):
         low = 216 * b // 128 * 128
@@ -312,132 +313,222 @@
             part = pltpu.roll(part, 384 - off, 1)
         r["gpad"][b] = part[:, 0:256].astype(BF16)
 
-    def core_copy(which, ab, xx):
-        rows = (pl.ds(0, 144), pl.ds(144, ROWS - 144))[which]
-        if ab == 0:
-            src, dst = r["part"].at[1 - core, 0, xx, :, :, rows], r["c_recv"].at[0, xx, :, :, rows]
-        else:
-            src, dst = r["part"].at[1 - core, 1, :, xx, :, rows], r["c_recv"].at[1, :, xx, :, rows]
-        return remote(
-            "core",
-            src_ref=src, dst_ref=dst, send_sem=r["c_ssem"].at[which, ab, xx], recv_sem=r["c_rsem"].at[which, ab, xx],
-            device_id=at_seq(seq + 1 - 2 * core), device_id_type=MESH,
-        )
-
-    def fill(which, xx, lo, value):
-        size = (144, 72)[which]
-        for c in range(2):
-            for hi in range(2):
-                for ab in range(2):
-                    yy = hi * 2 + lo
-                    slot = (c, 0, xx, yy) if ab == 0 else (c, 1, yy, xx)
-                    low = size * (c * 4 + hi * 2 + ab)
-                    for half in range(2):
-                        to = slot + (half, slice(144 * which, 144 * which + size))
-                        r["part"][to] = value[low : low + size, half * 128 : half * 128 + 128].astype(BF16)
-
-    for xx in range(4):
-        for lo in range(2):
-            fill(0, xx, lo, dot(r["h_t"][...], r["gpad"][2 * xx + lo]))
-        core_copy(0, 0, xx).start()
-        core_copy(0, 1, xx).start()
-
-    wait_exchange(2, r["at_recv"])
-    r["acc"][:, 0:HD] = r["at_recv"][...].astype(F32).reshape(N, HD)
-    r["turn"][0:HD, :] = r["acc"][:, 0:HD].T
-    for c in range(2):
-        for hi in range(2):
-            pieces = []
-            for zz in range(8):
-                first = zz * 72 + hi * 36 + c * 18
-                pieces.append(r["turn"][first : first + 18, :])
-            low = c * 288 + hi * 144
-            r["att_t"][low : low + 144, :] = jnp.concatenate(pieces, 0).astype(BF16)
-
-    for xx in range(4):
-        for lo in range(2):
-            fill(1, xx, lo, dot(r["att_t"][...], r["cpad"][2 * xx + lo]))
-        core_copy(1, 0, xx).start()
-        core_copy(1, 1, xx).start()
-
-    r["small"][:, 0:HD] = r["acc"][:, 0:HD].astype(BF16)
-    for n in range(0, D, 384):
-        o_out[:, n : n + 384] = (
-            r["res"][:, n : n + 384].astype(F32) + dot(r["small"][:, 0:HD], r["wto"][:, n : n + 384])
-        ).astype(BF16)
-
-    def add_in(dst, dst_at, src, src_at):
-        dst[dst_at] = (dst[dst_at].astype(F32) + src[src_at].astype(F32)).astype(BF16)
-
-    for xx in range(4):
-        for ab in range(2):
-            core_copy(0, ab, xx).wait_recv()
-            core_copy(1, ab, xx).wait_recv()
-            for yy in range(4):
-                slot = (xx, yy) if ab == 0 else (yy, xx)
-                add_in(r["part"], (core, ab) + slot, r["c_recv"], (ab,) + slot)
+    parts = (r["part_in"], r["part_out"])
+    c_recv = (r["c_recv_in"], r["c_recv_out"])
+    one_recv = (r["one_in"], r["one_out"])
+    two_recv = (r["two_in"], r["two_out"])
+    mid = (r["mid_in"], r["mid_out"])
+    three_recv = (r["three_in"], r["three_out"])
+    four_recv = (r["four_in"], r["four_out"])
+    turns = (2, 1, 3, 0)
+    both = ((0, 0), (1, 0), (0, 1), (1, 1))
 
     def places(first, ab):
         if (ab == 0) == first:
             return x, at_x
         return y, at_y
 
-    def one_copy(ab, way):
+    def target(ab, k):
+        me, _ = places(True, ab)
+        return (me + turns[k]) % 4
+
+    def core_copy(w, ab, k):
+        to = target(ab, k)
+        return remote(
+            "core",
+            src_ref=parts[w].at[1 - core, ab, to], dst_ref=c_recv[w].at[ab, to],
+            send_sem=r["c_ssem"].at[w, ab, k], recv_sem=r["c_rsem"].at[w, ab, k],
+            device_id=at_seq(seq + 1 - 2 * core), device_id_type=MESH,
+        )
+
+    def one_copy(w, ab, way):
         me, where = places(True, ab)
         to = (me + (1, 3)[way]) % 4
         return remote(
             "one",
-            src_ref=r["part"].at[core, ab, (me + 2) % 4, pl.ds(2 * way, 2)], dst_ref=r["one_recv"].at[ab, way],
-            send_sem=r["one_ssem"].at[ab, way], recv_sem=r["one_rsem"].at[ab, way],
+            src_ref=parts[w].at[core, ab, (me + 2) % 4, pl.ds(2 * way, 2)], dst_ref=one_recv[w].at[ab, way],
+            send_sem=r["one_ssem"].at[w, ab, way], recv_sem=r["one_rsem"].at[w, ab, way],
             device_id=where(to), device_id_type=MESH,
         )
 
-    def two_copy(ab, way, late):
+    def two_copy(w, ab, way, late):
         me, where = places(True, ab)
         to = (me + (1, 3)[way]) % 4
         low = 2 * way if late else 2 - 2 * way
         return remote(
             "two",
-            src_ref=r["part"].at[core, ab, to, pl.ds(low, 2)], dst_ref=r["two_recv"].at[ab, way, pl.ds(low, 2)],
-            send_sem=r["two_ssem"].at[ab, way, late], recv_sem=r["two_rsem"].at[ab, way, late],
+            src_ref=parts[w].at[core, ab, to, pl.ds(low, 2)], dst_ref=two_recv[w].at[ab, way, pl.ds(low, 2)],
+            send_sem=r["two_ssem"].at[w, ab, way, late], recv_sem=r["two_rsem"].at[w, ab, way, late],
             device_id=where(to), device_id_type=MESH,
         )
 
-    def three_copy(ab, way):
+    def three_copy(w, ab, way):
         me, where = places(False, ab)
         to = (me + (1, 3)[way]) % 4
         return remote(
             "three",
-            src_ref=r["mid"].at[ab, (me + 2) % 4, way], dst_ref=r["three_recv"].at[ab, way],
-            send_sem=r["three_ssem"].at[ab, way], recv_sem=r["three_rsem"].at[ab, way],
+            src_ref=mid[w].at[ab, (me + 2) % 4, way], dst_ref=three_recv[w].at[ab, way],
+            send_sem=r["three_ssem"].at[w, ab, way], recv_sem=r["three_rsem"].at[w, ab, way],
             device_id=where(to), device_id_type=MESH,
         )
 
-    def four_copy(ab, way, late):
+    def four_copy(w, ab, way, late):
         me, where = places(False, ab)
         to = (me + (1, 3)[way]) % 4
         half = way if late else 1 - way
         return remote(
             "four",
-            src_ref=r["mid"].at[ab, to, half], dst_ref=r["four_recv"].at[ab, way, half],
-            send_sem=r["four_ssem"].at[ab, way, late], recv_sem=r["four_rsem"].at[ab, way, late],
+            src_ref=mid[w].at[ab, to, half], dst_ref=four_recv[w].at[ab, way, half],
+            send_sem=r["four_ssem"].at[w, ab, way, late], recv_sem=r["four_rsem"].at[w, ab, way, late],
             device_id=where(to), device_id_type=MESH,
         )
 
-    both = ((0, 0), (1, 0), (0, 1), (1, 1))
-    for ab, way in both:
-        one_copy(ab, way).start()
-    for ab, way in both:
-        two_copy(ab, way, 0).start()
-
-    for ab, way in both:
-        one_copy(ab, way).wait_recv()
+    def add_in(dst, dst_at, src, src_at):
+        dst[dst_at] = (dst[dst_at].astype(F32) + src[src_at].astype(F32)).astype(BF16)
+
+    lane8 = lax.broadcasted_iota(jnp.int32, (8, 128), 1) // 16
+
+    def store(w, ab, slot, value):
+        if w == 0:
+            for half in range(2):
+                parts[0][slot + (half,)] = value[:, half * 128 : half * 128 + 128].astype(BF16)
+            return
+        tail = value[:, 128:256]
+        packed = tail[0:8, :]
+        for g in range(1, 8):
+            packed = jnp.where(lane8 == g, pltpu.roll(tail[8 * g : 8 * g + 8, :], 16 * g, 1), packed)
+        parts[1][slot + (0,)] = value[0:48, 0:128].astype(BF16)
+        rest = [value[48:72, 0:128], packed, tail[64:72, :], jnp.zeros((8, 128), F32)]
+        parts[1][slot + (1,)] = jnp.concatenate(rest, 0).astype(BF16)
+
+    def fill(w, ab, at):
+        left, right, size = ((r["h_t"], r["gpad"], 144), (r["att_t"], r["cpad"], 72))[w]
+        for i in range(2 if ab == 0 else 4):
+            xx, lo = (at, i) if ab == 0 else (i, at)
+            value = dot(left[ab * 4 * size : ab * 4 * size + 4 * size, :], right[2 * xx + lo])
+            for c in range(2):
+                for hi in range(2):
+                    yy = hi * 2 + lo
+                    slot = (c, 0, xx, yy) if ab == 0 else (c, 1, yy, xx)
+                    low = size * (c * 2 + hi)
+                    store(w, ab, slot, value[low : low + size, :])
+
+    def core_add(w, ab, k):
+        core_copy(w, ab, k).wait_recv()
+        to = target(ab, k)
+        for j in range(4):
+            add_in(parts[w], (core, ab, to, j), c_recv[w], (ab, to, j))
+        if k == 0:
+            one_copy(w, ab, 0).start()
+            one_copy(w, ab, 1).start()
+        elif k < 3:
+            two_copy(w, ab, k - 1, 0).start()
+
+    def pass_on(w, ab, way):
+        one_copy(w, ab, way).wait_recv()
         me, _ = places(True, ab)
         to = (me + (1, 3)[way]) % 4
-        for yy in range(2):
-            add_in(r["part"], (core, ab, to, 2 * way + yy), r["one_recv"], (ab, way, yy))
-        two_copy(ab, way, 1).start()
-
+        for j in range(2):
+            add_in(parts[w], (core, ab, to, 2 * way + j), one_recv[w], (ab, way, j))
+        two_copy(w, ab, way, 1).start()
+
+    def second_ring(w, ab):
+        for way in range(2):
+            for late in range(2):
+                two_copy(w, ab, way, late).wait_recv()
+        me, _ = places(True, ab)
+        for j in range(4):
+            mid[w][ab, j] = (
+                parts[w][core, ab, me, j].astype(F32)
+                + two_recv[w][ab, 0, j].astype(F32)
+                + two_recv[w][ab, 1, j].astype(F32)
+            ).astype(BF16)
+        for way in range(2):
+            three_copy(w, ab, way).start()
+        for way in range(2):
+            four_copy(w, ab, way, 0).start()
+
+    def pass_on_again(w, ab, way):
+        three_copy(w, ab, way).wait_recv()
+        me, _ = places(False, ab)
+        add_in(mid[w], (ab, (me + (1, 3)[way]) % 4, way), three_recv[w], (ab, way))
+        four_copy(w, ab, way, 1).start()
+
+    def ring_sum(w, ab, half):
+        me, _ = places(False, ab)
+        return (
+            mid[w][ab, me, half].astype(F32)
+            + four_recv[w][ab, 0, half].astype(F32)
+            + four_recv[w][ab, 1, half].astype(F32)
+        )
+
+    def ring_wait(w, ab):
+        for way in range(2):
+            for late in range(2):
+                four_copy(w, ab, way, late).wait_recv()
+
+    fill(0, 0, target(0, 0))
+    core_copy(0, 0, 0).start()
+    fill(0, 1, y_lo)
+    core_copy(0, 1, 0).start()
+    core_add(0, 0, 0)
+    fill(0, 0, target(0, 1))
+    core_copy(0, 0, 1).start()
+    core_add(0, 1, 0)
+    fill(0, 1, 1 - y_lo)
+    core_copy(0, 1, 1).start()
+    core_copy(0, 1, 2).start()
+    fill(0, 0, target(0, 2))
+    core_copy(0, 0, 2).start()
+    fill(0, 0, target(0, 3))
+    core_copy(0, 0, 3).start()
+    core_copy(0, 1, 3).start()
+    for k in (1, 2):
+        core_add(0, 0, k)
+        core_add(0, 1, k)
+
+    wait_exchange(2, r["at_recv"])
+    r["acc"][:, 0:HD] = r["at_recv"][...].astype(F32).reshape(N, HD)
+    r["small"][:, 0:HD] = r["acc"][:, 0:HD].astype(BF16)
+    r["turn"][0:HD, :] = r["acc"][:, 0:HD].T
+    for ab in range(2):
+        for c in range(2):
+            pieces = []
+            for hi in range(2):
+                for zz in range(4 * ab, 4 * ab + 4):
+                    first = zz * 72 + hi * 36 + c * 18
+                    pieces.append(r["turn"][first : first + 18, :])
+            low = ab * 288 + c * 144
+            r["att_t"][low : low + 144, :] = jnp.concatenate(pieces, 0).astype(BF16)
+    fill(1, 0, target(0, 0))
+    core_copy(1, 0, 0).start()
+    fill(1, 1, y_lo)
+    core_copy(1, 1, 0).start()
+    for k in range(1, 4):
+        fill(1, 0, target(0, k))
+        core_copy(1, 0, k).start()
+    fill(1, 1, 1 - y_lo)
+    for k in range(1, 4):
+        core_copy(1, 1, k).start()
+    for ab, way in both:
+        pass_on(0, ab, way)
+    for k in range(3):
+        core_add(1, 0, k)
+        core_add(1, 1, k)
+    for w in range(2):
+        for ab in range(2):
+            core_add(w, ab, 3)
+
+    for n in range(0, D, 384):
+        o_out[:, n : n + 384] = (
+            r["res"][:, n : n + 384].astype(F32) + dot(r["small"][:, 0:HD], r["wto"][:, n : n + 384])
+        ).astype(BF16)
+
+    for ab, way in both:
+        pass_on(1, ab, way)
+
+    for ab in range(2):
+        second_ring(0, ab)
     wait_exchange(3, r["gh_recv"])
 
     def norm_back_residual(i, carry):
@@ -449,59 +540,30 @@
         r["res"][rows, :] = (r["cot"][rows, :].astype(F32) + back).astype(BF16)
         return carry
 
-    lax.fori_loop(0, N // CHUNK, norm_back_residual, 0)
+    lax.fori_loop(0, N // CHUNK, norm_back_residual, 0, unroll=2)
     r["small"][:, 0:HD] = dot_nt(r["res"][...], r["wso"][...]).astype(BF16)
+    for ab, way in both:
+        pass_on_again(0, ab, way)
+    for ab in range(2):
+        second_ring(1, ab)
     backward_heads(r["sq"], r["sk"], r["sv"], r["sw"], r["small"], r["accq"], r["acck"], r["accv"])
-
+    for ab, way in both:
+        pass_on_again(1, ab, way)
     for ab in range(2):
-        for way in range(2):
-            for late in range(2):
-                two_copy(ab, way, late).wait_recv()
-        me, _ = places(True, ab)
-        for j in range(4):
-            r["mid"][ab, j] = (
-                r["part"][core, ab, me, j].astype(F32)
-                + r["two_recv"][ab, 0, j].astype(F32)
-                + r["two_recv"][ab, 1, j].astype(F32)
-            ).astype(BF16)
-        for way in range(2):
-            three_copy(ab, way).start()
-        for way in range(2):
-            four_copy(ab, way, 0).start()
-
+        ring_wait(0, ab)
+        for half in range(2):
+            r["zsum"][ab, half, 0:144] = ring_sum(0, ab, half)
     join(r["nat"], r["accq"], r["acck"], r["accv"])
-    for n in range(0, D, 384):
-        r["big"][:, n : n + 384] = dot(r["nat"][:, 0 : 3 * HD], r["wsi"][:, n : n + 384])
-
-    for ab, way in both:
-        three_copy(ab, way).wait_recv()
-        me, _ = places(False, ab)
-        to = (me + (1, 3)[way]) % 4
-        add_in(r["mid"], (ab, to, way), r["three_recv"], (ab, way))
-        four_copy(ab, way, 1).start()
-
-    def norm_back_video(i, carry):
-        rows = rows_of(i)
-        g = r["big"][rows, :]
-        inverse = r["s_inv"][rows, 0:1]
-        n = (r["vid"][rows, :].astype(F32) - r["s_mean"][rows, 0:1]) * inverse
-        back = inverse * (g - mean_of(g) - n * mean_of(g * n))
-        o_gv[rows, :] = (r["res"][rows, :].astype(F32) + back).astype(BF16)
-        return carry
-
-    lax.fori_loop(0, N // CHUNK, norm_back_video, 0)
-
     for ab in range(2):
-        for way in range(2):
-            for late in range(2):
-                four_copy(ab, way, late).wait_recv()
-        me, _ = places(False, ab)
+        ring_wait(1, ab)
+        first, rest = ring_sum(1, ab, 0), ring_sum(1, ab, 1)
+        r["zsum"][ab, 0, 144:192] = first
+        r["zsum"][ab, 0, 192:216] = rest[0:24, :]
+        for g in range(8):
+            tail = rest[24:32, :]
+            r["zsum"][ab, 1, 144 + 8 * g : 152 + 8 * g] = pltpu.roll(tail, 128 - 16 * g, 1) if g else tail
+        r["zsum"][ab, 1, 208:216] = rest[32:40, :]
         for half in range(2):
-            r["zsum"][ab, half] = (
-                r["mid"][ab, me, half].astype(F32)
-                + r["four_recv"][ab, 0, half].astype(F32)
-                + r["four_recv"][ab, 1, half].astype(F32)
-            )
             for j in range(4):
                 piece = jnp.concatenate(
                     [
@@ -524,6 +586,21 @@
 
     lax.fori_loop(1, 8, z_one, 0)
     r["z_recv"][z] = r["z_send"][z]
+
+    for n in range(0, D, 384):
+        r["big"][:, n : n + 384] = dot(r["nat"][:, 0 : 3 * HD], r["wsi"][:, n : n + 384])
+
+    def norm_back_video(i, carry):
+        rows = rows_of(i)
+        g = r["big"][rows, :]
+        inverse = r["s_inv"][rows, 0:1]
+        n = (r["vid"][rows, :].astype(F32) - r["s_mean"][rows, 0:1]) * inverse
+        back = inverse * (g - mean_of(g) - n * mean_of(g * n))
+        o_gv[rows, :] = (r["res"][rows, :].astype(F32) + back).astype(BF16)
+        return carry
+
+    lax.fori_loop(0, N // CHUNK, norm_back_video, 0, unroll=2)
+
     drain("z", r["z_recv"].at[pl.ds(0, 7)], r["z_rsem"])
     for half in range(2):
         total = r["z_recv"][0, half].astype(F32)
@@ -538,16 +615,16 @@
 
     for which, name in enumerate(("ga_send", "h_send", "at_send", "gh_send")):
         wait_sent(which, r[name])
-    for ab in range(2):
-        for xx in range(4):
-            core_copy(0, ab, xx).wait_send()
-            core_copy(1, ab, xx).wait_send()
-        for way in range(2):
-            one_copy(ab, way).wait_send()
-            three_copy(ab, way).wait_send()
-            for late in range(2):
-                two_copy(ab, way, late).wait_send()
-                four_copy(ab, way, late).wait_send()
+    for w in range(2):
+        for ab in range(2):
+            for k in range(4):
+                core_copy(w, ab, k).wait_send()
+            for way in range(2):
+                one_copy(w, ab, way).wait_send()
+                three_copy(w, ab, way).wait_send()
+                for late in range(2):
+                    two_copy(w, ab, way, late).wait_send()
+                    four_copy(w, ab, way, late).wait_send()
     drain("z", r["z_send"].at[pl.ds(0, 7)], r["z_ssem"])
 
 

time: 91.9 us -> 86.5 us (0.941)
  Pallas kernels: 91.1 us -> 85.2 us
    pallas_call x1, Pallas kernels: 88.8 us -> 82.9 us  [local(): pl.pallas_call(body, out_shape=results, in_specs=[anywhere] * 6, out_spec...]
where the time goes in v4:
time: 86.5 us; the launch traced here: 85.9 us
  Pallas kernels  85.2 us (98%)
    pallas_call x1, Pallas kernels, local(): pl.pallas_call(body, out_shape=results, in_specs=[anywhere] * 6, out_spec...  82.9 us
    pallas_call x1, Pallas kernels, local(): pl.pallas_call(hand_over, out_shape=results, in_specs=[whole] * 4, out_sp...  2.3 us

profile of v4, /device:TPU:8, one launch (start us, length us, event | category | flops | bytes accessed | tf_op | source)
XLA Modules:
  0.0 85.9 jit_solution(11712048246316021247)
XLA Ops:
  0.6 82.9 %shard_map.93 = (bf16[256,1152]{1,0:T(8,128)(2,1)}, bf16[256,1152]{1,0:T(8,128)(2,1)}, f32[36,216]{1,0:T(8,128)}, f32[18,144]{1,0:T(8,128)}) custom-call(bf16[256,1152]{1,0:T(8,128)(2,1)} %bitcast.8, bf16[1728,1152]{1,0:T(8,128)(2,1)} %bitcast.6, bf16[576,1152]{1,0:T(8,128)(2,1)} %refs_2_.1, bf16[1728,1152]{1,0:T(8,128)(2,1)} %bitcast.7, ...), custom_call_target="tpu_custom_call" | custom-call | flops 8999999488 | bytes 13000000 | tf_op jit(solution)/shard_map/pallas_call | solution.py:651
  83.6 2.3 %shard_map.94 = (bf16[256,1152]{1,0:T(8,128)(2,1)}, bf16[256,1152]{1,0:T(8,128)(2,1)}, f32[36,216]{1,0:T(8,128)}, f32[18,144]{1,0:T(8,128)}) custom-call(bf16[256,1152]{1,0:T(8,128)(2,1)} %get-tuple-element.12.refs_0_, bf16[256,1152]{1,0:T(8,128)(2,1)} %get-tuple-element.13.refs_1_, f32[36,216]{1,0:T(8,128)} %get-tuple-element.14.refs_2_, ...), custom_call_target="tpu_custom_call" | custom-call | bytes 2400000 | tf_op jit(solution)/shard_map/pallas_call | solution.py:662

commit v5 on v4

--- a/solution.py
+++ b/solution.py
@@ -16,7 +16,6 @@
 BF16 = jnp.bfloat16
 MESH = pl.DeviceIdType.MESH
 CHUNK = 32
-ZROWS = 56
 
 
 def dot(a, b):
@@ -64,7 +63,7 @@
         th=vm(N, D), tq=vm(N, PAD), tk=vm(N, PAD), tv=vm(N, PAD), tw=vm(HEADS, N, N),
         acc=vf(N, PAD), accq=vf(N, PAD), acck=vf(N, PAD), accv=vf(N, PAD),
         small=vm(N, PAD), nat=vm(N, 1792), big=vf(N, D),
-        res=vm(N, D), s_mean=vf(N, 128), s_inv=vf(N, 128), t_mean=vf(N, 128), t_inv=vf(N, 128),
+        res=vm(N, D), gres=vm(N, D), att=vm(N, HD), s_mean=vf(N, 128), s_inv=vf(N, 128), t_mean=vf(N, 128), t_inv=vf(N, 128),
         turn=vf(D, N), h_t=vm(D, N), att_t=vm(HD, N),
         gpad=vm(8, N, 256), cpad=vm(8, N, 256),
         part_in=vm(2, 2, 4, 4, *slab), part_out=vm(2, 2, 4, 4, *thin),
@@ -72,11 +71,12 @@
         one_in=vm(2, 2, 2, *slab), one_out=vm(2, 2, 2, *thin), two_in=vm(2, 2, 4, *slab), two_out=vm(2, 2, 4, *thin),
         mid_in=vm(2, 4, *slab), mid_out=vm(2, 4, *thin),
         three_in=vm(2, 2, *slab[1:]), three_out=vm(2, 2, *thin[1:]), four_in=vm(2, 2, *slab), four_out=vm(2, 2, *thin),
-        zsum=vf(2, 2, 216, 128), z_send=vm(8, 2, ZROWS, 128), z_recv=vm(8, 2, ZROWS, 128),
+        zsum=vf(2, 2, 216, 128), z_send_in=vm(8, 2, 40, 128), z_recv_in=vm(8, 2, 40, 128),
+        z_send_out=vm(8, 2, 24, 128), z_recv_out=vm(8, 2, 24, 128),
         load=dma((6,)), a_send=dma((4,)), a_recv=dma((4,)), c_ssem=dma((2, 2, 4)), c_rsem=dma((2, 2, 4)),
         one_ssem=dma((2, 2, 2)), one_rsem=dma((2, 2, 2)), two_ssem=dma((2, 2, 2, 2)), two_rsem=dma((2, 2, 2, 2)),
         three_ssem=dma((2, 2, 2)), three_rsem=dma((2, 2, 2)), four_ssem=dma((2, 2, 2, 2)), four_rsem=dma((2, 2, 2, 2)),
-        z_ssem=dma, z_rsem=dma,
+        z_ssem=dma((2,)), z_rsem=dma((2,)),
     )
 
 
@@ -162,7 +162,7 @@
 
     loads = []
     for i, (src, dst) in enumerate(
-        ((vid_hbm, "vid"), (cot_hbm, "cot"), (wto_hbm, "wto"), (wsi_hbm, "wsi"), (wso_hbm, "wso"), (wti_hbm, "wti"))
+        ((cot_hbm, "cot"), (wto_hbm, "wto"), (vid_hbm, "vid"), (wsi_hbm, "wsi"), (wso_hbm, "wso"), (wti_hbm, "wti"))
     ):
         copy = pltpu.make_async_copy(src, r[dst], r["load"].at[i])
         copy.start()
@@ -190,6 +190,14 @@
             device_id_type=MESH,
         )
 
+    def send_chunk(which, send, recv, i):
+        for j in range(4):
+            to = i * 4 + lax.rem(seq + 2 + j, 4)
+
+            @pl.when(to != seq)
+            def _():
+                slab_copy(which, send, recv, to).start()
+
     def exchange(which, send, recv):
         def one(i, carry):
             k = 16 + (i + 1) // 2 * (1 - 2 * (i % 2))
@@ -206,6 +214,13 @@
         drain("swap", send.at[pl.ds(0, 31)], r["a_send"].at[which])
 
     loads[0].wait()
+    loads[1].wait()
+    ga = dot_nt(r["cot"][...], r["wto"][...])
+    r["ga_send"][...] = ga.reshape(32, 8, HD).astype(BF16)
+    pl.semaphore_wait(barrier, 35)
+    exchange(0, r["ga_send"], r["ga_recv"])
+
+    loads[2].wait()
 
     def norm_video(i, carry):
         rows = rows_of(i)
@@ -219,13 +234,6 @@
         return carry
 
     lax.fori_loop(0, N // CHUNK, norm_video, 0, unroll=2)
-    loads[1].wait()
-    loads[2].wait()
-    ga = dot_nt(r["cot"][...], r["wto"][...])
-    r["ga_send"][...] = ga.reshape(32, 8, HD).astype(BF16)
-    pl.semaphore_wait(barrier, 35)
-    exchange(0, r["ga_send"], r["ga_recv"])
-
     loads[3].wait()
     project(r["sh"], r["wsi"], r["sq"], r["sk"], r["sv"])
     forward_heads(r["sq"], r["sk"], r["sv"], r["sw"], r["acc"], None)
@@ -246,13 +254,7 @@
         r["t_mean"][rows, :] = jnp.broadcast_to(mean, (CHUNK, 128))
         r["t_inv"][rows, :] = jnp.broadcast_to(inverse, (CHUNK, 128))
         r["h_send"][slabs_of(i)] = (center * inverse).reshape(CHUNK // 8, 8, D).astype(BF16)
-        for j in range(4):
-            to = i * 4 + lax.rem(seq + 2 + j, 4)
-
-            @pl.when(to != seq)
-            def _():
-                slab_copy(1, r["h_send"], r["h_recv"], to).start()
-
+        send_chunk(1, r["h_send"], r["h_recv"], i)
         return carry
 
     lax.fori_loop(0, N // CHUNK, norm_residual, 0)
@@ -288,12 +290,14 @@
     for n in range(0, D, 384):
         r["big"][:, n : n + 384] = dot(r["nat"][:, 0 : 3 * HD], r["wti"][:, n : n + 384])
 
-    def give_gh(i, carry):
+    def give_gh(step, carry):
+        i = lax.rem(z + 4 + (step + 1) // 2 * (1 - 2 * (step % 2)), 8)
         r["gh_send"][slabs_of(i)] = r["big"][rows_of(i), :].reshape(CHUNK // 8, 8, D).astype(BF16)
+        send_chunk(3, r["gh_send"], r["gh_recv"], i)
         return carry
 
     lax.fori_loop(0, N // CHUNK, give_gh, 0)
-    exchange(3, r["gh_send"], r["gh_recv"])
+    r["gh_recv"][seq] = r["gh_send"][seq]
 
     r["turn"][...] = r["th"][...].astype(F32).T
     for ab in range(2):
@@ -323,17 +327,20 @@
     turns = (2, 1, 3, 0)
     both = ((0, 0), (1, 0), (0, 1), (1, 1))
 
-    def places(first, ab):
-        if (ab == 0) == first:
+    def x_first(w, ab):
+        return w == 1 or ab == 0
+
+    def places(first, w, ab):
+        if x_first(w, ab) == first:
             return x, at_x
         return y, at_y
 
-    def target(ab, k):
-        me, _ = places(True, ab)
+    def target(w, ab, k):
+        me, _ = places(True, w, ab)
         return (me + turns[k]) % 4
 
     def core_copy(w, ab, k):
-        to = target(ab, k)
+        to = target(w, ab, k)
         return remote(
             "core",
             src_ref=parts[w].at[1 - core, ab, to], dst_ref=c_recv[w].at[ab, to],
@@ -342,7 +349,7 @@
         )
 
     def one_copy(w, ab, way):
-        me, where = places(True, ab)
+        me, where = places(True, w, ab)
         to = (me + (1, 3)[way]) % 4
         return remote(
             "one",
@@ -352,7 +359,7 @@
         )
 
     def two_copy(w, ab, way, late):
-        me, where = places(True, ab)
+        me, where = places(True, w, ab)
         to = (me + (1, 3)[way]) % 4
         low = 2 * way if late else 2 - 2 * way
         return remote(
@@ -363,7 +370,7 @@
         )
 
     def three_copy(w, ab, way):
-        me, where = places(False, ab)
+        me, where = places(False, w, ab)
         to = (me + (1, 3)[way]) % 4
         return remote(
             "three",
@@ -373,7 +380,7 @@
         )
 
     def four_copy(w, ab, way, late):
-        me, where = places(False, ab)
+        me, where = places(False, w, ab)
         to = (me + (1, 3)[way]) % 4
         half = way if late else 1 - way
         return remote(
@@ -403,19 +410,19 @@
 
     def fill(w, ab, at):
         left, right, size = ((r["h_t"], r["gpad"], 144), (r["att_t"], r["cpad"], 72))[w]
-        for i in range(2 if ab == 0 else 4):
-            xx, lo = (at, i) if ab == 0 else (i, at)
+        for i in range(2 if x_first(w, ab) else 4):
+            xx, lo = (at, i) if x_first(w, ab) else (i, at)
             value = dot(left[ab * 4 * size : ab * 4 * size + 4 * size, :], right[2 * xx + lo])
             for c in range(2):
                 for hi in range(2):
                     yy = hi * 2 + lo
-                    slot = (c, 0, xx, yy) if ab == 0 else (c, 1, yy, xx)
+                    slot = (c, ab, xx, yy) if x_first(w, ab) else (c, ab, yy, xx)
                     low = size * (c * 2 + hi)
                     store(w, ab, slot, value[low : low + size, :])
 
     def core_add(w, ab, k):
         core_copy(w, ab, k).wait_recv()
-        to = target(ab, k)
+        to = target(w, ab, k)
         for j in range(4):
             add_in(parts[w], (core, ab, to, j), c_recv[w], (ab, to, j))
         if k == 0:
@@ -426,7 +433,7 @@
 
     def pass_on(w, ab, way):
         one_copy(w, ab, way).wait_recv()
-        me, _ = places(True, ab)
+        me, _ = places(True, w, ab)
         to = (me + (1, 3)[way]) % 4
         for j in range(2):
             add_in(parts[w], (core, ab, to, 2 * way + j), one_recv[w], (ab, way, j))
@@ -436,7 +443,7 @@
         for way in range(2):
             for late in range(2):
                 two_copy(w, ab, way, late).wait_recv()
-        me, _ = places(True, ab)
+        me, _ = places(True, w, ab)
         for j in range(4):
             mid[w][ab, j] = (
                 parts[w][core, ab, me, j].astype(F32)
@@ -450,12 +457,12 @@
 
     def pass_on_again(w, ab, way):
         three_copy(w, ab, way).wait_recv()
-        me, _ = places(False, ab)
+        me, _ = places(False, w, ab)
         add_in(mid[w], (ab, (me + (1, 3)[way]) % 4, way), three_recv[w], (ab, way))
         four_copy(w, ab, way, 1).start()
 
     def ring_sum(w, ab, half):
-        me, _ = places(False, ab)
+        me, _ = places(False, w, ab)
         return (
             mid[w][ab, me, half].astype(F32)
             + four_recv[w][ab, 0, half].astype(F32)
@@ -467,20 +474,20 @@
             for late in range(2):
                 four_copy(w, ab, way, late).wait_recv()
 
-    fill(0, 0, target(0, 0))
+    fill(0, 0, target(0, 0, 0))
     core_copy(0, 0, 0).start()
     fill(0, 1, y_lo)
     core_copy(0, 1, 0).start()
     core_add(0, 0, 0)
-    fill(0, 0, target(0, 1))
+    fill(0, 0, target(0, 0, 1))
     core_copy(0, 0, 1).start()
     core_add(0, 1, 0)
     fill(0, 1, 1 - y_lo)
     core_copy(0, 1, 1).start()
     core_copy(0, 1, 2).start()
-    fill(0, 0, target(0, 2))
+    fill(0, 0, target(0, 0, 2))
     core_copy(0, 0, 2).start()
-    fill(0, 0, target(0, 3))
+    fill(0, 0, target(0, 0, 3))
     core_copy(0, 0, 3).start()
     core_copy(0, 1, 3).start()
     for k in (1, 2):
@@ -489,7 +496,7 @@
 
     wait_exchange(2, r["at_recv"])
     r["acc"][:, 0:HD] = r["at_recv"][...].astype(F32).reshape(N, HD)
-    r["small"][:, 0:HD] = r["acc"][:, 0:HD].astype(BF16)
+    r["att"][...] = r["acc"][:, 0:HD].astype(BF16)
     r["turn"][0:HD, :] = r["acc"][:, 0:HD].T
     for ab in range(2):
         for c in range(2):
@@ -500,16 +507,10 @@
                     pieces.append(r["turn"][first : first + 18, :])
             low = ab * 288 + c * 144
             r["att_t"][low : low + 144, :] = jnp.concatenate(pieces, 0).astype(BF16)
-    fill(1, 0, target(0, 0))
-    core_copy(1, 0, 0).start()
-    fill(1, 1, y_lo)
-    core_copy(1, 1, 0).start()
-    for k in range(1, 4):
-        fill(1, 0, target(0, k))
-        core_copy(1, 0, k).start()
-    fill(1, 1, 1 - y_lo)
-    for k in range(1, 4):
-        core_copy(1, 1, k).start()
+    for k in range(4):
+        for ab in range(2):
+            fill(1, ab, target(1, ab, k))
+            core_copy(1, ab, k).start()
     for ab, way in both:
         pass_on(0, ab, way)
     for k in range(3):
@@ -519,11 +520,6 @@
         for ab in range(2):
             core_add(w, ab, 3)
 
-    for n in range(0, D, 384):
-        o_out[:, n : n + 384] = (
-            r["res"][:, n : n + 384].astype(F32) + dot(r["small"][:, 0:HD], r["wto"][:, n : n + 384])
-        ).astype(BF16)
-
     for ab, way in both:
         pass_on(1, ab, way)
 
@@ -537,23 +533,52 @@
         inverse = r["t_inv"][rows, 0:1]
         n = (r["res"][rows, :].astype(F32) - r["t_mean"][rows, 0:1]) * inverse
         back = inverse * (g - mean_of(g) - n * mean_of(g * n))
-        r["res"][rows, :] = (r["cot"][rows, :].astype(F32) + back).astype(BF16)
+        r["gres"][rows, :] = (r["cot"][rows, :].astype(F32) + back).astype(BF16)
         return carry
 
     lax.fori_loop(0, N // CHUNK, norm_back_residual, 0, unroll=2)
-    r["small"][:, 0:HD] = dot_nt(r["res"][...], r["wso"][...]).astype(BF16)
+    r["small"][:, 0:HD] = dot_nt(r["gres"][...], r["wso"][...]).astype(BF16)
     for ab, way in both:
         pass_on_again(0, ab, way)
     for ab in range(2):
         second_ring(1, ab)
     backward_heads(r["sq"], r["sk"], r["sv"], r["sw"], r["small"], r["accq"], r["acck"], r["accv"])
-    for ab, way in both:
-        pass_on_again(1, ab, way)
+    z_send = (r["z_send_in"], r["z_send_out"])
+    z_recv = (r["z_recv_in"], r["z_recv_out"])
+
+    def give_z(w):
+        first, size, pad = ((0, 36, 4), (144, 18, 6))[w]
+        for ab in range(2):
+            for half in range(2):
+                for j in range(4):
+                    low = first + size * j
+                    piece = jnp.concatenate([r["zsum"][ab, half, low : low + size, :], jnp.zeros((pad, 128), F32)], 0)
+                    z_send[w][4 * ab + j, half] = piece.astype(BF16)
+
+        def z_one(k, carry):
+            to = lax.rem(z + 4 + (k + 1) // 2 * (1 - 2 * (k % 2)), 8)
+            remote(
+                "z",
+                src_ref=z_send[w].at[to], dst_ref=z_recv[w].at[z],
+                send_sem=r["z_ssem"].at[w], recv_sem=r["z_rsem"].at[w],
+                device_id=at_seq(to * 4 + y_hi * 2 + core), device_id_type=MESH,
+            ).start()
+            return carry
+
+        lax.fori_loop(0, 7, z_one, 0)
+        z_recv[w][z] = z_send[w][z]
+
     for ab in range(2):
         ring_wait(0, ab)
         for half in range(2):
             r["zsum"][ab, half, 0:144] = ring_sum(0, ab, half)
+    give_z(0)
+    for ab, way in both:
+        pass_on_again(1, ab, way)
     join(r["nat"], r["accq"], r["acck"], r["accv"])
+    for n in range(0, D, 384):
+        r["big"][:, n : n + 384] = dot(r["nat"][:, 0 : 3 * HD], r["wsi"][:, n : n + 384])
+
     for ab in range(2):
         ring_wait(1, ab)
         first, rest = ring_sum(1, ab, 0), ring_sum(1, ab, 1)
@@ -563,32 +588,7 @@
             tail = rest[24:32, :]
             r["zsum"][ab, 1, 144 + 8 * g : 152 + 8 * g] = pltpu.roll(tail, 128 - 16 * g, 1) if g else tail
         r["zsum"][ab, 1, 208:216] = rest[32:40, :]
-        for half in range(2):
-            for j in range(4):
-                piece = jnp.concatenate(
-                    [
-                        r["zsum"][ab, half, 36 * j : 36 * j + 36, :],
-                        r["zsum"][ab, half, 144 + 18 * j : 144 + 18 * j + 18, :],
-                        jnp.zeros((ZROWS - 54, 128), F32),
-                    ],
-                    0,
-                )
-                r["z_send"][4 * ab + j, half] = piece.astype(BF16)
-
-    def z_one(k, carry):
-        to = lax.rem(z + k, 8)
-        remote(
-            "z",
-            src_ref=r["z_send"].at[to], dst_ref=r["z_recv"].at[z], send_sem=r["z_ssem"], recv_sem=r["z_rsem"],
-            device_id=at_seq(to * 4 + y_hi * 2 + core), device_id_type=MESH,
-        ).start()
-        return carry
-
-    lax.fori_loop(1, 8, z_one, 0)
-    r["z_recv"][z] = r["z_send"][z]
-
-    for n in range(0, D, 384):
-        r["big"][:, n : n + 384] = dot(r["nat"][:, 0 : 3 * HD], r["wsi"][:, n : n + 384])
+    give_z(1)
 
     def norm_back_video(i, carry):
         rows = rows_of(i)
@@ -596,22 +596,26 @@
         inverse = r["s_inv"][rows, 0:1]
         n = (r["vid"][rows, :].astype(F32) - r["s_mean"][rows, 0:1]) * inverse
         back = inverse * (g - mean_of(g) - n * mean_of(g * n))
-        o_gv[rows, :] = (r["res"][rows, :].astype(F32) + back).astype(BF16)
+        o_gv[rows, :] = (r["gres"][rows, :].astype(F32) + back).astype(BF16)
         return carry
 
     lax.fori_loop(0, N // CHUNK, norm_back_video, 0, unroll=2)
 
-    drain("z", r["z_recv"].at[pl.ds(0, 7)], r["z_rsem"])
-    for half in range(2):
-        total = r["z_recv"][0, half].astype(F32)
-        for j in range(1, 8):
-            total = total + r["z_recv"][j, half].astype(F32)
-        if half == 0:
-            o_gi[:, 0:128] = total[0:36, :]
-            o_go[:, 0:128] = total[36:54, :]
-        else:
-            o_gi[:, 128:216] = total[0:36, 0:88]
-            o_go[:, 128:144] = total[36:54, 0:16]
+    for n in range(0, D, 384):
+        o_out[:, n : n + 384] = (
+            r["res"][:, n : n + 384].astype(F32) + dot(r["att"][...], r["wto"][:, n : n + 384])
+        ).astype(BF16)
+
+    for w in range(2):
+        drain("z", z_recv[w].at[pl.ds(0, 7)], r["z_rsem"].at[w])
+        for half in range(2):
+            total = z_recv[w][0, half].astype(F32)
+            for j in range(1, 8):
+                total = total + z_recv[w][j, half].astype(F32)
+            if w == 0:
+                o_gi[:, half * 128 : (128, 216)[half]] = total[0:36, 0 : (128, 88)[half]]
+            else:
+                o_go[:, half * 128 : (128, 144)[half]] = total[0:18, 0 : (128, 16)[half]]
 
     for which, name in enumerate(("ga_send", "h_send", "at_send", "gh_send")):
         wait_sent(which, r[name])
@@ -625,7 +629,8 @@
                 for late in range(2):
                     two_copy(w, ab, way, late).wait_send()
                     four_copy(w, ab, way, late).wait_send()
-    drain("z", r["z_send"].at[pl.ds(0, 7)], r["z_ssem"])
+    for w in range(2):
+        drain("z", z_send[w].at[pl.ds(0, 7)], r["z_ssem"].at[w])
 
 
 def hand_over(*refs):

time: 86.5 us -> 83 us (0.960)
  Pallas kernels: 85.2 us -> 81.6 us
    pallas_call x1, Pallas kernels: 82.9 us -> 79.3 us  [local(): pl.pallas_call(body, out_shape=results, in_specs=[anywhere] * 6, out_spec...]
where the time goes in v5:
time: 83 us; the launch traced here: 82.2 us
  Pallas kernels  81.6 us (98%)
    pallas_call x1, Pallas kernels, local(): pl.pallas_call(body, out_shape=results, in_specs=[anywhere] * 6, out_spec...  79.3 us
    pallas_call x1, Pallas kernels, local(): pl.pallas_call(hand_over, out_shape=results, in_specs=[whole] * 4, out_sp...  2.3 us

profile of v5, /device:TPU:8, one launch (start us, length us, event | category | flops | bytes accessed | tf_op | source)
XLA Modules:
  0.0 82.2 jit_solution(15525514081573565453)
XLA Ops:
  0.6 79.3 %shard_map.93 = (bf16[256,1152]{1,0:T(8,128)(2,1)}, bf16[256,1152]{1,0:T(8,128)(2,1)}, f32[36,216]{1,0:T(8,128)}, f32[18,144]{1,0:T(8,128)}) custom-call(bf16[256,1152]{1,0:T(8,128)(2,1)} %bitcast.8, bf16[1728,1152]{1,0:T(8,128)(2,1)} %bitcast.6, bf16[576,1152]{1,0:T(8,128)(2,1)} %refs_2_.1, bf16[1728,1152]{1,0:T(8,128)(2,1)} %bitcast.7, ...), custom_call_target="tpu_custom_call" | custom-call | flops 8999999488 | bytes 13000000 | tf_op jit(solution)/shard_map/pallas_call | solution.py:656
  79.9 2.3 %shard_map.94 = (bf16[256,1152]{1,0:T(8,128)(2,1)}, bf16[256,1152]{1,0:T(8,128)(2,1)}, f32[36,216]{1,0:T(8,128)}, f32[18,144]{1,0:T(8,128)}) custom-call(bf16[256,1152]{1,0:T(8,128)(2,1)} %get-tuple-element.12.refs_0_, bf16[256,1152]{1,0:T(8,128)(2,1)} %get-tuple-element.13.refs_1_, f32[36,216]{1,0:T(8,128)} %get-tuple-element.14.refs_2_, ...), custom_call_target="tpu_custom_call" | custom-call | bytes 2400000 | tf_op jit(solution)/shard_map/pallas_call | solution.py:667

commit v6 on v5

--- a/solution.py
+++ b/solution.py
@@ -64,16 +64,15 @@
         acc=vf(N, PAD), accq=vf(N, PAD), acck=vf(N, PAD), accv=vf(N, PAD),
         small=vm(N, PAD), nat=vm(N, 1792), big=vf(N, D),
         res=vm(N, D), gres=vm(N, D), att=vm(N, HD), s_mean=vf(N, 128), s_inv=vf(N, 128), t_mean=vf(N, 128), t_inv=vf(N, 128),
-        turn=vf(D, N), h_t=vm(D, N), att_t=vm(HD, N),
-        gpad=vm(8, N, 256), cpad=vm(8, N, 256),
-        part_in=vm(2, 2, 4, 4, *slab), part_out=vm(2, 2, 4, 4, *thin),
-        c_recv_in=vm(2, 4, 4, *slab), c_recv_out=vm(2, 4, 4, *thin),
+        turn=vf(D, N), h_t=vm(2, HD, N), att_t=vm(2, HD // 2, N), h_t_pair=vm(HD, N), att_t_pair=vm(HD // 2, N),
+        gpad=vm(8, N, 256), cpad=vm(8, N, 256), gpad_pair=vm(8, N, 256), cpad_pair=vm(8, N, 256),
+        part_in=vm(2, 4, 4, *slab), part_out=vm(2, 4, 4, *thin),
         one_in=vm(2, 2, 2, *slab), one_out=vm(2, 2, 2, *thin), two_in=vm(2, 2, 4, *slab), two_out=vm(2, 2, 4, *thin),
         mid_in=vm(2, 4, *slab), mid_out=vm(2, 4, *thin),
         three_in=vm(2, 2, *slab[1:]), three_out=vm(2, 2, *thin[1:]), four_in=vm(2, 2, *slab), four_out=vm(2, 2, *thin),
         zsum=vf(2, 2, 216, 128), z_send_in=vm(8, 2, 40, 128), z_recv_in=vm(8, 2, 40, 128),
         z_send_out=vm(8, 2, 24, 128), z_recv_out=vm(8, 2, 24, 128),
-        load=dma((6,)), a_send=dma((4,)), a_recv=dma((4,)), c_ssem=dma((2, 2, 4)), c_rsem=dma((2, 2, 4)),
+        load=dma((6,)), a_send=dma((4,)), a_recv=dma((4,)), c_ssem=dma((7,)), c_rsem=dma((7,)),
         one_ssem=dma((2, 2, 2)), one_rsem=dma((2, 2, 2)), two_ssem=dma((2, 2, 2, 2)), two_rsem=dma((2, 2, 2, 2)),
         three_ssem=dma((2, 2, 2)), three_rsem=dma((2, 2, 2)), four_ssem=dma((2, 2, 2, 2)), four_rsem=dma((2, 2, 2, 2)),
         z_ssem=dma((2,)), z_rsem=dma((2,)),
@@ -260,11 +259,30 @@
     lax.fori_loop(0, N // CHUNK, norm_residual, 0)
     r["h_recv"][seq] = r["h_send"][seq]
 
+    turns = (2, 1, 3, 0)
+
+    def pair_copy(i):
+        if i < 4:
+            blocks = pl.ds(2 * ((x + turns[i]) % 4), 2)
+            src, dst = r["gpad"].at[blocks], r["gpad_pair"].at[blocks]
+        elif i == 4:
+            src, dst = r["cpad"], r["cpad_pair"]
+        elif i == 5:
+            src, dst = r["h_t"].at[1 - core], r["h_t_pair"]
+        else:
+            src, dst = r["att_t"].at[1 - core], r["att_t_pair"]
+        return remote(
+            "core",
+            src_ref=src, dst_ref=dst, send_sem=r["c_ssem"].at[i], recv_sem=r["c_rsem"].at[i],
+            device_id=at_seq(seq + 1 - 2 * core), device_id_type=MESH,
+        )
+
     for b in range(8):
         part = r["cot"][:, 128 * b : 128 * b + 256].astype(F32)
         if b:
             part = pltpu.roll(part, 256 - 16 * b, 1)
         r["cpad"][b] = part.astype(BF16)
+    pair_copy(4).start()
     loads[5].wait()
 
     wait_exchange(0, r["ga_recv"])
@@ -284,20 +302,6 @@
     forward_heads(r["tq"], r["tk"], r["tv"], r["tw"], r["acc"], place == other)
     r["at_send"][...] = r["acc"][:, 0:HD].reshape(32, 8, HD).astype(BF16)
     exchange(2, r["at_send"], r["at_recv"])
-
-    backward_heads(r["tq"], r["tk"], r["tv"], r["tw"], r["small"], r["accq"], r["acck"], r["accv"])
-    join(r["nat"], r["accq"], r["acck"], r["accv"])
-    for n in range(0, D, 384):
-        r["big"][:, n : n + 384] = dot(r["nat"][:, 0 : 3 * HD], r["wti"][:, n : n + 384])
-
-    def give_gh(step, carry):
-        i = lax.rem(z + 4 + (step + 1) // 2 * (1 - 2 * (step % 2)), 8)
-        r["gh_send"][slabs_of(i)] = r["big"][rows_of(i), :].reshape(CHUNK // 8, 8, D).astype(BF16)
-        send_chunk(3, r["gh_send"], r["gh_recv"], i)
-        return carry
-
-    lax.fori_loop(0, N // CHUNK, give_gh, 0)
-    r["gh_recv"][seq] = r["gh_send"][seq]
 
     r["turn"][...] = r["th"][...].astype(F32).T
     for ab in range(2):
@@ -307,8 +311,12 @@
                 for zz in range(4 * ab, 4 * ab + 4):
                     first = zz * 144 + hi * 72 + c * 36
                     pieces.append(r["turn"][first : first + 36, :])
-                low = ab * 576 + c * 288 + hi * 144
-                r["h_t"][low : low + 144, :] = jnp.concatenate(pieces, 0).astype(BF16)
+                low = ab * 288 + hi * 144
+                r["h_t"][c, low : low + 144, :] = jnp.concatenate(pieces, 0).astype(BF16)
+    pair_copy(5).start()
+
+    backward_heads(r["tq"], r["tk"], r["tv"], r["tw"], r["small"], r["accq"], r["acck"], r["accv"])
+    join(r["nat"], r["accq"], r["acck"], r["accv"])
     for b in range(8):
         low = 216 * b // 128 * 128
         off = 216 * b - low
@@ -316,15 +324,26 @@
         if off:
             part = pltpu.roll(part, 384 - off, 1)
         r["gpad"][b] = part[:, 0:256].astype(BF16)
+    for k in range(4):
+        pair_copy(k).start()
+    for n in range(0, D, 384):
+        r["big"][:, n : n + 384] = dot(r["nat"][:, 0 : 3 * HD], r["wti"][:, n : n + 384])
+
+    def give_gh(step, carry):
+        i = lax.rem(z + 4 + (step + 1) // 2 * (1 - 2 * (step % 2)), 8)
+        r["gh_send"][slabs_of(i)] = r["big"][rows_of(i), :].reshape(CHUNK // 8, 8, D).astype(BF16)
+        send_chunk(3, r["gh_send"], r["gh_recv"], i)
+        return carry
+
+    lax.fori_loop(0, N // CHUNK, give_gh, 0)
+    r["gh_recv"][seq] = r["gh_send"][seq]
 
     parts = (r["part_in"], r["part_out"])
-    c_recv = (r["c_recv_in"], r["c_recv_out"])
     one_recv = (r["one_in"], r["one_out"])
     two_recv = (r["two_in"], r["two_out"])
     mid = (r["mid_in"], r["mid_out"])
     three_recv = (r["three_in"], r["three_out"])
     four_recv = (r["four_in"], r["four_out"])
-    turns = (2, 1, 3, 0)
     both = ((0, 0), (1, 0), (0, 1), (1, 1))
 
     def x_first(w, ab):
@@ -338,22 +357,13 @@
     def target(w, ab, k):
         me, _ = places(True, w, ab)
         return (me + turns[k]) % 4
-
-    def core_copy(w, ab, k):
-        to = target(w, ab, k)
-        return remote(
-            "core",
-            src_ref=parts[w].at[1 - core, ab, to], dst_ref=c_recv[w].at[ab, to],
-            send_sem=r["c_ssem"].at[w, ab, k], recv_sem=r["c_rsem"].at[w, ab, k],
-            device_id=at_seq(seq + 1 - 2 * core), device_id_type=MESH,
-        )
 
     def one_copy(w, ab, way):
         me, where = places(True, w, ab)
         to = (me + (1, 3)[way]) % 4
         return remote(
             "one",
-            src_ref=parts[w].at[core, ab, (me + 2) % 4, pl.ds(2 * way, 2)], dst_ref=one_recv[w].at[ab, way],
+            src_ref=parts[w].at[ab, (me + 2) % 4, pl.ds(2 * way, 2)], dst_ref=one_recv[w].at[ab, way],
             send_sem=r["one_ssem"].at[w, ab, way], recv_sem=r["one_rsem"].at[w, ab, way],
             device_id=where(to), device_id_type=MESH,
         )
@@ -364,7 +374,7 @@
         low = 2 * way if late else 2 - 2 * way
         return remote(
             "two",
-            src_ref=parts[w].at[core, ab, to, pl.ds(low, 2)], dst_ref=two_recv[w].at[ab, way, pl.ds(low, 2)],
+            src_ref=parts[w].at[ab, to, pl.ds(low, 2)], dst_ref=two_recv[w].at[ab, way, pl.ds(low, 2)],
             send_sem=r["two_ssem"].at[w, ab, way, late], recv_sem=r["two_rsem"].at[w, ab, way, late],
             device_id=where(to), device_id_type=MESH,
         )
@@ -410,21 +420,18 @@
 
     def fill(w, ab, at):
         left, right, size = ((r["h_t"], r["gpad"], 144), (r["att_t"], r["cpad"], 72))[w]
+        left_pair, right_pair = ((r["h_t_pair"], r["gpad_pair"]), (r["att_t_pair"], r["cpad_pair"]))[w]
+        rows = slice(ab * 2 * size, ab * 2 * size + 2 * size)
         for i in range(2 if x_first(w, ab) else 4):
             xx, lo = (at, i) if x_first(w, ab) else (i, at)
-            value = dot(left[ab * 4 * size : ab * 4 * size + 4 * size, :], right[2 * xx + lo])
-            for c in range(2):
-                for hi in range(2):
-                    yy = hi * 2 + lo
-                    slot = (c, ab, xx, yy) if x_first(w, ab) else (c, ab, yy, xx)
-                    low = size * (c * 2 + hi)
-                    store(w, ab, slot, value[low : low + size, :])
-
-    def core_add(w, ab, k):
-        core_copy(w, ab, k).wait_recv()
-        to = target(w, ab, k)
-        for j in range(4):
-            add_in(parts[w], (core, ab, to, j), c_recv[w], (ab, to, j))
+            b = 2 * xx + lo
+            value = dot(left[core, rows, :], right[b]) + dot(left_pair[rows, :], right_pair[b])
+            for hi in range(2):
+                yy = hi * 2 + lo
+                slot = (ab, xx, yy) if x_first(w, ab) else (ab, yy, xx)
+                store(w, ab, slot, value[size * hi : size * hi + size, :])
+
+    def start_ring(w, ab, k):
         if k == 0:
             one_copy(w, ab, 0).start()
             one_copy(w, ab, 1).start()
@@ -436,7 +443,7 @@
         me, _ = places(True, w, ab)
         to = (me + (1, 3)[way]) % 4
         for j in range(2):
-            add_in(parts[w], (core, ab, to, 2 * way + j), one_recv[w], (ab, way, j))
+            add_in(parts[w], (ab, to, 2 * way + j), one_recv[w], (ab, way, j))
         two_copy(w, ab, way, 1).start()
 
     def second_ring(w, ab):
@@ -446,7 +453,7 @@
         me, _ = places(True, w, ab)
         for j in range(4):
             mid[w][ab, j] = (
-                parts[w][core, ab, me, j].astype(F32)
+                parts[w][ab, me, j].astype(F32)
                 + two_recv[w][ab, 0, j].astype(F32)
                 + two_recv[w][ab, 1, j].astype(F32)
             ).astype(BF16)
@@ -474,25 +481,18 @@
             for late in range(2):
                 four_copy(w, ab, way, late).wait_recv()
 
-    fill(0, 0, target(0, 0, 0))
-    core_copy(0, 0, 0).start()
+    pair_copy(5).wait_recv()
+    for k in range(4):
+        pair_copy(k).wait_recv()
+        if k < 3:
+            fill(0, 0, target(0, 0, k))
+            start_ring(0, 0, k)
     fill(0, 1, y_lo)
-    core_copy(0, 1, 0).start()
-    core_add(0, 0, 0)
-    fill(0, 0, target(0, 0, 1))
-    core_copy(0, 0, 1).start()
-    core_add(0, 1, 0)
+    start_ring(0, 1, 0)
     fill(0, 1, 1 - y_lo)
-    core_copy(0, 1, 1).start()
-    core_copy(0, 1, 2).start()
-    fill(0, 0, target(0, 0, 2))
-    core_copy(0, 0, 2).start()
+    start_ring(0, 1, 1)
+    start_ring(0, 1, 2)
     fill(0, 0, target(0, 0, 3))
-    core_copy(0, 0, 3).start()
-    core_copy(0, 1, 3).start()
-    for k in (1, 2):
-        core_add(0, 0, k)
-        core_add(0, 1, k)
 
     wait_exchange(2, r["at_recv"])
     r["acc"][:, 0:HD] = r["at_recv"][...].astype(F32).reshape(N, HD)
@@ -505,21 +505,16 @@
                 for zz in range(4 * ab, 4 * ab + 4):
                     first = zz * 72 + hi * 36 + c * 18
                     pieces.append(r["turn"][first : first + 18, :])
-            low = ab * 288 + c * 144
-            r["att_t"][low : low + 144, :] = jnp.concatenate(pieces, 0).astype(BF16)
+            r["att_t"][c, ab * 144 : ab * 144 + 144, :] = jnp.concatenate(pieces, 0).astype(BF16)
+    pair_copy(6).start()
+    for ab, way in both:
+        pass_on(0, ab, way)
+    pair_copy(4).wait_recv()
+    pair_copy(6).wait_recv()
     for k in range(4):
         for ab in range(2):
             fill(1, ab, target(1, ab, k))
-            core_copy(1, ab, k).start()
-    for ab, way in both:
-        pass_on(0, ab, way)
-    for k in range(3):
-        core_add(1, 0, k)
-        core_add(1, 1, k)
-    for w in range(2):
-        for ab in range(2):
-            core_add(w, ab, 3)
-
+            start_ring(1, ab, k)
     for ab, way in both:
         pass_on(1, ab, way)
 
@@ -619,10 +614,10 @@
 
     for which, name in enumerate(("ga_send", "h_send", "at_send", "gh_send")):
         wait_sent(which, r[name])
+    for i in range(7):
+        pair_copy(i).wait_send()
     for w in range(2):
         for ab in range(2):
-            for k in range(4):
-                core_copy(w, ab, k).wait_send()
             for way in range(2):
                 one_copy(w, ab, way).wait_send()
                 three_copy(w, ab, way).wait_send()

time: 83 us -> 82.6 us (level)
  no operation moved by 1% of the time
where the time goes in v6:
time: 82.6 us; the launch traced here: 81.8 us
  Pallas kernels  81.2 us (98%)
    pallas_call x1, Pallas kernels, local(): pl.pallas_call(body, out_shape=results, in_specs=[anywhere] * 6, out_spec...  78.9 us
    pallas_call x1, Pallas kernels, local(): pl.pallas_call(hand_over, out_shape=results, in_specs=[whole] * 4, out_sp...  2.3 us

profile of v6, /device:TPU:8, one launch (start us, length us, event | category | flops | bytes accessed | tf_op | source)
XLA Modules:
  0.0 81.8 jit_solution(783788562592948083)
XLA Ops:
  0.6 78.9 %shard_map.93 = (bf16[256,1152]{1,0:T(8,128)(2,1)}, bf16[256,1152]{1,0:T(8,128)(2,1)}, f32[36,216]{1,0:T(8,128)}, f32[18,144]{1,0:T(8,128)}) custom-call(bf16[256,1152]{1,0:T(8,128)(2,1)} %bitcast.8, bf16[1728,1152]{1,0:T(8,128)(2,1)} %bitcast.6, bf16[576,1152]{1,0:T(8,128)(2,1)} %refs_2_.1, bf16[1728,1152]{1,0:T(8,128)(2,1)} %bitcast.7, ...), custom_call_target="tpu_custom_call" | custom-call | flops 8999999488 | bytes 13000000 | tf_op jit(solution)/shard_map/pallas_call | solution.py:651
  79.5 2.3 %shard_map.94 = (bf16[256,1152]{1,0:T(8,128)(2,1)}, bf16[256,1152]{1,0:T(8,128)(2,1)}, f32[36,216]{1,0:T(8,128)}, f32[18,144]{1,0:T(8,128)}) custom-call(bf16[256,1152]{1,0:T(8,128)(2,1)} %get-tuple-element.12.refs_0_, bf16[256,1152]{1,0:T(8,128)(2,1)} %get-tuple-element.13.refs_1_, f32[36,216]{1,0:T(8,128)} %get-tuple-element.14.refs_2_, ...), custom_call_target="tpu_custom_call" | custom-call | bytes 2400000 | tf_op jit(solution)/shard_map/pallas_call | solution.py:662

commit v7 on v6

--- a/solution.py
+++ b/solution.py
@@ -69,12 +69,12 @@
         part_in=vm(2, 4, 4, *slab), part_out=vm(2, 4, 4, *thin),
         one_in=vm(2, 2, 2, *slab), one_out=vm(2, 2, 2, *thin), two_in=vm(2, 2, 4, *slab), two_out=vm(2, 2, 4, *thin),
         mid_in=vm(2, 4, *slab), mid_out=vm(2, 4, *thin),
-        three_in=vm(2, 2, *slab[1:]), three_out=vm(2, 2, *thin[1:]), four_in=vm(2, 2, *slab), four_out=vm(2, 2, *thin),
+        last_in=vm(2, 3, *slab), last_out=vm(2, 3, *thin),
         zsum=vf(2, 2, 216, 128), z_send_in=vm(8, 2, 40, 128), z_recv_in=vm(8, 2, 40, 128),
-        z_send_out=vm(8, 2, 24, 128), z_recv_out=vm(8, 2, 24, 128),
+        z_send_out=vm(8, 24, 128), z_recv_out=vm(8, 24, 128),
         load=dma((6,)), a_send=dma((4,)), a_recv=dma((4,)), c_ssem=dma((7,)), c_rsem=dma((7,)),
         one_ssem=dma((2, 2, 2)), one_rsem=dma((2, 2, 2)), two_ssem=dma((2, 2, 2, 2)), two_rsem=dma((2, 2, 2, 2)),
-        three_ssem=dma((2, 2, 2)), three_rsem=dma((2, 2, 2)), four_ssem=dma((2, 2, 2, 2)), four_rsem=dma((2, 2, 2, 2)),
+        last_ssem=dma((2, 2, 3)), last_rsem=dma((2, 2, 3)),
         z_ssem=dma((2,)), z_rsem=dma((2,)),
     )
 
@@ -174,8 +174,9 @@
         return carry
 
     lax.fori_loop(1, 32, greet, 0)
+    for step in (1, 2, 3):
+        pl.semaphore_signal(barrier, inc=1, device_id=at_x((x + step) % 4), device_id_type=MESH)
     for step in (1, 3):
-        pl.semaphore_signal(barrier, inc=1, device_id=at_x((x + step) % 4), device_id_type=MESH)
         pl.semaphore_signal(barrier, inc=1, device_id=at_y((y + step) % 4), device_id_type=MESH)
 
     def slab_copy(which, send, recv, to):
@@ -216,7 +217,7 @@
     loads[1].wait()
     ga = dot_nt(r["cot"][...], r["wto"][...])
     r["ga_send"][...] = ga.reshape(32, 8, HD).astype(BF16)
-    pl.semaphore_wait(barrier, 35)
+    pl.semaphore_wait(barrier, 36)
     exchange(0, r["ga_send"], r["ga_recv"])
 
     loads[2].wait()
@@ -342,8 +343,7 @@
     one_recv = (r["one_in"], r["one_out"])
     two_recv = (r["two_in"], r["two_out"])
     mid = (r["mid_in"], r["mid_out"])
-    three_recv = (r["three_in"], r["three_out"])
-    four_recv = (r["four_in"], r["four_out"])
+    last_recv = (r["last_in"], r["last_out"])
     both = ((0, 0), (1, 0), (0, 1), (1, 1))
 
     def x_first(w, ab):
@@ -379,24 +379,13 @@
             device_id=where(to), device_id_type=MESH,
         )
 
-    def three_copy(w, ab, way):
+    def last_copy(w, ab, step):
         me, where = places(False, w, ab)
-        to = (me + (1, 3)[way]) % 4
+        to = (me + step) % 4
         return remote(
-            "three",
-            src_ref=mid[w].at[ab, (me + 2) % 4, way], dst_ref=three_recv[w].at[ab, way],
-            send_sem=r["three_ssem"].at[w, ab, way], recv_sem=r["three_rsem"].at[w, ab, way],
-            device_id=where(to), device_id_type=MESH,
-        )
-
-    def four_copy(w, ab, way, late):
-        me, where = places(False, w, ab)
-        to = (me + (1, 3)[way]) % 4
-        half = way if late else 1 - way
-        return remote(
-            "four",
-            src_ref=mid[w].at[ab, to, half], dst_ref=four_recv[w].at[ab, way, half],
-            send_sem=r["four_ssem"].at[w, ab, way, late], recv_sem=r["four_rsem"].at[w, ab, way, late],
+            "last",
+            src_ref=mid[w].at[ab, to], dst_ref=last_recv[w].at[ab, step - 1],
+            send_sem=r["last_ssem"].at[w, ab, step - 1], recv_sem=r["last_rsem"].at[w, ab, step - 1],
             device_id=where(to), device_id_type=MESH,
         )
 
@@ -457,29 +446,19 @@
                 + two_recv[w][ab, 0, j].astype(F32)
                 + two_recv[w][ab, 1, j].astype(F32)
             ).astype(BF16)
-        for way in range(2):
-            three_copy(w, ab, way).start()
-        for way in range(2):
-            four_copy(w, ab, way, 0).start()
-
-    def pass_on_again(w, ab, way):
-        three_copy(w, ab, way).wait_recv()
-        me, _ = places(False, w, ab)
-        add_in(mid[w], (ab, (me + (1, 3)[way]) % 4, way), three_recv[w], (ab, way))
-        four_copy(w, ab, way, 1).start()
+        for step in (2, 1, 3):
+            last_copy(w, ab, step).start()
 
     def ring_sum(w, ab, half):
         me, _ = places(False, w, ab)
-        return (
-            mid[w][ab, me, half].astype(F32)
-            + four_recv[w][ab, 0, half].astype(F32)
-            + four_recv[w][ab, 1, half].astype(F32)
-        )
+        total = mid[w][ab, me, half].astype(F32)
+        for i in range(3):
+            total = total + last_recv[w][ab, i, half].astype(F32)
+        return total
 
     def ring_wait(w, ab):
-        for way in range(2):
-            for late in range(2):
-                four_copy(w, ab, way, late).wait_recv()
+        for step in range(1, 4):
+            last_copy(w, ab, step).wait_recv()
 
     pair_copy(5).wait_recv()
     for k in range(4):
@@ -494,6 +473,8 @@
     start_ring(0, 1, 2)
     fill(0, 0, target(0, 0, 3))
 
+    for ab, way in both:
+        pass_on(0, ab, way)
     wait_exchange(2, r["at_recv"])
     r["acc"][:, 0:HD] = r["at_recv"][...].astype(F32).reshape(N, HD)
     r["att"][...] = r["acc"][:, 0:HD].astype(BF16)
@@ -507,8 +488,6 @@
                     pieces.append(r["turn"][first : first + 18, :])
             r["att_t"][c, ab * 144 : ab * 144 + 144, :] = jnp.concatenate(pieces, 0).astype(BF16)
     pair_copy(6).start()
-    for ab, way in both:
-        pass_on(0, ab, way)
     pair_copy(4).wait_recv()
     pair_copy(6).wait_recv()
     for k in range(4):
@@ -533,22 +512,29 @@
 
     lax.fori_loop(0, N // CHUNK, norm_back_residual, 0, unroll=2)
     r["small"][:, 0:HD] = dot_nt(r["gres"][...], r["wso"][...]).astype(BF16)
-    for ab, way in both:
-        pass_on_again(0, ab, way)
     for ab in range(2):
         second_ring(1, ab)
     backward_heads(r["sq"], r["sk"], r["sv"], r["sw"], r["small"], r["accq"], r["acck"], r["accv"])
     z_send = (r["z_send_in"], r["z_send_out"])
     z_recv = (r["z_recv_in"], r["z_recv_out"])
 
+    lane6 = lax.broadcasted_iota(jnp.int32, (6, 128), 1) // 16
+
     def give_z(w):
-        first, size, pad = ((0, 36, 4), (144, 18, 6))[w]
         for ab in range(2):
-            for half in range(2):
-                for j in range(4):
-                    low = first + size * j
-                    piece = jnp.concatenate([r["zsum"][ab, half, low : low + size, :], jnp.zeros((pad, 128), F32)], 0)
-                    z_send[w][4 * ab + j, half] = piece.astype(BF16)
+            for j in range(4):
+                if w == 0:
+                    for half in range(2):
+                        piece = [r["zsum"][ab, half, 36 * j : 36 * j + 36, :], jnp.zeros((4, 128), F32)]
+                        z_send[0][4 * ab + j, half] = jnp.concatenate(piece, 0).astype(BF16)
+                else:
+                    low = 144 + 18 * j
+                    tail = r["zsum"][ab, 1, low : low + 6, :]
+                    for g in range(1, 3):
+                        more = r["zsum"][ab, 1, low + 6 * g : low + 6 * g + 6, :]
+                        tail = jnp.where(lane6 == g, pltpu.roll(more, 16 * g, 1), tail)
+                    piece = [r["zsum"][ab, 0, low : low + 18, :], tail]
+                    z_send[1][4 * ab + j] = jnp.concatenate(piece, 0).astype(BF16)
 
         def z_one(k, carry):
             to = lax.rem(z + 4 + (k + 1) // 2 * (1 - 2 * (k % 2)), 8)
@@ -568,8 +554,6 @@
         for half in range(2):
             r["zsum"][ab, half, 0:144] = ring_sum(0, ab, half)
     give_z(0)
-    for ab, way in both:
-        pass_on_again(1, ab, way)
     join(r["nat"], r["accq"], r["acck"], r["accv"])
     for n in range(0, D, 384):
         r["big"][:, n : n + 384] = dot(r["nat"][:, 0 : 3 * HD], r["wsi"][:, n : n + 384])
@@ -601,16 +585,19 @@
             r["res"][:, n : n + 384].astype(F32) + dot(r["att"][...], r["wto"][:, n : n + 384])
         ).astype(BF16)
 
-    for w in range(2):
-        drain("z", z_recv[w].at[pl.ds(0, 7)], r["z_rsem"].at[w])
-        for half in range(2):
-            total = z_recv[w][0, half].astype(F32)
-            for j in range(1, 8):
-                total = total + z_recv[w][j, half].astype(F32)
-            if w == 0:
-                o_gi[:, half * 128 : (128, 216)[half]] = total[0:36, 0 : (128, 88)[half]]
-            else:
-                o_go[:, half * 128 : (128, 144)[half]] = total[0:18, 0 : (128, 16)[half]]
+    drain("z", z_recv[0].at[pl.ds(0, 7)], r["z_rsem"].at[0])
+    for half in range(2):
+        total = z_recv[0][0, half].astype(F32)
+        for j in range(1, 8):
+            total = total + z_recv[0][j, half].astype(F32)
+        o_gi[:, half * 128 : (128, 216)[half]] = total[0:36, 0 : (128, 88)[half]]
+    drain("z", z_recv[1].at[pl.ds(0, 7)], r["z_rsem"].at[1])
+    total = z_recv[1][0].astype(F32)
+    for j in range(1, 8):
+        total = total + z_recv[1][j].astype(F32)
+    o_go[:, 0:128] = total[0:18, :]
+    for g in range(3):
+        o_go[6 * g : 6 * g + 6, 128:144] = total[18:24, 16 * g : 16 * g + 16]
 
     for which, name in enumerate(("ga_send", "h_send", "at_send", "gh_send")):
         wait_sent(which, r[name])
@@ -620,10 +607,10 @@
         for ab in range(2):
             for way in range(2):
                 one_copy(w, ab, way).wait_send()
-                three_copy(w, ab, way).wait_send()
                 for late in range(2):
                     two_copy(w, ab, way, late).wait_send()
-                    four_copy(w, ab, way, late).wait_send()
+            for step in range(1, 4):
+                last_copy(w, ab, step).wait_send()
     for w in range(2):
         drain("z", z_send[w].at[pl.ds(0, 7)], r["z_ssem"].at[w])
 

time: 82.6 us -> 80.2 us (0.971)
  Pallas kernels: 81.2 us -> 79.4 us
    pallas_call x1, Pallas kernels: 78.9 us -> 77.1 us  [local(): pl.pallas_call(body, out_shape=results, in_specs=[anywhere] * 6, out_spec...]
where the time goes in v7:
time: 80.2 us; the launch traced here: 80.1 us
  Pallas kernels  79.4 us (99%)
    pallas_call x1, Pallas kernels, local(): pl.pallas_call(body, out_shape=results, in_specs=[anywhere] * 6, out_spec...  77.1 us
    pallas_call x1, Pallas kernels, local(): pl.pallas_call(hand_over, out_shape=results, in_specs=[whole] * 4, out_sp...  2.3 us

profile of v7, /device:TPU:8, one launch (start us, length us, event | category | flops | bytes accessed | tf_op | source)
XLA Modules:
  0.0 80.1 jit_solution(2612667542808968883)
XLA Ops:
  0.6 77.1 %shard_map.93 = (bf16[256,1152]{1,0:T(8,128)(2,1)}, bf16[256,1152]{1,0:T(8,128)(2,1)}, f32[36,216]{1,0:T(8,128)}, f32[18,144]{1,0:T(8,128)}) custom-call(bf16[256,1152]{1,0:T(8,128)(2,1)} %bitcast.8, bf16[1728,1152]{1,0:T(8,128)(2,1)} %bitcast.6, bf16[576,1152]{1,0:T(8,128)(2,1)} %refs_2_.1, bf16[1728,1152]{1,0:T(8,128)(2,1)} %bitcast.7, ...), custom_call_target="tpu_custom_call" | custom-call | flops 8999999488 | bytes 13000000 | tf_op jit(solution)/shard_map/pallas_call | solution.py:638
  77.8 2.3 %shard_map.94 = (bf16[256,1152]{1,0:T(8,128)(2,1)}, bf16[256,1152]{1,0:T(8,128)(2,1)}, f32[36,216]{1,0:T(8,128)}, f32[18,144]{1,0:T(8,128)}) custom-call(bf16[256,1152]{1,0:T(8,128)(2,1)} %get-tuple-element.12.refs_0_, bf16[256,1152]{1,0:T(8,128)(2,1)} %get-tuple-element.13.refs_1_, f32[36,216]{1,0:T(8,128)} %get-tuple-element.14.refs_2_, ...), custom_call_target="tpu_custom_call" | custom-call | bytes 2400000 | tf_op jit(solution)/shard_map/pallas_call | solution.py:649

commit v8 on v7

--- a/solution.py
+++ b/solution.py
@@ -510,7 +510,7 @@
         r["gres"][rows, :] = (r["cot"][rows, :].astype(F32) + back).astype(BF16)
         return carry
 
-    lax.fori_loop(0, N // CHUNK, norm_back_residual, 0, unroll=2)
+    lax.fori_loop(0, N // CHUNK, norm_back_residual, 0, unroll=4)
     r["small"][:, 0:HD] = dot_nt(r["gres"][...], r["wso"][...]).astype(BF16)
     for ab in range(2):
         second_ring(1, ab)
@@ -555,9 +555,6 @@
             r["zsum"][ab, half, 0:144] = ring_sum(0, ab, half)
     give_z(0)
     join(r["nat"], r["accq"], r["acck"], r["accv"])
-    for n in range(0, D, 384):
-        r["big"][:, n : n + 384] = dot(r["nat"][:, 0 : 3 * HD], r["wsi"][:, n : n + 384])
-
     for ab in range(2):
         ring_wait(1, ab)
         first, rest = ring_sum(1, ab, 0), ring_sum(1, ab, 1)
@@ -569,6 +566,9 @@
         r["zsum"][ab, 1, 208:216] = rest[32:40, :]
     give_z(1)
 
+    for n in range(0, D, 384):
+        r["big"][:, n : n + 384] = dot(r["nat"][:, 0 : 3 * HD], r["wsi"][:, n : n + 384])
+
     def norm_back_video(i, carry):
         rows = rows_of(i)
         g = r["big"][rows, :]
@@ -578,7 +578,7 @@
         o_gv[rows, :] = (r["gres"][rows, :].astype(F32) + back).astype(BF16)
         return carry
 
-    lax.fori_loop(0, N // CHUNK, norm_back_video, 0, unroll=2)
+    lax.fori_loop(0, N // CHUNK, norm_back_video, 0, unroll=4)
 
     for n in range(0, D, 384):
         o_out[:, n : n + 384] = (

time: 80.2 us -> 80.2 us (level)
  no operation moved by 1% of the time
where the time goes in v8:
time: 80.2 us; the launch traced here: 80.1 us
  Pallas kernels  79.4 us (99%)
    pallas_call x1, Pallas kernels, local(): pl.pallas_call(body, out_shape=results, in_specs=[anywhere] * 6, out_spec...  77.1 us
    pallas_call x1, Pallas kernels, local(): pl.pallas_call(hand_over, out_shape=results, in_specs=[whole] * 4, out_sp...  2.3 us

profile of v8, /device:TPU:8, one launch (start us, length us, event | category | flops | bytes accessed | tf_op | source)
XLA Modules:
  0.0 80.1 jit_solution(14414395010061738695)
XLA Ops:
  0.6 77.1 %shard_map.93 = (bf16[256,1152]{1,0:T(8,128)(2,1)}, bf16[256,1152]{1,0:T(8,128)(2,1)}, f32[36,216]{1,0:T(8,128)}, f32[18,144]{1,0:T(8,128)}) custom-call(bf16[256,1152]{1,0:T(8,128)(2,1)} %bitcast.8, bf16[1728,1152]{1,0:T(8,128)(2,1)} %bitcast.6, bf16[576,1152]{1,0:T(8,128)(2,1)} %refs_2_.1, bf16[1728,1152]{1,0:T(8,128)(2,1)} %bitcast.7, ...), custom_call_target="tpu_custom_call" | custom-call | flops 8999999488 | bytes 13000000 | tf_op jit(solution)/shard_map/pallas_call | solution.py:638
  77.8 2.3 %shard_map.94 = (bf16[256,1152]{1,0:T(8,128)(2,1)}, bf16[256,1152]{1,0:T(8,128)(2,1)}, f32[36,216]{1,0:T(8,128)}, f32[18,144]{1,0:T(8,128)}) custom-call(bf16[256,1152]{1,0:T(8,128)(2,1)} %get-tuple-element.12.refs_0_, bf16[256,1152]{1,0:T(8,128)(2,1)} %get-tuple-element.13.refs_1_, f32[36,216]{1,0:T(8,128)} %get-tuple-element.14.refs_2_, ...), custom_call_target="tpu_custom_call" | custom-call | bytes 2400000 | tf_op jit(solution)/shard_map/pallas_call | solution.py:649

commit v9 on v7

--- a/solution.py
+++ b/solution.py
@@ -499,6 +499,11 @@
 
     for ab in range(2):
         second_ring(0, ab)
+    for n in range(0, D, 384):
+        o_out[:, n : n + 384] = (
+            r["res"][:, n : n + 384].astype(F32) + dot(r["att"][...], r["wto"][:, n : n + 384])
+        ).astype(BF16)
+
     wait_exchange(3, r["gh_recv"])
 
     def norm_back_residual(i, carry):
@@ -579,11 +584,6 @@
         return carry
 
     lax.fori_loop(0, N // CHUNK, norm_back_video, 0, unroll=2)
-
-    for n in range(0, D, 384):
-        o_out[:, n : n + 384] = (
-            r["res"][:, n : n + 384].astype(F32) + dot(r["att"][...], r["wto"][:, n : n + 384])
-        ).astype(BF16)
 
     drain("z", z_recv[0].at[pl.ds(0, 7)], r["z_rsem"].at[0])
     for half in range(2):

time: 80.2 us -> 80.3 us (level)
  no operation moved by 1% of the time
where the time goes in v9:
time: 80.3 us; the launch traced here: 80.1 us
  Pallas kernels  79.5 us (99%)
    pallas_call x1, Pallas kernels, local(): pl.pallas_call(body, out_shape=results, in_specs=[anywhere] * 6, out_spec...  77.1 us
    pallas_call x1, Pallas kernels, local(): pl.pallas_call(hand_over, out_shape=results, in_specs=[whole] * 4, out_sp...  2.3 us

profile of v9, /device:TPU:8, one launch (start us, length us, event | category | flops | bytes accessed | tf_op | source)
XLA Modules:
  0.0 80.1 jit_solution(12797560352032311566)
XLA Ops:
  0.6 77.1 %shard_map.93 = (bf16[256,1152]{1,0:T(8,128)(2,1)}, bf16[256,1152]{1,0:T(8,128)(2,1)}, f32[36,216]{1,0:T(8,128)}, f32[18,144]{1,0:T(8,128)}) custom-call(bf16[256,1152]{1,0:T(8,128)(2,1)} %bitcast.8, bf16[1728,1152]{1,0:T(8,128)(2,1)} %bitcast.6, bf16[576,1152]{1,0:T(8,128)(2,1)} %refs_2_.1, bf16[1728,1152]{1,0:T(8,128)(2,1)} %bitcast.7, ...), custom_call_target="tpu_custom_call" | custom-call | flops 8999999488 | bytes 13000000 | tf_op jit(solution)/shard_map/pallas_call | solution.py:638
  77.8 2.3 %shard_map.94 = (bf16[256,1152]{1,0:T(8,128)(2,1)}, bf16[256,1152]{1,0:T(8,128)(2,1)}, f32[36,216]{1,0:T(8,128)}, f32[18,144]{1,0:T(8,128)}) custom-call(bf16[256,1152]{1,0:T(8,128)(2,1)} %get-tuple-element.12.refs_0_, bf16[256,1152]{1,0:T(8,128)(2,1)} %get-tuple-element.13.refs_1_, f32[36,216]{1,0:T(8,128)} %get-tuple-element.14.refs_2_, ...), custom_call_target="tpu_custom_call" | custom-call | bytes 2400000 | tf_op jit(solution)/shard_map/pallas_call | solution.py:649
